TPU v7x, 32 devices: a whole 2x2x4 slice. The times are simulated.
32 devices in a mesh: wide: 8 (over z, x), narrow: 4 (over y, core).
Axes of the slice: x: 2, y: 2, z: 4, core: 2. Of those that a mesh axis runs over, the one named last changes fastest.
Arguments:
- pixels: bfloat16 [8, 1568, 1536], P('wide'), may hold values from -24 to 24
- visible: int32 [16, 156], P('wide'), may hold values from 0 to 1567, as said below
- masked: int32 [16, 1412], P('wide'), may hold values from 0 to 1567
- groups: int32 [1536], replicated, may hold values from 0 to 2, as said below
- enc_qkv: float32 [3, 768, 768], P(None, None, ('narrow', 'wide')), may hold values from -0.21875 to 0.21875
- enc_qkv_mom: float32 [3, 768, 768], P(None, None, ('narrow', 'wide')), may hold values from -8.940697e-08 to 8.940697e-08
- enc_out: float32 [768, 768], P(('narrow', 'wide')), may hold values from -0.4375 to 0.4375
- enc_out_mom: float32 [768, 768], P(('narrow', 'wide')), may hold values from -8.940697e-08 to 8.940697e-08
- enc_up: float32 [768, 3072], P(None, ('narrow', 'wide')), may hold values from -0.21875 to 0.21875
- enc_up_mom: float32 [768, 3072], P(None, ('narrow', 'wide')), may hold values from -1.8626451e-08 to 1.8626451e-08
- enc_down: float32 [3072, 768], P(('narrow', 'wide')), may hold values from -0.109375 to 0.109375
- enc_down_mom: float32 [3072, 768], P(('narrow', 'wide')), may hold values from -8.940697e-08 to 8.940697e-08
- dec_qkv: float32 [384, 1152], P(None, ('wide', 'narrow')), may hold values from -0.3125 to 0.3125
- dec_qkv_mom: float32 [384, 1152], P(None, ('wide', 'narrow')), may hold values from -3.5762787e-07 to 3.5762787e-07
- dec_out: float32 [384, 384], P(('wide', 'narrow')), may hold values from -0.625 to 0.625
- dec_out_mom: float32 [384, 384], P(('wide', 'narrow')), may hold values from -3.5762787e-07 to 3.5762787e-07
- dec_up: float32 [384, 1536], P(None, ('wide', 'narrow')), may hold values from -0.3125 to 0.3125
- dec_up_mom: float32 [384, 1536], P(None, ('wide', 'narrow')), may hold values from -3.5762787e-07 to 3.5762787e-07
- dec_down: float32 [1536, 384], P(('wide', 'narrow')), may hold values from -0.15625 to 0.15625
- dec_down_mom: float32 [1536, 384], P(('wide', 'narrow')), may hold values from -3.5762787e-07 to 3.5762787e-07
- embed: float32 [1536, 768], P('wide'), may hold values from -0.15625 to 0.15625
- embed_m: float32 [1536, 768], P('wide'), may hold values from -5.820766e-10 to 5.820766e-10
- embed_v: float32 [1536, 768], P('wide'), may hold values from 3.4e-20 to 1.35e-19
- enc_to_dec: float32 [768, 384], P('wide'), may hold values from -0.21875 to 0.21875
- enc_to_dec_m: float32 [768, 384], P('wide'), may hold values from -3.7252903e-08 to 3.7252903e-08
- enc_to_dec_v: float32 [768, 384], P('wide'), may hold values from 1.8e-16 to 7.3e-16
- head: float32 [384, 1536], P(('wide', 'narrow')), may hold values from -0.078125 to 0.078125
- head_m: float32 [384, 1536], P(('wide', 'narrow')), may hold values from -3.7252903e-08 to 3.7252903e-08
- head_v: float32 [384, 1536], P(('wide', 'narrow')), may hold values from 1.8e-16 to 7.3e-16
- vectors: float32 [19200], replicated, may hold values from -1.2 to 1.6
- vectors_m: float32 [19200], replicated, may hold values from -4.172325e-07 to 4.172325e-07
- vectors_v: float32 [19200], replicated, may hold values from 1.8e-14 to 7.3e-14
Outputs:
- loss_sum: float32 [], replicated
- grad_norm: float32 [], replicated
- enc_qkv_new: float32 [3, 768, 768], P(None, None, ('narrow', 'wide'))
- enc_qkv_mom_new: float32 [3, 768, 768], P(None, None, ('narrow', 'wide'))
- enc_out_new: float32 [768, 768], P(('narrow', 'wide'))
- enc_out_mom_new: float32 [768, 768], P(('narrow', 'wide'))
- enc_up_new: float32 [768, 3072], P(None, ('narrow', 'wide'))
- enc_up_mom_new: float32 [768, 3072], P(None, ('narrow', 'wide'))
- enc_down_new: float32 [3072, 768], P(('narrow', 'wide'))
- enc_down_mom_new: float32 [3072, 768], P(('narrow', 'wide'))
- dec_qkv_new: float32 [384, 1152], P(None, ('wide', 'narrow'))
- dec_qkv_mom_new: float32 [384, 1152], P(None, ('wide', 'narrow'))
- dec_out_new: float32 [384, 384], P(('wide', 'narrow'))
- dec_out_mom_new: float32 [384, 384], P(('wide', 'narrow'))
- dec_up_new: float32 [384, 1536], P(None, ('wide', 'narrow'))
- dec_up_mom_new: float32 [384, 1536], P(None, ('wide', 'narrow'))
- dec_down_new: float32 [1536, 384], P(('wide', 'narrow'))
- dec_down_mom_new: float32 [1536, 384], P(('wide', 'narrow'))
- embed_m_new: float32 [1536, 768], P('wide')
- embed_v_new: float32 [1536, 768], P('wide')
- embed_new: float32 [1536, 768], P('wide')
- enc_to_dec_m_new: float32 [768, 384], P('wide')
- enc_to_dec_v_new: float32 [768, 384], P('wide')
- enc_to_dec_new: float32 [768, 384], P('wide')
- head_m_new: float32 [384, 1536], P(('wide', 'narrow'))
- head_v_new: float32 [384, 1536], P(('wide', 'narrow'))
- head_new: float32 [384, 1536], P(('wide', 'narrow'))
- vectors_m_new: float32 [19200], replicated
- vectors_v_new: float32 [19200], replicated
- vectors_new: float32 [19200], replicated
Inputs may be any that keep to these rules, and one draw needn't show every extreme that they name: For each clip, visible and masked together hold each of 0 to 1567 exactly once. `groups`: each group holds exactly 512 of the values.
All inputs are finite; a program needn't handle non-finite values.
Results may differ from a plain program's by a relative error of at most 0.0095.
Values may be sent and summed in bfloat16 or wider, within the bound.
No kernel may reach another device: no remote copies, remote signals or barrier semaphores. Data moves between devices by JAX's collectives and lax.ppermute only.
A program may use at most 320 MiB of HBM per device.

v0:
```python
import math

import jax
import jax.numpy as jnp
import numpy as np
from jax import lax
from jax.sharding import PartitionSpec as P

WD = "wide"
NR = "narrow"
D = 768
HD = 64
FE = 3072
DD = 384
FD = 1536
PIX = 1536
GROUPS = 3
NS_STEPS = 5
STEP = 10
QN = 4

EPS_NORM = 1e-06
TARGET_EPS = 1.0
CLIP_AT = 0.0002
MOMENTUM = 0.95
RATE_MUON = 0.15
RATE_ADAM = 0.02
RATE_VECTOR = 0.2
DECAY = 0.05
BETA_ONE = 0.9
BETA_TWO = 0.95
EPS_ADAM = 1e-12
NS_A = 3.4445
NS_B = -4.775
NS_C = 2.0315
ROOT_HALF = 0.7071067811865476
INV_ROOT_TWO_PI = 0.3989422804014327
HIGHEST = lax.Precision.HIGHEST
HIGH = lax.Precision.HIGH
BF = jnp.bfloat16
F32 = jnp.float32

BLOCK = "ln1_g ln1_b q_b v_b out_b ln2_g ln2_b up_b down_b"
BLOCK = ("ln1_g", "ln1_b", "q_b", "v_b", "out_b", "ln2_g", "ln2_b", "up_b", "down_b")


def vector_layout():
    entries = []
    for side, width, hidden in (("e", D, FE), ("d", DD, FD)):
        if side == "d":
            entries += [("in_b", DD), ("mask", DD)]
        entries += [(side + name, hidden if name == "up_b" else width) for name in BLOCK]
        entries += [(side + "lnf_g", width), (side + "lnf_b", width)]
        if side == "e":
            entries += [("emb_b", D)]
    entries += [("head_b", PIX)]
    table, offset = {}, 0
    for name, extent in entries:
        table[name] = (offset, extent)
        offset += extent
    return table


def wide_digits(count):
    digits, rest, step = [], count, 1
    while rest > 1:
        radix = 2 if not digits or rest % 4 else 4
        digits.append((step, radix))
        step, rest = step * radix, rest // radix
    return digits


def shift_pairs(count, digit, delta, keep=None):
    step, radix = digit
    pairs = []
    for src in range(count):
        place = src // step % radix
        if 0 <= place + delta < radix and (keep is None or keep(place)):
            pairs.append((src, src + delta * step))
    return pairs


def wide_move(value, digit, delta, keep=None):
    return lax.ppermute(value, WD, shift_pairs(lax.axis_size(WD), digit, delta, keep))


def wide_flip(value, bit):
    count = lax.axis_size(WD)
    return lax.ppermute(value, WD, [(src, src ^ bit) for src in range(count)])


def narrow_flip(value, bit):
    return lax.ppermute(value, NR, [(src, src ^ bit) for src in range(QN)])


def place_in(digit):
    return lax.axis_index(WD) // digit[0] % digit[1]


def pick_half(value, which, axis):
    return lax.dynamic_index_in_dim(value, which, axis, keepdims=False)


def both(mine, theirs, place, axis):
    first = jnp.where(place == 0, mine, theirs)
    second = jnp.where(place == 0, theirs, mine)
    return jnp.stack([first, second], axis)


def line_gather(block, digit, axis):
    radix = digit[1]
    place = place_in(digit)
    if radix == 2:
        return both(block, wide_flip(block, digit[0]), place, axis)
    right, left = [block], [block]
    for hop in range(1, radix):
        right.append(wide_move(right[-1], digit, 1, lambda p, h=hop: p >= h - 1))
        left.append(wide_move(left[-1], digit, -1, lambda p, h=hop: p <= radix - h))
    row = jnp.stack(right[:0:-1] + left, axis)
    return lax.dynamic_slice_in_dim(row, radix - 1 - place, radix, axis)


def wide_gather(block):
    digits = wide_digits(lax.axis_size(WD))
    value = block
    for axis, digit in enumerate(digits[::-1]):
        value = line_gather(value, digit, axis)
    return value.reshape((-1,) + block.shape)


def narrow_gather(block):
    place = lax.axis_index(NR)
    value = both(block, narrow_flip(block, 2), place // 2, 0)
    value = both(value, narrow_flip(value, 1), place % 2, 1)
    return value.reshape((QN,) + block.shape)


def line_scatter(value, digit, axis):
    radix = digit[1]
    place = place_in(digit)
    if radix == 2:
        sent = pick_half(value, 1 - place, axis).astype(BF)
        return pick_half(value, place, axis).astype(F32) + wide_flip(sent, digit[0]).astype(F32)
    total = pick_half(value, place, axis).astype(F32)
    for sign in (1, -1):
        carried = None
        for hop in range(radix - 1, 0, -1):
            target = jnp.clip(place + sign * hop, 0, radix - 1)
            part = pick_half(value, target, axis).astype(F32)
            if carried is not None:
                part = part + carried
            moved = wide_move(
                part.astype(BF), digit, sign, lambda p, h=hop, s=sign: 0 <= p + s * h < radix
            )
            carried = moved.astype(F32)
        total = total + carried
    return total


def slow_exchange(value, digit):
    place = place_in(digit)
    radix = digit[1]
    got = [pick_half(value, place, 0)]
    for mask in range(1, radix):
        got.append(wide_flip(pick_half(value, place ^ mask, 0), mask * digit[0]))
    stacked = jnp.stack(got, 0)
    return jnp.stack([pick_half(stacked, place ^ src, 0) for src in range(radix)], 0)


def pair_sum(value):
    return value + narrow_flip(value, 1)


def sum_all(value):
    value = pair_sum(value)
    value = value + narrow_flip(value, 2)
    bit = 1
    while bit < lax.axis_size(WD):
        value = value + wide_flip(value, bit)
        bit *= 2
    return value


def narrow_total(value):
    place = lax.axis_index(NR) % 2
    cols = value.shape[1] // 2
    low, high = value[:, :cols], value[:, cols:]
    mine = jnp.where(place == 0, low, high)
    other = jnp.where(place == 0, high, low)
    part = (mine + narrow_flip(other, 1)).astype(BF)
    part = part.astype(F32) + narrow_flip(part, 2).astype(F32)
    mate = narrow_flip(part, 1)
    return jnp.concatenate(
        [jnp.where(place == 0, part, mate), jnp.where(place == 0, mate, part)], 1
    )


def sinusoid(positions, extent):
    half_extent = extent // 2
    frequency = jnp.exp(
        jnp.arange(half_extent, dtype=F32) * (-2.0 * math.log(10000.0) / extent)
    )
    angles = positions.astype(F32)[:, None] * frequency[None, :]
    return jnp.concatenate([jnp.sin(angles), jnp.cos(angles)], axis=1)


def low(value):
    return value.astype(BF)


def mm(left, right):
    return jnp.dot(left, right, preferred_element_type=F32)


def mm_tn(left, right):
    return lax.dot_general(left, right, (((0,), (0,)), ((), ())), preferred_element_type=F32)


def mm_nt(left, right):
    return lax.dot_general(left, right, (((1,), (1,)), ((), ())), preferred_element_type=F32)


def col_sum(value):
    return jnp.sum(value, 0)


def layer_norm(value, gain, bias):
    center = value - jnp.mean(value, -1, keepdims=True)
    inv = lax.rsqrt(jnp.mean(center * center, -1, keepdims=True) + EPS_NORM)
    normed = center * inv
    return (normed * gain + bias, (normed, inv))


def norm_back(grad, saved, gain):
    normed, inv = saved
    grad_n = grad * gain
    grad_in = inv * (
        grad_n
        - jnp.mean(grad_n, -1, keepdims=True)
        - normed * jnp.mean(grad_n * normed, -1, keepdims=True)
    )
    return (grad_in, col_sum(grad * normed), col_sum(grad))


def gelu_value(upper):
    return 0.5 * upper * (1.0 + lax.erf(upper * ROOT_HALF))


def gelu_slope(upper):
    return (
        0.5 * (1.0 + lax.erf(upper * ROOT_HALF))
        + upper * jnp.exp(-0.5 * upper * upper) * INV_ROOT_TWO_PI
    )


def group_targets(pix, groups):
    rows = pix.astype(F32)
    masks = [(groups == g).astype(F32)[None, :] for g in range(GROUPS)]
    per_group = pix.shape[-1] // GROUPS

    def spread(parts):
        return sum(part * mask for part, mask in zip(parts, masks))

    means = [jnp.sum(rows * mask, -1, keepdims=True) / per_group for mask in masks]
    center = rows - spread(means)
    squares = center * center
    scale = [
        lax.rsqrt(jnp.sum(squares * mask, -1, keepdims=True) / per_group + TARGET_EPS)
        for mask in masks
    ]
    return center * spread(scale)


def heads_of(value, clips):
    rows, width = value.shape
    return value.reshape(clips, rows // clips, width // HD, HD)


def attention_forward(queries, keys, values):
    scores = (
        jnp.einsum("cqhd,ckhd->chqk", queries, keys, preferred_element_type=F32) * HD**-0.5
    )
    peak = jnp.max(scores, -1, keepdims=True)
    exp_scores = jnp.exp(scores - peak)
    total = jnp.sum(exp_scores, -1, keepdims=True)
    mixed = jnp.einsum(
        "chqk,ckhd->cqhd", low(exp_scores / total), values, preferred_element_type=F32
    )
    return (mixed, peak + jnp.log(total))


def attention_backward(queries, keys, values, log_total, grad_low):
    scores = (
        jnp.einsum("cqhd,ckhd->chqk", queries, keys, preferred_element_type=F32) * HD**-0.5
    )
    prob = jnp.exp(scores - log_total)
    grad_v = jnp.einsum("chqk,cqhd->ckhd", low(prob), grad_low, preferred_element_type=F32)
    grad_p = jnp.einsum("cqhd,ckhd->chqk", grad_low, values, preferred_element_type=F32)
    grad_s = low(prob * (grad_p - jnp.sum(prob * grad_p, -1, keepdims=True)))
    grad_q = (
        jnp.einsum("chqk,ckhd->cqhd", grad_s, keys, preferred_element_type=F32) * HD**-0.5
    )
    grad_k = (
        jnp.einsum("chqk,cqhd->ckhd", grad_s, queries, preferred_element_type=F32) * HD**-0.5
    )
    return (grad_q, grad_k, grad_v)


def gram_of(rows):
    return lax.dot_general(
        rows, rows, (((0,), (0,)), ((), ())), precision=HIGH, preferred_element_type=F32
    )


def pack_symmetric(gram):
    block = gram.shape[0] // 3
    return jnp.concatenate(
        [
            gram[i * block : (i + 1) * block, j * block : (j + 1) * block]
            for i in range(3)
            for j in range(i, 3)
        ],
        0,
    )


def unpack_symmetric(packed):
    block = packed.shape[1]
    tiles = {}
    at = 0
    for i in range(3):
        for j in range(i, 3):
            tile = packed[at : at + block]
            at += block
            tiles[i, j] = tile
            if i != j:
                tiles[j, i] = tile.T
    return jnp.concatenate(
        [jnp.concatenate([tiles[i, j] for j in range(3)], 1) for i in range(3)], 0
    )


def group_total(value):
    place = lax.axis_index(NR) % 2
    parts = value.reshape((2, value.shape[0] // 2) + value.shape[1:])
    mine = pick_half(parts, place, 0) + narrow_flip(pick_half(parts, 1 - place, 0), 1)
    rows = mine.shape[0] // 2
    one, two = mine[:rows], mine[rows:]
    digits = wide_digits(lax.axis_size(WD))
    bits = []
    bit = 1
    while bit < digits[-1][0]:
        bits.append(bit)
        bit *= 2
    for bit in bits:
        one = one + wide_flip(one, bit)
    one = one + narrow_flip(one, 2)
    two = two + narrow_flip(two, 2)
    for bit in bits:
        two = two + wide_flip(two, bit)
    mine = jnp.concatenate([one, two], 0)
    return both(mine, narrow_flip(mine, 1), place, 0).reshape(value.shape)


def hdot(left, right):
    return jnp.dot(left, right, precision=HIGH, preferred_element_type=F32)


def iterate(gram):
    eye = jnp.eye(gram.shape[0], dtype=F32)
    product = None
    for step in range(NS_STEPS):
        poly = NS_A * eye + NS_B * gram + NS_C * hdot(gram, gram)
        product = poly if product is None else hdot(poly, product)
        if step < NS_STEPS - 1:
            gram = hdot(hdot(poly, gram), poly)
    return product


def adam_update(weight, first, second, gradient, rate, decay):
    first_new = BETA_ONE * first + (1.0 - BETA_ONE) * gradient
    second_new = BETA_TWO * second + (1.0 - BETA_TWO) * gradient * gradient
    direction = (
        first_new
        / (1.0 - BETA_ONE**STEP)
        / (jnp.sqrt(second_new / (1.0 - BETA_TWO**STEP)) + EPS_ADAM)
    )
    return (first_new, second_new, weight - rate * (direction + decay * weight))


def pad_rows(value, rows, axis):
    if value.shape[axis] == rows:
        return value
    widths = [(0, 0)] * value.ndim
    widths[axis] = (0, rows - value.shape[axis])
    return jnp.pad(value, widths)


def per_device(
    pixels,
    visible,
    masked,
    groups,
    enc_qkv,
    enc_qkv_mom,
    enc_out,
    enc_out_mom,
    enc_up,
    enc_up_mom,
    enc_down,
    enc_down_mom,
    dec_qkv,
    dec_qkv_mom,
    dec_out,
    dec_out_mom,
    dec_up,
    dec_up_mom,
    dec_down,
    dec_down_mom,
    embed,
    embed_m,
    embed_v,
    enc_to_dec,
    enc_to_dec_m,
    enc_to_dec_v,
    head,
    head_m,
    head_v,
    vectors,
    vectors_m,
    vectors_v,
):
    wide = lax.axis_size(WD)
    me = lax.axis_index(NR)
    half, clip = me % 2, me // 2
    slow = wide_digits(wide)[-1]
    fast = slow[0]
    plane = place_in(slow)
    clips, vis = visible.shape
    tubs = pixels.shape[1]
    own = tubs // 2
    rows = clips * vis

    n_up = enc_up.shape[1]
    n_q = enc_qkv.shape[2]
    n_out = enc_out.shape[0]
    n_emb = embed.shape[0] // QN
    n_link = enc_to_dec.shape[0] * DD // D // QN
    m_up = dec_up.shape[1]
    m_qkv = dec_qkv.shape[1]
    m_out = dec_out.shape[0]
    m_head = head.shape[0] * (PIX // DD)

    up_rows, down_rows = enc_up.T, enc_down
    qkv_rows = jnp.swapaxes(enc_qkv, 1, 2).reshape(3 * n_q, D)
    dqkv_rows, dup_rows = dec_qkv.T, dec_up.T
    head_rows = head.reshape(m_head, DD)
    emb_rows = lax.dynamic_slice_in_dim(embed, me * n_emb, n_emb, 0)
    link_rows = lax.dynamic_slice_in_dim(enc_to_dec.reshape(-1, D), me * n_link, n_link, 0)
    pack_a = low(jnp.concatenate([emb_rows, link_rows], 0))
    pack_b = low(jnp.concatenate([qkv_rows, enc_out], 0))
    pack_c = low(jnp.concatenate([up_rows, down_rows], 0))
    pack_d = low(jnp.concatenate([dup_rows, dqkv_rows, dec_out, dec_down, head_rows], 0))
    full_a = narrow_gather(wide_gather(pack_a))
    embed_w = jnp.swapaxes(full_a[:, :, :n_emb], 0, 1).reshape(PIX, D)
    link_w = jnp.swapaxes(full_a[:, :, n_emb:], 0, 1).reshape(D, DD)
    full_b = wide_gather(pack_b)
    w_qkv = [full_b[:, k * n_q : (k + 1) * n_q].reshape(wide * n_q, D) for k in range(3)]
    w_out = full_b[:, 3 * n_q :].reshape(wide * n_out, D)
    full_c = wide_gather(pack_c)
    w_up = full_c[:, :n_up].reshape(wide * n_up, D)
    w_down = full_c[:, n_up:].reshape(wide * n_up, D)
    full_d = jnp.swapaxes(narrow_gather(wide_gather(pack_d)), 0, 1)
    at, taken = 0, []
    for extent in (m_up, m_qkv, m_out, m_up, m_head):
        taken.append(full_d[:, :, at : at + extent].reshape(wide * QN * extent, DD))
        at += extent
    d_up, d_qkv, d_out, d_down, d_head = taken
    d_head = d_head.reshape(DD, PIX)

    table = vector_layout()

    def vec_of(name):
        offset, extent = table[name]
        return vectors[offset : offset + extent]

    def share_of(name):
        offset, extent = table[name]
        share = extent // QN
        return lax.dynamic_slice_in_dim(vectors, offset + me * share, share)

    grads = {}

    vis_rows = visible.reshape(rows)
    tube_ids = jnp.arange(tubs, dtype=jnp.int32)
    vis_pix = mm(low(vis_rows[:, None] == tube_ids[None, :]), pixels[0]).astype(BF)
    stream = mm(vis_pix, embed_w) + vec_of("emb_b") + sinusoid(vis_rows, D)
    hid1, saved1 = layer_norm(stream, vec_of("eln1_g"), vec_of("eln1_b"))
    hid1 = low(hid1)
    eq = low(mm_nt(hid1, w_qkv[0]) + share_of("eq_b"))
    ek = low(mm_nt(hid1, w_qkv[1]))
    ev = low(mm_nt(hid1, w_qkv[2]) + share_of("ev_b"))
    mixed, elog = attention_forward(heads_of(eq, clips), heads_of(ek, clips), heads_of(ev, clips))
    eattn = low(mixed.reshape(eq.shape))
    middle = stream + narrow_total(mm(eattn, w_out)) + vec_of("eout_b")
    hid2, saved2 = layer_norm(middle, vec_of("eln2_g"), vec_of("eln2_b"))
    hid2 = low(hid2)
    upper = mm_nt(hid2, w_up) + share_of("eup_b")
    active = low(gelu_value(upper))
    enc_result = middle + narrow_total(mm(active, w_down)) + vec_of("edown_b")
    final, fsaved = layer_norm(enc_result, vec_of("elnf_g"), vec_of("elnf_b"))
    final = low(final)

    clip_final = lax.dynamic_slice_in_dim(final, clip * vis, vis, 0)
    latent = mm(clip_final, link_w) + vec_of("in_b")
    clip_vis = pick_half(visible, clip, 0)
    own_pos = half * own + jnp.arange(own, dtype=jnp.int32)
    pick = (own_pos[:, None] == clip_vis[None, :]).astype(F32)
    shown = jnp.sum(pick, -1, keepdims=True)
    hidden_row = 1.0 - shown
    dstream = (
        jnp.dot(pick, latent, precision=HIGHEST)
        + hidden_row * vec_of("mask")
        + sinusoid(own_pos, DD)
    )
    dh1, dsaved1 = layer_norm(dstream, vec_of("dln1_g"), vec_of("dln1_b"))
    dh1 = low(dh1)
    joined = mm_nt(dh1, d_qkv)
    dq = low(joined[:, :DD] + vec_of("dq_b"))
    dkv = low(
        jnp.concatenate([joined[:, DD : 2 * DD], joined[:, 2 * DD :] + vec_of("dv_b")], 1)
    )
    all_kv = both(dkv, narrow_flip(dkv, 1), half, 0).reshape(tubs, 2 * DD)
    dk, dv = all_kv[:, :DD], all_kv[:, DD:]
    mixed, dlog = attention_forward(heads_of(dq, 1), heads_of(dk, 1), heads_of(dv, 1))
    dattn = low(mixed.reshape(dq.shape))
    dmiddle = dstream + mm(dattn, d_out) + vec_of("dout_b")
    dh2, dsaved2 = layer_norm(dmiddle, vec_of("dln2_g"), vec_of("dln2_b"))
    dh2 = low(dh2)
    dupper = mm_nt(dh2, d_up) + vec_of("dup_b")
    dactive = low(gelu_value(dupper))
    dresult = dmiddle + mm(dactive, d_down) + vec_of("ddown_b")
    hf, hsaved = layer_norm(dresult, vec_of("dlnf_g"), vec_of("dlnf_b"))
    hf = low(hf)
    predicted = mm(hf, d_head) + vec_of("head_b")
    own_pix = lax.dynamic_slice_in_dim(pixels[0], half * own, own, 0)
    error = (predicted - group_targets(own_pix, groups)) * hidden_row
    loss_part = jnp.sum(error * error)
    pred_grad = error * (2.0 / (clips * wide * (tubs - vis) * PIX))

    pred_low = low(pred_grad)
    g_head = mm_tn(hf, pred_low)
    grads["head_b"] = col_sum(pred_grad)
    dgrad, grads["dlnf_g"], grads["dlnf_b"] = norm_back(
        mm_nt(pred_low, d_head), hsaved, vec_of("dlnf_g")
    )
    down_low = low(dgrad)
    g_ddown = mm_tn(dactive, down_low)
    grads["ddown_b"] = col_sum(dgrad)
    upper_low = low(mm_nt(down_low, d_down) * gelu_slope(dupper))
    g_dup = mm_tn(upper_low, dh2)
    grads["dup_b"] = col_sum(upper_low.astype(F32))
    mid_grad, grads["dln2_g"], grads["dln2_b"] = norm_back(
        mm(upper_low, d_up), dsaved2, vec_of("dln2_g")
    )
    mid_grad = mid_grad + dgrad
    out_low = low(mid_grad)
    g_dout = mm_tn(dattn, out_low)
    grads["dout_b"] = col_sum(mid_grad)
    attn_grad = low(mm_nt(out_low, d_out))
    gq, gk, gv = attention_backward(
        heads_of(dq, 1), heads_of(dk, 1), heads_of(dv, 1), dlog, heads_of(attn_grad, 1)
    )
    gkv = jnp.concatenate([gk.reshape(2, own, DD), gv.reshape(2, own, DD)], 2)
    gkv = pick_half(gkv, half, 0) + narrow_flip(low(pick_half(gkv, 1 - half, 0)), 1).astype(F32)
    joined_low = jnp.concatenate([low(gq.reshape(own, DD)), low(gkv)], 1)
    sums = col_sum(joined_low.astype(F32))
    grads["dq_b"], grads["dv_b"] = sums[:DD], sums[2 * DD :]
    g_dqkv = mm_tn(joined_low, dh1)
    sgrad, grads["dln1_g"], grads["dln1_b"] = norm_back(
        mm(joined_low, d_qkv), dsaved1, vec_of("dln1_g")
    )
    din_grad = sgrad + mid_grad
    grads["mask"] = jnp.sum(hidden_row * din_grad, 0)
    latent_part = lax.dot_general(
        pick, din_grad, (((0,), (0,)), ((), ())), precision=HIGHEST, preferred_element_type=F32
    )

    def dec_parts(value, extent):
        return low(value).reshape(4, fast, QN, extent, DD)

    cut = m_head - m_qkv if False else m_up - m_qkv
    p_head = dec_parts(g_head.reshape(-1, DD), m_head)
    dec_pack = jnp.stack(
        [
            dec_parts(g_dup, m_up),
            jnp.concatenate([dec_parts(g_dqkv, m_qkv), p_head[:, :, :, :cut]], 3),
            jnp.concatenate([dec_parts(g_dout, m_out), p_head[:, :, :, cut:]], 3),
            dec_parts(g_ddown, m_up),
        ],
        0,
    )
    dec_pack = dec_pack.reshape(4, 4, fast, 2, 2, m_up, DD).transpose(4, 0, 2, 3, 1, 5, 6)
    dec_sum = pick_half(dec_pack, half, 0).astype(F32) + narrow_flip(
        pick_half(dec_pack, 1 - half, 0), 1
    ).astype(F32)

    def fast_scatter(value, axis):
        digits = wide_digits(wide)[:-1]
        shape = value.shape
        value = value.reshape(
            shape[:axis] + tuple(radix for _, radix in digits[::-1]) + shape[axis + 1 :]
        )
        for count, digit in enumerate(digits):
            value = line_scatter(value, digit, axis + len(digits) - 1 - count)
        return value

    dec_sum = line_scatter(fast_scatter(dec_sum, 1), slow, 0)
    dec_sum = pick_half(dec_sum, clip, 0) + narrow_flip(
        low(pick_half(dec_sum, 1 - clip, 0)), 2
    ).astype(F32)

    latent_pair = pair_sum(latent_part)
    latent_grad = both(low(latent_pair), narrow_flip(low(latent_pair), 2), clip, 0)
    latent_low = latent_grad.reshape(rows, DD)
    g_link = mm_tn(final, latent_low)
    grads["in_b"] = col_sum(latent_low.astype(F32))
    egrad, grads["elnf_g"], grads["elnf_b"] = norm_back(
        mm_nt(latent_low, link_w), fsaved, vec_of("elnf_g")
    )
    down_low = low(egrad)
    g_down = mm_tn(active, down_low)
    grads["edown_b"] = col_sum(egrad)
    upper_low = low(mm_nt(down_low, w_down) * gelu_slope(upper))
    g_up = mm_tn(upper_low, hid2)
    grads["eup_b"] = col_sum(upper_low.astype(F32))

    def enc_parts(value, extent):
        return low(value).reshape(4, fast, extent, D).transpose(1, 0, 2, 3)

    sum_up = fast_scatter(enc_parts(g_up, n_up), 0)
    sum_down = fast_scatter(enc_parts(g_down, n_up), 0)
    mid_grad, grads["eln2_g"], grads["eln2_b"] = norm_back(
        narrow_total(mm(upper_low, w_up)), saved2, vec_of("eln2_g")
    )
    mid_grad = mid_grad + egrad
    out_low = low(mid_grad)
    g_out = mm_tn(eattn, out_low)
    grads["eout_b"] = col_sum(mid_grad)
    attn_grad = low(mm_nt(out_low, w_out))
    gq, gk, gv = attention_backward(
        heads_of(eq, clips), heads_of(ek, clips), heads_of(ev, clips), elog, heads_of(attn_grad, clips)
    )
    lows = [low(g.reshape(eq.shape)) for g in (gq, gk, gv)]
    grads["eq_b"] = col_sum(lows[0].astype(F32))
    grads["ev_b"] = col_sum(lows[2].astype(F32))
    g_qkv = [mm_tn(g, hid1) for g in lows]
    hid1_grad = narrow_total(sum(mm(g, w) for g, w in zip(lows, w_qkv)))
    sgrad, grads["eln1_g"], grads["eln1_b"] = norm_back(hid1_grad, saved1, vec_of("eln1_g"))
    stream_grad = sgrad + mid_grad
    g_embed = mm_tn(vis_pix, low(stream_grad))
    grads["emb_b"] = col_sum(stream_grad)
    g_embed = pick_half(g_embed.reshape(wide, QN, n_emb, D), me, 1)
    g_link = pick_half(g_link.reshape(wide, QN, n_link, D), me, 1)
    part_qkv = jnp.concatenate([enc_parts(g, n_q) for g in g_qkv], 2)
    part_rest = jnp.concatenate(
        [enc_parts(g_out, n_out), enc_parts(g_embed, n_emb), enc_parts(g_link, n_link)], 2
    )
    sum_qkv = fast_scatter(pad_rows(part_qkv, n_up, 2), 0)
    sum_rest = fast_scatter(pad_rows(part_rest, n_up, 2), 0)
    enc_sum = line_scatter(jnp.stack([sum_up, sum_qkv, sum_rest, sum_down], 0), slow, 0)

    leading = jnp.where(me == 0, 1.0, 0.0)

    def spread(share):
        full = jnp.zeros((share.shape[0] * QN,), F32)
        return lax.dynamic_update_slice_in_dim(full, share, me * share.shape[0], 0)

    pieces = []
    for name in table:
        if name in ("eq_b", "ev_b", "eup_b"):
            pieces.append(spread(grads[name]))
        elif name[0] == "e" or name == "in_b":
            pieces.append(leading * grads[name])
        else:
            pieces.append(grads[name])
    vec_total = sum_all(jnp.concatenate(pieces + [loss_part[None]]).reshape(1, -1))[0]
    loss_sum = vec_total[-1]
    vec_total = vec_total[:-1]
    squares = jnp.sum(dec_sum * dec_sum) + jnp.sum(enc_sum * enc_sum)
    square_total = sum_all(jnp.broadcast_to(squares, (8, 128)))[0, 0]
    grad_norm = jnp.sqrt(square_total + jnp.sum(vec_total * vec_total))
    factor = jnp.minimum(1.0, CLIP_AT / grad_norm)

    def plane_rows(parts):
        return jnp.stack([pad_rows(low(part), parts[0].shape[0], 0) for part in parts], 0)

    qkv_mom_rows = jnp.swapaxes(enc_qkv_mom, 1, 2).reshape(3 * n_q, D)
    enc_moms = [enc_up_mom.T, qkv_mom_rows, enc_out_mom, enc_down_mom]
    dec_moms = [dec_up_mom.T, dec_qkv_mom.T, dec_out_mom, dec_down_mom]
    enc_mom = slow_exchange(plane_rows(enc_moms), slow)
    dec_mom = slow_exchange(plane_rows(dec_moms), slow)

    def valid(total, counts):
        count = jnp.asarray(counts, jnp.int32)[plane]
        return (jnp.arange(total, dtype=jnp.int32) < count).astype(F32)[None, :, None]

    enc_slab = MOMENTUM * enc_mom.astype(F32) + factor * enc_sum * valid(
        n_up, [n_up, 3 * n_q, n_out, n_up]
    )
    dec_slab = MOMENTUM * dec_mom.astype(F32) + factor * dec_sum * valid(
        m_up, [m_up, m_qkv, m_out, m_up]
    )
    enc_slab = enc_slab.reshape(-1, D)
    dec_slab = dec_slab.reshape(-1, DD)
    enc_packed = pack_symmetric(gram_of(enc_slab))
    dec_packed = pack_symmetric(gram_of(dec_slab))
    width = enc_packed.shape[1]
    packed = group_total(jnp.concatenate([enc_packed, dec_packed.reshape(-1, width)], 0))
    cut_at = enc_packed.shape[0]
    ortho = []
    for slab, gram in (
        (enc_slab, unpack_symmetric(packed[:cut_at])),
        (dec_slab, unpack_symmetric(packed[cut_at:].reshape(dec_packed.shape))),
    ):
        scale = 1.0 / (jnp.sqrt(jnp.trace(gram)) + 1e-07)
        ortho.append(hdot(slab * scale, iterate(gram * (scale * scale))))
    enc_ortho = slow_exchange(low(ortho[0]).reshape(4, n_up, D), slow).astype(F32)
    dec_ortho = slow_exchange(low(ortho[1]).reshape(4, m_up, DD), slow).astype(F32)
    enc_grad = slow_exchange(low(enc_sum), slow).astype(F32) * factor
    dec_grad = slow_exchange(low(dec_sum), slow).astype(F32) * factor

    def turned(value):
        return value.T

    def same(value):
        return value

    def unqkv(value):
        return jnp.swapaxes(value.reshape(3, n_q, D), 1, 2)

    results = [loss_sum, grad_norm]
    for weight, mom, grad, part, side, largest in [
        (enc_qkv, enc_qkv_mom, enc_grad[1, : 3 * n_q], enc_ortho[1, : 3 * n_q], unqkv, 3 * D),
        (enc_out, enc_out_mom, enc_grad[2, :n_out], enc_ortho[2, :n_out], same, D),
        (enc_up, enc_up_mom, enc_grad[0], enc_ortho[0], turned, FE),
        (enc_down, enc_down_mom, enc_grad[3], enc_ortho[3], same, FE),
        (dec_qkv, dec_qkv_mom, dec_grad[1, :m_qkv], dec_ortho[1, :m_qkv], turned, 3 * DD),
        (dec_out, dec_out_mom, dec_grad[2, :m_out], dec_ortho[2, :m_out], same, DD),
        (dec_up, dec_up_mom, dec_grad[0], dec_ortho[0], turned, FD),
        (dec_down, dec_down_mom, dec_grad[3], dec_ortho[3], same, FD),
    ]:
        new_weight = weight * (1.0 - RATE_MUON * DECAY) - RATE_MUON * 0.2 * math.sqrt(
            largest
        ) * side(part)
        results += [new_weight, MOMENTUM * mom + side(grad)]
    rest = enc_grad[2, n_out : n_out + n_emb + n_link]
    rest = narrow_gather(rest)
    embed_grad = rest[:, :n_emb].reshape(embed.shape)
    link_grad = rest[:, n_emb:].reshape(enc_to_dec.shape)
    head_grad = jnp.concatenate([dec_grad[1, m_qkv:], dec_grad[2, m_out:]], 0).reshape(head.shape)
    for weight, first, second, grad, rate, decay in [
        (embed, embed_m, embed_v, embed_grad, RATE_ADAM, DECAY),
        (enc_to_dec, enc_to_dec_m, enc_to_dec_v, link_grad, RATE_ADAM, DECAY),
        (head, head_m, head_v, head_grad, RATE_ADAM, DECAY),
        (vectors, vectors_m, vectors_v, factor * vec_total, RATE_VECTOR, 0.0),
    ]:
        first_new, second_new, new_weight = adam_update(weight, first, second, grad, rate, decay)
        results += [first_new, second_new, new_weight]
    return tuple(results)


def solution(mesh):
    enc, dec = (NR, WD), (WD, NR)
    muon = [P(None, None, enc), P(enc, None), P(None, enc), P(enc, None)]
    muon += [P(None, dec), P(dec, None), P(None, dec), P(dec, None)]
    pairs = [spec for spec in muon for _ in range(2)]
    adam = [P(WD, None)] * 6 + [P(dec, None)] * 3 + [P()] * 3
    in_specs = [P(WD, None, None), P(WD, None), P(WD, None), P()] + pairs + adam
    out_specs = [P(), P()] + pairs + adam
    return jax.shard_map(
        per_device,
        mesh=mesh,
        in_specs=tuple(in_specs),
        out_specs=tuple(out_specs),
        check_vma=False,
    )
```

profile of v0, /device:TPU:0, one launch (start us, length us, event | category | flops | bytes accessed | tf_op | source)
XLA Modules:
  0.0 830.7 jit_solution(7909163304227388682)
XLA Ops:
  4.1 5.6 collective-permute-start
  12.8 4.6 collective-permute-start.9
  21.9 3.9 collective-permute-start.29
  28.5 5.3 fusion.21
  41.2 4.9 multiply_reduce_fusion.5
  53.0 3.6 collective-permute-done.4
  60.0 6.6 collective-permute-done.5
  68.0 5.5 collective-permute-start.19
  75.3 3.9 collective-permute-start.82
  81.9 6.2 collective-permute-done.33
  100.1 4.5 collective-permute-done.23
  113.6 6.9 collective-permute-done.7
  143.5 9.6 %collective-permute-done.25 = bf16[4,192,768]{2,1,0:T(8,128)(2,1)} collective-permute-done((bf16[4,192,768]{2,1,0:T(8,128)(2,1)}, bf16[4,192,768]{2,1,0:T(8,128)(2,1)}, u32[]{:S(2)}, u32[]{:S(2)}) %collective-permute-start.25) | collective-permute-done | bytes 1179680 | tf_op jit(solution)/shard_map/ppermute | solution.py:89
  156.7 5.9 collective-permute-done.17
  169.8 4.1 multiply_sine_fusion
  177.9 4.5 collective-permute-done.27
  202.9 3.4 fusion.307
  224.3 12.4 %multiply_reduce_fusion.1 = (f32[6,784]{1,0:T(8,128)S(1)}, f32[6,784,1568]{2,1,0:T(8,128)}) fusion(bf16[784,6,64]{0,2,1:T(8,128)(2,1)S(1)} %bitcast.711, bf16[1568,6,64]{0,2,1:T(8,128)(2,1)S(1)} %bitcast.701), kind=kOutput, calls=%fused_computation.6 | convolution fusion | flops 958858624 | bytes 31328640 | tf_op jit(solution)/shard_map/cqhd,ckhd->chqk/dot_general | solution.py:294
  236.6 12.6 %fusion = f32[6,784]{1,0:T(8,128)S(1)} fusion(f32[6,784,1568]{2,1,0:T(8,128)} %get-tuple-element.270, f32[6,784]{1,0:T(8,128)S(1)} %get-tuple-element.269), kind=kLoop, calls=%fused_computation.5 | loop fusion | flops 22122912 | bytes 29541120 | tf_op jit(solution)/shard_map/reduce_sum | solution.py:285
  249.3 14.4 %fusion.72 = bf16[6,64,784]{2,1,0:T(8,128)(2,1)} fusion(bf16[1568,6,64]{0,2,1:T(8,128)(2,1)S(1)} %bitcast.713, f32[6,784,1568]{2,1,0:T(8,128)} %get-tuple-element.270, f32[6,784]{1,0:T(8,128)S(1)} %fusion, f32[6,784]{1,0:T(8,128)S(1)} %get-tuple-element.269), kind=kOutput, calls=%fused_computation.123 | convolution fusion | flops 973916160 | bytes 31347456 | tf_op jit(solution)/shard_map/chqk,ckhd->cqhd/dot_general | solution.py:286
  270.4 4.8 multiply_reduce_fusion.2
  277.9 3.7 convert_reduce_fusion
  287.1 14.3 %fusion.18 = f32[1,1568,6,64]{1,3,2,0:T(8,128)} fusion(bf16[784,6,64]{0,2,1:T(8,128)(2,1)S(1)} %bitcast.707, f32[6,784,1568]{2,1,0:T(8,128)} %get-tuple-element.270, f32[6,784]{1,0:T(8,128)S(1)} %log_add_fusion), kind=kOutput, calls=%fused_computation.53 | convolution fusion | flops 966239232 | bytes 32532864 | tf_op jit(solution)/shard_map/chqk,cqhd->ckhd/dot_general | solution.py:297
  301.4 24.2 %multiply_reduce_fusion = (f32[6,784]{1,0:T(8,128)S(1)}, f32[6,784,1568]{2,1,0:T(8,128)}) fusion(f32[6,784,1568]{2,1,0:T(8,128)} %get-tuple-element.270, f32[6,784]{1,0:T(8,128)S(1)} %log_add_fusion, bf16[784,6,64]{0,2,1:T(8,128)(2,1)S(1)} %bitcast.708, bf16[1568,6,64]{0,2,1:T(8,128)(2,1)S(1)} %bitcast.714), kind=kOutput, calls=%fused_computation.1 | convolution fusion | flops 973610368 | bytes 60850944 | tf_op jit(solution)/shard_map/cqhd,ckhd->chqk/dot_general | solution.py:298
  325.6 25.7 %multiply_convert_fusion = bf16[6,784,1568]{2,1,0:T(8,128)(2,1)} fusion(f32[6,784,1568]{2,1,0:T(8,128)} %get-tuple-element.280, f32[6,784,1568]{2,1,0:T(8,128)} %get-tuple-element.270, f32[6,784]{1,0:T(8,128)S(1)} %get-tuple-element.279, f32[6,784]{1,0:T(8,128)S(1)} %log_add_fusion), kind=kLoop, calls=%fused_computation | loop fusion | flops 36879360 | bytes 73796352 | tf_op jit(solution)/shard_map/convert_element_type | solution.py:208
  351.2 11.5 %fusion.71 = bf16[6,64,784]{2,1,0:T(8,128)(2,1)} fusion(bf16[1568,6,64]{0,2,1:T(8,128)(2,1)} %bitcast.702, bf16[6,784,1568]{2,1,0:T(8,128)(2,1)} %multiply_convert_fusion), kind=kOutput, calls=%fused_computation.122 | convolution fusion | flops 944713728 | bytes 16558080 | tf_op jit(solution)/shard_map/chqk,ckhd->cqhd/dot_general | solution.py:301
  362.8 9.5 %fusion.17 = f32[1,1568,6,64]{1,3,2,0:T(8,128)} fusion(bf16[784,6,64]{0,2,1:T(8,128)(2,1)S(1)} %bitcast.712, bf16[6,784,1568]{2,1,0:T(8,128)(2,1)} %multiply_convert_fusion), kind=kOutput, calls=%fused_computation.52 | convolution fusion | flops 944713728 | bytes 17762304 | tf_op jit(solution)/shard_map/chqk,cqhd->ckhd/dot_general | solution.py:304
  372.3 4.8 reshape.842
  377.1 5.7 copy.238
  382.8 4.8 reshape.841
  387.6 5.7 copy.237
  396.2 5.0 convolution_convert_fusion.1
  401.2 3.6 convert_element_type.682
  415.8 4.9 convolution_convert_fusion
  457.3 3.8 collective-permute-done.43
  487.4 8.3 collective-permute-done.63
  505.1 35.3 %collective-permute-done.64 = bf16[4,96,768]{2,1,0:T(8,128)(2,1)S(1)} collective-permute-done((bf16[4,96,768]{2,1,0:T(8,128)(2,1)S(1)}, bf16[4,96,768]{2,1,0:T(8,128)(2,1)S(1)}, u32[]{:S(2)}, u32[]{:S(2)}) %collective-permute-start.64) | collective-permute-done | bytes 589856 | tf_op jit(solution)/shard_map/ppermute | solution.py:89
  541.1 5.3 collective-permute-start.66
  548.8 16.3 %collective-permute-done.55 = bf16[2,4,48,384]{3,2,0,1:T(8,128)(2,1)S(1)} collective-permute-done((bf16[2,4,48,384]{3,2,0,1:T(8,128)(2,1)S(1)}, bf16[2,4,48,384]{3,2,0,1:T(8,128)(2,1)S(1)}, u32[]{:S(2)}, u32[]{:S(2)}) %collective-permute-start.55) | collective-permute-done | bytes 294944 | tf_op jit(solution)/shard_map/ppermute | solution.py:84
  565.2 4.4 collective-permute-start.56
  572.4 4.6 collective-permute-done.56
  577.9 5.0 collective-permute-start.57
  584.3 5.3 collective-permute-done.67
  593.7 4.5 collective-permute-start.68
  606.4 10.6 %collective-permute-start.81 = (bf16[48,384]{1,0:T(8,128)(2,1)S(1)}, bf16[48,384]{1,0:T(8,128)(2,1)S(1)}, u32[]{:S(2)}, u32[]{:S(2)}) collective-permute-start(bf16[48,384]{1,0:T(8,128)(2,1)S(1)} %copy-done.169), channel_id=1, source_target_pairs={{0,16},{4,20},{8,24},{12,28},{16,0},{20,4},{24,8},{28,12},{1,17},{... | collective-permute-start | bytes 110600 | tf_op jit(solution)/shard_map/ppermute | solution.py:89
  649.3 4.6 collective-permute-done.93
  662.5 4.4 collective-permute-done.79
  666.9 4.5 collective-permute-done.78
  681.9 9.6 %collective-permute-done.84 = f32[480,256]{1,0:T(8,128)S(1)} collective-permute-done((f32[480,256]{1,0:T(8,128)S(1)}, f32[480,256]{1,0:T(8,128)S(1)}, u32[]{:S(2)}, u32[]{:S(2)}) %collective-permute-start.84) | collective-permute-done | bytes 491552 | tf_op jit(solution)/shard_map/ppermute | solution.py:89
  698.3 9.2 %collective-permute-done.85 = f32[480,256]{1,0:T(8,128)S(1)} collective-permute-done((f32[480,256]{1,0:T(8,128)S(1)}, f32[480,256]{1,0:T(8,128)S(1)}, u32[]{:S(2)}, u32[]{:S(2)}) %collective-permute-start.85) | collective-permute-done | bytes 491552 | tf_op jit(solution)/shard_map/ppermute | solution.py:93
  735.3 3.3 fusion.30
  741.7 3.4 fusion.328
  748.2 3.4 fusion.63
  751.7 3.4 fusion.67
  774.0 3.3 fusion.330
  777.3 3.4 fusion.61
  780.7 3.3 fusion.57
  784.0 3.2 fusion.59
  787.3 3.4 fusion.331
  790.7 3.4 fusion.55
  794.0 3.4 fusion.51
  797.4 3.5 fusion.53
  804.0 3.3 fusion.35
  822.5 3.5 collective-permute-done.90
  (1137 shorter events, 378.9 us)
Async XLA Ops:
  2.8 46.4 %collective-permute-start.3 = (bf16[60,768]{1,0:T(8,128)(2,1)S(1)}, bf16[60,768]{1,0:T(8,128)(2,1)S(1)}, u32[]{:S(2)}, u32[]{:S(2)}) collective-permute-start(bf16[60,768]{1,0:T(8,128)(2,1)S(1)} %pad_maximum_fusion.39), channel_id=1, source_target_pairs={{8,0},{12,4},{16,8},{20,12},{24,16},{28,20},{9,1},{13,5},{17,9},{2... | collective-permute-start | bytes 276488 | tf_op jit(solution)/shard_map/ppermute | solution.py:84
  4.1 42.7 %collective-permute-start = (bf16[60,768]{1,0:T(8,128)(2,1)S(1)}, bf16[60,768]{1,0:T(8,128)(2,1)S(1)}, u32[]{:S(2)}, u32[]{:S(2)}) collective-permute-start(bf16[60,768]{1,0:T(8,128)(2,1)S(1)} %pad_maximum_fusion.39), channel_id=1, source_target_pairs={{0,8},{4,12},{8,16},{12,20},{16,24},{20,28},{1,9},{5,13},{9,17},{1... | collective-permute-start | bytes 276488 | tf_op jit(solution)/shard_map/ppermute | solution.py:84
  11.5 63.8 %collective-permute-start.12 = (bf16[96,768]{1,0:T(8,128)(2,1)S(1)}, bf16[96,768]{1,0:T(8,128)(2,1)S(1)}, u32[]{:S(2)}, u32[]{:S(2)}) collective-permute-start(bf16[96,768]{1,0:T(8,128)(2,1)S(1)} %pad_maximum_fusion.32), channel_id=1, source_target_pairs={{8,0},{12,4},{16,8},{20,12},{24,16},{28,20},{9,1},{13,5},{17,9},{2... | collective-permute-start | bytes 442376 | tf_op jit(solution)/shard_map/ppermute | solution.py:84
  12.8 45.9 %collective-permute-start.9 = (bf16[96,768]{1,0:T(8,128)(2,1)S(1)}, bf16[96,768]{1,0:T(8,128)(2,1)S(1)}, u32[]{:S(2)}, u32[]{:S(2)}) collective-permute-start(bf16[96,768]{1,0:T(8,128)(2,1)S(1)} %pad_maximum_fusion.32), channel_id=1, source_target_pairs={{0,8},{4,12},{8,16},{12,20},{16,24},{20,28},{1,9},{5,13},{9,17},{1... | collective-permute-start | bytes 442376 | tf_op jit(solution)/shard_map/ppermute | solution.py:84
  21.9 29.8 %collective-permute-start.29 = (bf16[192,384]{1,0:T(8,128)(2,1)S(1)}, bf16[192,384]{1,0:T(8,128)(2,1)S(1)}, u32[]{:S(2)}, u32[]{:S(2)}) collective-permute-start(bf16[192,384]{1,0:T(8,128)(2,1)S(1)} %concatenate.186), channel_id=1, source_target_pairs={{0,8},{4,12},{8,16},{12,20},{16,24},{20,28},{1,9},{5,13},{9,17},{1... | collective-permute-start | bytes 442376 | tf_op jit(solution)/shard_map/ppermute | solution.py:84
  51.7 27.5 %collective-permute-start.32 = (bf16[192,384]{1,0:T(8,128)(2,1)S(1)}, bf16[192,384]{1,0:T(8,128)(2,1)S(1)}, u32[]{:S(2)}, u32[]{:S(2)}) collective-permute-start(bf16[192,384]{1,0:T(8,128)(2,1)S(1)} %concatenate.186), channel_id=1, source_target_pairs={{8,0},{12,4},{16,8},{20,12},{24,16},{28,20},{9,1},{13,5},{17,9},{2... | collective-permute-start | bytes 442376 | tf_op jit(solution)/shard_map/ppermute | solution.py:84
  56.6 10.7 %collective-permute-start.30 = (bf16[192,384]{1,0:T(8,128)(2,1)S(1)}, bf16[192,384]{1,0:T(8,128)(2,1)S(1)}, u32[]{:S(2)}, u32[]{:S(2)}) collective-permute-start(bf16[192,384]{1,0:T(8,128)(2,1)S(1)} %collective-permute-done.29), channel_id=1, source_target_pairs={{8,16},{12,20},{16,24},{20,28},{9,17},{13,21},{17,25},{21,29},{10,... | collective-permute-start | bytes 442376 | tf_op jit(solution)/shard_map/ppermute | solution.py:84
  58.7 33.3 %collective-permute-start.22 = (bf16[192,768]{1,0:T(8,128)(2,1)S(1)}, bf16[192,768]{1,0:T(8,128)(2,1)S(1)}, u32[]{:S(2)}, u32[]{:S(2)}) collective-permute-start(bf16[192,768]{1,0:T(8,128)(2,1)S(1)} %pad_maximum_fusion.27), channel_id=1, source_target_pairs={{8,0},{12,4},{16,8},{20,12},{24,16},{28,20},{9,1},{13,5},{17,9},{2... | collective-permute-start | bytes 884744 | tf_op jit(solution)/shard_map/ppermute | solution.py:84
  68.0 25.4 %collective-permute-start.19 = (bf16[192,768]{1,0:T(8,128)(2,1)S(1)}, bf16[192,768]{1,0:T(8,128)(2,1)S(1)}, u32[]{:S(2)}, u32[]{:S(2)}) collective-permute-start(bf16[192,768]{1,0:T(8,128)(2,1)S(1)} %pad_maximum_fusion.27), channel_id=1, source_target_pairs={{0,8},{4,12},{8,16},{12,20},{16,24},{20,28},{1,9},{5,13},{9,17},{1... | collective-permute-start | bytes 884744 | tf_op jit(solution)/shard_map/ppermute | solution.py:84
  75.3 551.5 %collective-permute-start.82 = (bf16[48,384]{1,0:T(8,128)(2,1)}, bf16[48,384]{1,0:T(8,128)(2,1)}, u32[]{:S(2)}, u32[]{:S(2)}) collective-permute-start(bf16[48,384]{1,0:T(8,128)(2,1)} %get-tuple-element.219), channel_id=1, source_target_pairs={{0,24},{4,28},{8,16},{12,20},{16,8},{20,12},{24,0},{28,4},{1,25},{... | collective-permute-start | bytes 110600 | tf_op jit(solution)/shard_map/ppermute | solution.py:89
  79.2 11.5 %collective-permute-start.13 = (bf16[96,768]{1,0:T(8,128)(2,1)S(1)}, bf16[96,768]{1,0:T(8,128)(2,1)S(1)}, u32[]{:S(2)}, u32[]{:S(2)}) collective-permute-start(bf16[96,768]{1,0:T(8,128)(2,1)S(1)} %collective-permute-done.12), channel_id=1, source_target_pairs={{8,0},{12,4},{16,8},{20,12},{9,1},{13,5},{17,9},{21,13},{10,2},{14... | collective-permute-start | bytes 442376 | tf_op jit(solution)/shard_map/ppermute | solution.py:84
  88.2 17.8 %collective-permute-start.6 = (bf16[4,60,768]{2,1,0:T(8,128)(2,1)S(1)}, bf16[4,60,768]{2,1,0:T(8,128)(2,1)S(1)}, u32[]{:S(2)}, u32[]{:S(2)}) collective-permute-start(bf16[4,60,768]{2,1,0:T(8,128)(2,1)S(1)} %constant_dynamic-slice_fusion.35), channel_id=1, source_target_pairs={{0,4},{4,0},{8,12},{12,8},{16,20},{20,16},{24,28},{28,24},{1,5},{5... | collective-permute-start | bytes 1105928 | tf_op jit(solution)/shard_map/ppermute | solution.py:89
  93.4 11.3 %collective-permute-start.23 = (bf16[192,768]{1,0:T(8,128)(2,1)S(1)}, bf16[192,768]{1,0:T(8,128)(2,1)}, u32[]{:S(2)}, u32[]{:S(2)}) collective-permute-start(bf16[192,768]{1,0:T(8,128)(2,1)S(1)} %collective-permute-done.22), channel_id=1, source_target_pairs={{8,0},{12,4},{16,8},{20,12},{9,1},{13,5},{17,9},{21,13},{10,2},{14... | collective-permute-start | bytes 884744 | tf_op jit(solution)/shard_map/ppermute | solution.py:84
  100.0 26.1 %collective-permute-start.35 = (bf16[4,192,384]{2,1,0:T(8,128)(2,1)}, bf16[4,192,384]{2,1,0:T(8,128)(2,1)}, u32[]{:S(2)}, u32[]{:S(2)}) collective-permute-start(bf16[4,192,384]{2,1,0:T(8,128)(2,1)} %constant_dynamic-slice_fusion.31), channel_id=1, source_target_pairs={{0,4},{4,0},{8,12},{12,8},{16,20},{20,16},{24,28},{28,24},{1,5},{5... | collective-permute-start | bytes 1769480 | tf_op jit(solution)/shard_map/ppermute | solution.py:89
  104.6 24.5 %collective-permute-start.15 = (bf16[4,96,768]{2,1,0:T(8,128)(2,1)S(1)}, bf16[4,96,768]{2,1,0:T(8,128)(2,1)}, u32[]{:S(2)}, u32[]{:S(2)}) collective-permute-start(bf16[4,96,768]{2,1,0:T(8,128)(2,1)S(1)} %constant_dynamic-slice_fusion.34), channel_id=1, source_target_pairs={{0,4},{4,0},{8,12},{12,8},{16,20},{20,16},{24,28},{28,24},{1,5},{5... | collective-permute-start | bytes 1769480 | tf_op jit(solution)/shard_map/ppermute | solution.py:89
  104.6 17.2 %collective-permute-start.24 = (bf16[192,768]{1,0:T(8,128)(2,1)}, bf16[192,768]{1,0:T(8,128)(2,1)}, u32[]{:S(2)}, u32[]{:S(2)}) collective-permute-start(bf16[192,768]{1,0:T(8,128)(2,1)} %collective-permute-done.23), channel_id=1, source_target_pairs={{8,0},{12,4},{9,1},{13,5},{10,2},{14,6},{11,3},{15,7}} | collective-permute-start | bytes 884744 | tf_op jit(solution)/shard_map/ppermute | solution.py:84
  109.0 11.5 %collective-permute-start.7 = (bf16[8,60,768]{2,0,1:T(8,128)(2,1)S(1)}, bf16[8,60,768]{2,0,1:T(8,128)(2,1)S(1)}, u32[]{:S(2)}, u32[]{:S(2)}) collective-permute-start(bf16[8,60,768]{2,0,1:T(8,128)(2,1)S(1)} %reshape.813), channel_id=1, source_target_pairs={{0,2},{1,3},{2,0},{3,1},{4,6},{5,7},{6,4},{7,5},{8,10},{9,11},{10,... | collective-permute-start | bytes 2211848 | tf_op jit(solution)/shard_map/ppermute | solution.py:93
  120.8 9.7 %collective-permute-start.8 = (bf16[2,8,60,768]{3,1,2,0:T(8,128)(2,1)S(1)}, bf16[2,8,60,768]{3,1,2,0:T(8,128)(2,1)S(1)}, u32[]{:S(2)}, u32[]{:S(2)}) collective-permute-start(bf16[2,8,60,768]{3,1,2,0:T(8,128)(2,1)S(1)} %pad_maximum_fusion.9), channel_id=1, source_target_pairs={{0,1},{1,0},{2,3},{3,2},{4,5},{5,4},{6,7},{7,6},{8,9},{9,8},{10,11... | collective-permute-start | bytes 4423688 | tf_op jit(solution)/shard_map/ppermute | solution.py:93
  124.2 29.0 %collective-permute-start.25 = (bf16[4,192,768]{2,1,0:T(8,128)(2,1)}, bf16[4,192,768]{2,1,0:T(8,128)(2,1)}, u32[]{:S(2)}, u32[]{:S(2)}) collective-permute-start(bf16[4,192,768]{2,1,0:T(8,128)(2,1)} %constant_dynamic-slice_fusion.33), channel_id=1, source_target_pairs={{0,4},{4,0},{8,12},{12,8},{16,20},{20,16},{24,28},{28,24},{1,5},{5... | collective-permute-start | bytes 3538952 | tf_op jit(solution)/shard_map/ppermute | solution.py:89
  127.5 35.2 %collective-permute-start.36 = (bf16[8,192,384]{2,1,0:T(8,128)(2,1)S(1)}, bf16[8,192,384]{2,1,0:T(8,128)(2,1)}, u32[]{:S(2)}, u32[]{:S(2)}) collective-permute-start(bf16[8,192,384]{2,1,0:T(8,128)(2,1)S(1)} %bitcast.719), channel_id=1, source_target_pairs={{0,2},{1,3},{2,0},{3,1},{4,6},{5,7},{6,4},{7,5},{8,10},{9,11},{10,... | collective-permute-start | bytes 3538952 | tf_op jit(solution)/shard_map/ppermute | solution.py:93
  143.4 11.4 %collective-permute-start.16 = (f32[312,384]{1,0:T(8,128)S(1)}, f32[312,384]{1,0:T(8,128)S(1)}, u32[]{:S(2)}, u32[]{:S(2)}) collective-permute-start(f32[312,384]{1,0:T(8,128)S(1)} %slice_select_fusion.3), channel_id=1, source_target_pairs={{0,1},{1,0},{2,3},{3,2},{4,5},{5,4},{6,7},{7,6},{8,9},{9,8},{10,11... | collective-permute-start | bytes 1437704 | tf_op jit(solution)/shard_map/ppermute | solution.py:93
  166.1 17.4 %collective-permute-start.37 = (bf16[2,8,192,384]{3,2,1,0:T(8,128)(2,1)}, bf16[2,8,192,384]{3,2,1,0:T(8,128)(2,1)}, u32[]{:S(2)}, u32[]{:S(2)}) collective-permute-start(bf16[2,8,192,384]{3,2,1,0:T(8,128)(2,1)} %pad_maximum_fusion.6), channel_id=1, source_target_pairs={{0,1},{1,0},{2,3},{3,2},{4,5},{5,4},{6,7},{7,6},{8,9},{9,8},{10,11... | collective-permute-start | bytes 7077896 | tf_op jit(solution)/shard_map/ppermute | solution.py:93
  199.7 15.9 %collective-permute-start.38 = (bf16[784,768]{1,0:T(8,128)(2,1)}, bf16[784,768]{1,0:T(8,128)(2,1)}, u32[]{:S(2)}, u32[]{:S(2)}) collective-permute-start(bf16[784,768]{1,0:T(8,128)(2,1)} %pad_maximum_fusion.10), channel_id=1, source_target_pairs={{0,1},{1,0},{2,3},{3,2},{4,5},{5,4},{6,7},{7,6},{8,9},{9,8},{10,11... | collective-permute-start | bytes 3612680 | tf_op jit(solution)/shard_map/ppermute | solution.py:93
  396.2 27.5 %collective-permute-start.39 = (bf16[784,768]{1,0:T(8,128)(2,1)}, bf16[784,768]{1,0:T(8,128)(2,1)}, u32[]{:S(2)}, u32[]{:S(2)}) collective-permute-start(bf16[784,768]{1,0:T(8,128)(2,1)} %fusion.81), channel_id=1, source_target_pairs={{0,1},{1,0},{2,3},{3,2},{4,5},{5,4},{6,7},{7,6},{8,9},{9,8},{10,11... | collective-permute-start | bytes 3612680 | tf_op jit(solution)/shard_map/ppermute | solution.py:93
  441.7 54.3 %collective-permute-start.53 = (bf16[4,2,2,4,48,384]{5,4,2,1,3,0:T(8,128)(2,1)}, bf16[4,2,2,4,48,384]{5,4,2,1,3,0:T(8,128)(2,1)}, u32[]{:S(2)}, u32[]{:S(2)}) collective-permute-start(bf16[4,2,2,4,48,384]{5,4,2,1,3,0:T(8,128)(2,1)} %dynamic-slice_bitcast_fusion), channel_id=1, source_target_pairs={{0,1},{1,0},{2,3},{3,2},{4,5},{5,4},{6,7},{7,6},{8,9},{9,8},{10,11... | collective-permute-start | bytes 7077896 | tf_op jit(solution)/shard_map/ppermute | solution.py:93
  449.4 16.0 %collective-permute-start.65 = (bf16[4,96,768]{2,1,0:T(8,128)(2,1)}, bf16[4,96,768]{2,1,0:T(8,128)(2,1)}, u32[]{:S(2)}, u32[]{:S(2)}) collective-permute-start(bf16[4,96,768]{2,1,0:T(8,128)(2,1)} %dynamic-slice_bitcast_fusion.2), channel_id=1, source_target_pairs={{0,4},{4,0},{8,12},{12,8},{16,20},{20,16},{24,28},{28,24},{1,5},{5... | collective-permute-start | bytes 1769480 | tf_op jit(solution)/shard_map/ppermute | solution.py:89
  464.6 16.8 %collective-permute-start.62 = (bf16[4,96,768]{2,1,0:T(8,128)(2,1)}, bf16[4,96,768]{2,1,0:T(8,128)(2,1)}, u32[]{:S(2)}, u32[]{:S(2)}) collective-permute-start(bf16[4,96,768]{2,1,0:T(8,128)(2,1)} %dynamic-slice_bitcast_fusion.5), channel_id=1, source_target_pairs={{0,4},{4,0},{8,12},{12,8},{16,20},{20,16},{24,28},{28,24},{1,5},{5... | collective-permute-start | bytes 1769480 | tf_op jit(solution)/shard_map/ppermute | solution.py:89
  479.8 15.9 %collective-permute-start.63 = (bf16[4,96,768]{2,1,0:T(8,128)(2,1)}, bf16[4,96,768]{2,1,0:T(8,128)(2,1)S(1)}, u32[]{:S(2)}, u32[]{:S(2)}) collective-permute-start(bf16[4,96,768]{2,1,0:T(8,128)(2,1)} %dynamic-slice_bitcast_fusion.4), channel_id=1, source_target_pairs={{0,4},{4,0},{8,12},{12,8},{16,20},{20,16},{24,28},{28,24},{1,5},{5... | collective-permute-start | bytes 1769480 | tf_op jit(solution)/shard_map/ppermute | solution.py:89
  485.9 10.0 %collective-permute-start.46 = (bf16[312,384]{1,0:T(8,128)(2,1)S(1)}, bf16[312,384]{1,0:T(8,128)(2,1)S(1)}, u32[]{:S(2)}, u32[]{:S(2)}) collective-permute-start(bf16[312,384]{1,0:T(8,128)(2,1)S(1)} %add_convert_fusion.6), channel_id=1, source_target_pairs={{0,2},{1,3},{2,0},{3,1},{4,6},{5,7},{6,4},{7,5},{8,10},{9,11},{10,... | collective-permute-start | bytes 718856 | tf_op jit(solution)/shard_map/ppermute | solution.py:93
  499.3 47.1 %collective-permute-start.54 = (bf16[4,2,4,48,384]{4,3,1,2,0:T(8,128)(2,1)S(1)}, bf16[4,2,4,48,384]{4,3,1,2,0:T(8,128)(2,1)S(1)}, u32[]{:S(2)}, u32[]{:S(2)}) collective-permute-start(bf16[4,2,4,48,384]{4,3,1,2,0:T(8,128)(2,1)S(1)} %fusion.84), channel_id=1, source_target_pairs={{0,4},{4,0},{8,12},{12,8},{16,20},{20,16},{24,28},{28,24},{1,5},{5... | collective-permute-start | bytes 3538952 | tf_op jit(solution)/shard_map/ppermute | solution.py:89
  504.0 36.4 %collective-permute-start.64 = (bf16[4,96,768]{2,1,0:T(8,128)(2,1)S(1)}, bf16[4,96,768]{2,1,0:T(8,128)(2,1)S(1)}, u32[]{:S(2)}, u32[]{:S(2)}) collective-permute-start(bf16[4,96,768]{2,1,0:T(8,128)(2,1)S(1)} %dynamic-slice_bitcast_fusion.3), channel_id=1, source_target_pairs={{0,4},{4,0},{8,12},{12,8},{16,20},{20,16},{24,28},{28,24},{1,5},{5... | collective-permute-start | bytes 1769480 | tf_op jit(solution)/shard_map/ppermute | solution.py:89
  541.1 29.2 %collective-permute-start.66 = (bf16[4,96,768]{2,1,0:T(8,128)(2,1)S(1)}, bf16[4,96,768]{2,1,0:T(8,128)(2,1)S(1)}, u32[]{:S(2)}, u32[]{:S(2)}) collective-permute-start(bf16[4,96,768]{2,1,0:T(8,128)(2,1)S(1)} %get-tuple-element.94), channel_id=1, source_target_pairs={{0,8},{4,12},{1,9},{5,13},{2,10},{6,14},{3,11},{7,15}} | collective-permute-start | bytes 1769480 | tf_op jit(solution)/shard_map/ppermute | solution.py:84
  546.7 18.3 %collective-permute-start.55 = (bf16[2,4,48,384]{3,2,0,1:T(8,128)(2,1)S(1)}, bf16[2,4,48,384]{3,2,0,1:T(8,128)(2,1)S(1)}, u32[]{:S(2)}, u32[]{:S(2)}) collective-permute-start(bf16[2,4,48,384]{3,2,0,1:T(8,128)(2,1)S(1)} %get-tuple-element.111), channel_id=1, source_target_pairs={{0,8},{4,12},{1,9},{5,13},{2,10},{6,14},{3,11},{7,15}} | collective-permute-start | bytes 884744 | tf_op jit(solution)/shard_map/ppermute | solution.py:84
  548.1 24.3 %collective-permute-start.58 = (bf16[2,4,48,384]{3,2,0,1:T(8,128)(2,1)S(1)}, bf16[2,4,48,384]{3,2,0,1:T(8,128)(2,1)S(1)}, u32[]{:S(2)}, u32[]{:S(2)}) collective-permute-start(bf16[2,4,48,384]{3,2,0,1:T(8,128)(2,1)S(1)} %get-tuple-element.112), channel_id=1, source_target_pairs={{24,16},{28,20},{25,17},{29,21},{26,18},{30,22},{27,19},{31,23}} | collective-permute-start | bytes 884744 | tf_op jit(solution)/shard_map/ppermute | solution.py:84
  565.2 11.8 %collective-permute-start.56 = (bf16[2,4,48,384]{3,2,0,1:T(8,128)(2,1)S(1)}, bf16[2,4,48,384]{3,2,0,1:T(8,128)(2,1)S(1)}, u32[]{:S(2)}, u32[]{:S(2)}) collective-permute-start(bf16[2,4,48,384]{3,2,0,1:T(8,128)(2,1)S(1)} %fusion.168), channel_id=1, source_target_pairs={{0,8},{4,12},{8,16},{12,20},{1,9},{5,13},{9,17},{13,21},{2,10},{6,... | collective-permute-start | bytes 884744 | tf_op jit(solution)/shard_map/ppermute | solution.py:84
  569.6 14.7 %collective-permute-start.69 = (bf16[4,96,768]{2,1,0:T(8,128)(2,1)S(1)}, bf16[4,96,768]{2,1,0:T(8,128)(2,1)S(1)}, u32[]{:S(2)}, u32[]{:S(2)}) collective-permute-start(bf16[4,96,768]{2,1,0:T(8,128)(2,1)S(1)} %get-tuple-element.95), channel_id=1, source_target_pairs={{24,16},{28,20},{25,17},{29,21},{26,18},{30,22},{27,19},{31,23}} | collective-permute-start | bytes 1769480 | tf_op jit(solution)/shard_map/ppermute | solution.py:84
  570.5 19.2 %collective-permute-start.67 = (bf16[4,96,768]{2,1,0:T(8,128)(2,1)S(1)}, bf16[4,96,768]{2,1,0:T(8,128)(2,1)S(1)}, u32[]{:S(2)}, u32[]{:S(2)}) collective-permute-start(bf16[4,96,768]{2,1,0:T(8,128)(2,1)S(1)} %fusion.95), channel_id=1, source_target_pairs={{0,8},{4,12},{8,16},{12,20},{1,9},{5,13},{9,17},{13,21},{2,10},{6,... | collective-permute-start | bytes 1769480 | tf_op jit(solution)/shard_map/ppermute | solution.py:84
  577.9 15.9 %collective-permute-start.57 = (bf16[2,4,48,384]{3,2,0,1:T(8,128)(2,1)S(1)}, bf16[2,4,48,384]{3,2,0,1:T(8,128)(2,1)S(1)}, u32[]{:S(2)}, u32[]{:S(2)}) collective-permute-start(bf16[2,4,48,384]{3,2,0,1:T(8,128)(2,1)S(1)} %get-tuple-element.109), channel_id=1, source_target_pairs={{0,8},{4,12},{8,16},{12,20},{16,24},{20,28},{1,9},{5,13},{9,17},{1... | collective-permute-start | bytes 884744 | tf_op jit(solution)/shard_map/ppermute | solution.py:84
  583.0 15.3 %collective-permute-start.60 = (bf16[2,4,48,384]{3,2,0,1:T(8,128)(2,1)S(1)}, bf16[2,4,48,384]{3,2,0,1:T(8,128)(2,1)S(1)}, u32[]{:S(2)}, u32[]{:S(2)}) collective-permute-start(bf16[2,4,48,384]{3,2,0,1:T(8,128)(2,1)S(1)} %fusion.167), channel_id=1, source_target_pairs={{8,0},{12,4},{16,8},{20,12},{24,16},{28,20},{9,1},{13,5},{17,9},{2... | collective-permute-start | bytes 884744 | tf_op jit(solution)/shard_map/ppermute | solution.py:84
  590.0 10.0 %collective-permute-start.70 = (bf16[4,96,768]{2,1,0:T(8,128)(2,1)S(1)}, bf16[4,96,768]{2,1,0:T(8,128)(2,1)S(1)}, u32[]{:S(2)}, u32[]{:S(2)}) collective-permute-start(bf16[4,96,768]{2,1,0:T(8,128)(2,1)S(1)} %get-tuple-element.93), channel_id=1, source_target_pairs={{16,8},{20,12},{24,16},{28,20},{17,9},{21,13},{25,17},{29,21},{18,... | collective-permute-start | bytes 1769480 | tf_op jit(solution)/shard_map/ppermute | solution.py:84
  591.5 10.4 %collective-permute-start.48 = (f32[1,19201]{1,0:T(1,128)S(1)}, f32[1,19201]{1,0:T(1,128)S(1)}, u32[]{:S(2)}, u32[]{:S(2)}) collective-permute-start(f32[1,19201]{1,0:T(1,128)S(1)} %reshape.845), channel_id=1, source_target_pairs={{0,1},{1,0},{2,3},{3,2},{4,5},{5,4},{6,7},{7,6},{8,9},{9,8},{10,11... | collective-permute-start | bytes 230420 | tf_op jit(solution)/shard_map/ppermute | solution.py:93
  593.7 24.7 %collective-permute-start.68 = (bf16[4,96,768]{2,1,0:T(8,128)(2,1)S(1)}, bf16[4,96,768]{2,1,0:T(8,128)(2,1)S(1)}, u32[]{:S(2)}, u32[]{:S(2)}) collective-permute-start(bf16[4,96,768]{2,1,0:T(8,128)(2,1)S(1)} %get-tuple-element.92), channel_id=1, source_target_pairs={{0,8},{4,12},{8,16},{12,20},{16,24},{20,28},{1,9},{5,13},{9,17},{1... | collective-permute-start | bytes 1769480 | tf_op jit(solution)/shard_map/ppermute | solution.py:84
  598.4 18.7 %collective-permute-start.61 = (bf16[4,48,384]{2,1,0:T(8,128)(2,1)S(1)}, bf16[4,48,384]{2,1,0:T(8,128)(2,1)S(1)}, u32[]{:S(2)}, u32[]{:S(2)}) collective-permute-start(bf16[4,48,384]{2,1,0:T(8,128)(2,1)S(1)} %fusion.217), channel_id=1, source_target_pairs={{0,2},{1,3},{2,0},{3,1},{4,6},{5,7},{6,4},{7,5},{8,10},{9,11},{10,... | collective-permute-start | bytes 442376 | tf_op jit(solution)/shard_map/ppermute | solution.py:93
  600.2 19.8 %collective-permute-start.71 = (bf16[4,96,768]{2,1,0:T(8,128)(2,1)S(1)}, bf16[4,96,768]{2,1,0:T(8,128)(2,1)S(1)}, u32[]{:S(2)}, u32[]{:S(2)}) collective-permute-start(bf16[4,96,768]{2,1,0:T(8,128)(2,1)S(1)} %fusion.94), channel_id=1, source_target_pairs={{8,0},{12,4},{16,8},{20,12},{24,16},{28,20},{9,1},{13,5},{17,9},{2... | collective-permute-start | bytes 1769480 | tf_op jit(solution)/shard_map/ppermute | solution.py:84
  606.4 20.4 %collective-permute-start.81 = (bf16[48,384]{1,0:T(8,128)(2,1)S(1)}, bf16[48,384]{1,0:T(8,128)(2,1)S(1)}, u32[]{:S(2)}, u32[]{:S(2)}) collective-permute-start(bf16[48,384]{1,0:T(8,128)(2,1)S(1)} %copy-done.169), channel_id=1, source_target_pairs={{0,16},{4,20},{8,24},{12,28},{16,0},{20,4},{24,8},{28,12},{1,17},{... | collective-permute-start | bytes 110600 | tf_op jit(solution)/shard_map/ppermute | solution.py:89
  617.1 9.7 %collective-permute-start.80 = (bf16[48,384]{1,0:T(8,128)(2,1)S(1)}, bf16[48,384]{1,0:T(8,128)(2,1)S(1)}, u32[]{:S(2)}, u32[]{:S(2)}) collective-permute-start(bf16[48,384]{1,0:T(8,128)(2,1)S(1)} %copy-done.168), channel_id=1, source_target_pairs={{0,8},{4,12},{8,0},{12,4},{16,24},{20,28},{24,16},{28,20},{1,9},{5... | collective-permute-start | bytes 110600 | tf_op jit(solution)/shard_map/ppermute | solution.py:89
  642.3 11.6 %collective-permute-start.93 = (bf16[96,768]{1,0:T(8,128)(2,1)S(1)}, bf16[96,768]{1,0:T(8,128)(2,1)S(1)}, u32[]{:S(2)}, u32[]{:S(2)}) collective-permute-start(bf16[96,768]{1,0:T(8,128)(2,1)S(1)} %get-tuple-element.170), channel_id=1, source_target_pairs={{0,16},{4,20},{8,24},{12,28},{16,0},{20,4},{24,8},{28,12},{1,17},{... | collective-permute-start | bytes 442376 | tf_op jit(solution)/shard_map/ppermute | solution.py:89
  644.2 9.6 %collective-permute-start.92 = (bf16[96,768]{1,0:T(8,128)(2,1)S(1)}, bf16[96,768]{1,0:T(8,128)(2,1)S(1)}, u32[]{:S(2)}, u32[]{:S(2)}) collective-permute-start(bf16[96,768]{1,0:T(8,128)(2,1)S(1)} %get-tuple-element.171), channel_id=1, source_target_pairs={{0,8},{4,12},{8,0},{12,4},{16,24},{20,28},{24,16},{28,20},{1,9},{5... | collective-permute-start | bytes 442376 | tf_op jit(solution)/shard_map/ppermute | solution.py:89
  659.7 11.7 %collective-permute-start.78 = (bf16[96,768]{1,0:T(8,128)(2,1)}, bf16[96,768]{1,0:T(8,128)(2,1)}, u32[]{:S(2)}, u32[]{:S(2)}) collective-permute-start(bf16[96,768]{1,0:T(8,128)(2,1)} %get-tuple-element.186), channel_id=1, source_target_pairs={{0,16},{4,20},{8,24},{12,28},{16,0},{20,4},{24,8},{28,12},{1,17},{... | collective-permute-start | bytes 442376 | tf_op jit(solution)/shard_map/ppermute | solution.py:89
  659.7 11.7 %collective-permute-start.77 = (bf16[96,768]{1,0:T(8,128)(2,1)S(1)}, bf16[96,768]{1,0:T(8,128)(2,1)}, u32[]{:S(2)}, u32[]{:S(2)}) collective-permute-start(bf16[96,768]{1,0:T(8,128)(2,1)S(1)} %get-tuple-element.187), channel_id=1, source_target_pairs={{0,8},{4,12},{8,0},{12,4},{16,24},{20,28},{24,16},{28,20},{1,9},{5... | collective-permute-start | bytes 442376 | tf_op jit(solution)/shard_map/ppermute | solution.py:89
  678.2 13.3 %collective-permute-start.84 = (f32[480,256]{1,0:T(8,128)S(1)}, f32[480,256]{1,0:T(8,128)S(1)}, u32[]{:S(2)}, u32[]{:S(2)}) collective-permute-start(f32[480,256]{1,0:T(8,128)S(1)} %get-tuple-element.148), channel_id=1, source_target_pairs={{0,4},{4,0},{8,12},{12,8},{16,20},{20,16},{24,28},{28,24},{1,5},{5... | collective-permute-start | bytes 1474568 | tf_op jit(solution)/shard_map/ppermute | solution.py:89
  679.8 14.1 %collective-permute-start.86 = (f32[480,256]{1,0:T(8,128)S(1)}, f32[480,256]{1,0:T(8,128)S(1)}, u32[]{:S(2)}, u32[]{:S(2)}) collective-permute-start(f32[480,256]{1,0:T(8,128)S(1)} %get-tuple-element.149), channel_id=1, source_target_pairs={{0,2},{1,3},{2,0},{3,1},{4,6},{5,7},{6,4},{7,5},{8,10},{9,11},{10,... | collective-permute-start | bytes 1474568 | tf_op jit(solution)/shard_map/ppermute | solution.py:93
  681.3 16.8 %collective-permute-start.101 = (f32[60,768]{1,0:T(8,128)S(1)}, f32[60,768]{1,0:T(8,128)S(1)}, u32[]{:S(2)}, u32[]{:S(2)}) collective-permute-start(f32[60,768]{1,0:T(8,128)S(1)} %slice_bitcast_fusion.4), channel_id=1, source_target_pairs={{0,2},{1,3},{2,0},{3,1},{4,6},{5,7},{6,4},{7,5},{8,10},{9,11},{10,... | collective-permute-start | bytes 552968 | tf_op jit(solution)/shard_map/ppermute | solution.py:93
  694.0 13.5 %collective-permute-start.85 = (f32[480,256]{1,0:T(8,128)S(1)}, f32[480,256]{1,0:T(8,128)S(1)}, u32[]{:S(2)}, u32[]{:S(2)}) collective-permute-start(f32[480,256]{1,0:T(8,128)S(1)} %get-tuple-element.146), channel_id=1, source_target_pairs={{0,2},{1,3},{2,0},{3,1},{4,6},{5,7},{6,4},{7,5},{8,10},{9,11},{10,... | collective-permute-start | bytes 1474568 | tf_op jit(solution)/shard_map/ppermute | solution.py:93
  695.6 12.0 %collective-permute-start.87 = (f32[480,256]{1,0:T(8,128)S(1)}, f32[480,256]{1,0:T(8,128)S(1)}, u32[]{:S(2)}, u32[]{:S(2)}) collective-permute-start(f32[480,256]{1,0:T(8,128)S(1)} %get-tuple-element.147), channel_id=1, source_target_pairs={{0,4},{4,0},{8,12},{12,8},{16,20},{20,16},{24,28},{28,24},{1,5},{5... | collective-permute-start | bytes 1474568 | tf_op jit(solution)/shard_map/ppermute | solution.py:89
  698.2 11.2 %collective-permute-start.102 = (f32[2,60,768]{2,1,0:T(8,128)S(1)}, f32[2,60,768]{2,1,0:T(8,128)S(1)}, u32[]{:S(2)}, u32[]{:S(2)}) collective-permute-start(f32[2,60,768]{2,1,0:T(8,128)S(1)} %pad_maximum_fusion.26), channel_id=1, source_target_pairs={{0,1},{1,0},{2,3},{3,2},{4,5},{5,4},{6,7},{7,6},{8,9},{9,8},{10,11... | collective-permute-start | bytes 1105928 | tf_op jit(solution)/shard_map/ppermute | solution.py:93
  755.3 54.2 %collective-permute-start.100 = (bf16[48,384]{1,0:T(8,128)(2,1)S(1)}, bf16[48,384]{1,0:T(8,128)(2,1)S(1)}, u32[]{:S(2)}, u32[]{:S(2)}) collective-permute-start(bf16[48,384]{1,0:T(8,128)(2,1)S(1)} %get-tuple-element.203), channel_id=1, source_target_pairs={{0,24},{4,28},{8,16},{12,20},{16,8},{20,12},{24,0},{28,4},{1,25},{... | collective-permute-start | bytes 110600 | tf_op jit(solution)/shard_map/ppermute | solution.py:89
  757.4 54.5 %collective-permute-start.99 = (bf16[48,384]{1,0:T(8,128)(2,1)S(1)}, bf16[48,384]{1,0:T(8,128)(2,1)S(1)}, u32[]{:S(2)}, u32[]{:S(2)}) collective-permute-start(bf16[48,384]{1,0:T(8,128)(2,1)S(1)} %get-tuple-element.204), channel_id=1, source_target_pairs={{0,16},{4,20},{8,24},{12,28},{16,0},{20,4},{24,8},{28,12},{1,17},{... | collective-permute-start | bytes 110600 | tf_op jit(solution)/shard_map/ppermute | solution.py:89
  757.4 56.5 %collective-permute-start.98 = (bf16[48,384]{1,0:T(8,128)(2,1)S(1)}, bf16[48,384]{1,0:T(8,128)(2,1)S(1)}, u32[]{:S(2)}, u32[]{:S(2)}) collective-permute-start(bf16[48,384]{1,0:T(8,128)(2,1)S(1)} %get-tuple-element.205), channel_id=1, source_target_pairs={{0,8},{4,12},{8,0},{12,4},{16,24},{20,28},{24,16},{28,20},{1,9},{5... | collective-permute-start | bytes 110600 | tf_op jit(solution)/shard_map/ppermute | solution.py:89
  768.6 48.0 %collective-permute-start.97 = (bf16[48,384]{1,0:T(8,128)(2,1)S(1)}, bf16[48,384]{1,0:T(8,128)(2,1)S(1)}, u32[]{:S(2)}, u32[]{:S(2)}) collective-permute-start(bf16[48,384]{1,0:T(8,128)(2,1)S(1)} %get-tuple-element.211), channel_id=1, source_target_pairs={{0,24},{4,28},{8,16},{12,20},{16,8},{20,12},{24,0},{28,4},{1,25},{... | collective-permute-start | bytes 110600 | tf_op jit(solution)/shard_map/ppermute | solution.py:89
  770.7 48.3 %collective-permute-start.96 = (bf16[48,384]{1,0:T(8,128)(2,1)S(1)}, bf16[48,384]{1,0:T(8,128)(2,1)S(1)}, u32[]{:S(2)}, u32[]{:S(2)}) collective-permute-start(bf16[48,384]{1,0:T(8,128)(2,1)S(1)} %get-tuple-element.212), channel_id=1, source_target_pairs={{0,16},{4,20},{8,24},{12,28},{16,0},{20,4},{24,8},{28,12},{1,17},{... | collective-permute-start | bytes 110600 | tf_op jit(solution)/shard_map/ppermute | solution.py:89
  809.4 9.6 %collective-permute-start.95 = (bf16[48,384]{1,0:T(8,128)(2,1)S(1)}, bf16[48,384]{1,0:T(8,128)(2,1)S(1)}, u32[]{:S(2)}, u32[]{:S(2)}) collective-permute-start(bf16[48,384]{1,0:T(8,128)(2,1)S(1)} %get-tuple-element.213), channel_id=1, source_target_pairs={{0,8},{4,12},{8,0},{12,4},{16,24},{20,28},{24,16},{28,20},{1,9},{5... | collective-permute-start | bytes 110600 | tf_op jit(solution)/shard_map/ppermute | solution.py:89
  811.9 10.6 %collective-permute-start.91 = (bf16[96,768]{1,0:T(8,128)(2,1)S(1)}, bf16[96,768]{1,0:T(8,128)(2,1)S(1)}, u32[]{:S(2)}, u32[]{:S(2)}) collective-permute-start(bf16[96,768]{1,0:T(8,128)(2,1)S(1)} %get-tuple-element.177), channel_id=1, source_target_pairs={{0,24},{4,28},{8,16},{12,20},{16,8},{20,12},{24,0},{28,4},{1,25},{... | collective-permute-start | bytes 442376 | tf_op jit(solution)/shard_map/ppermute | solution.py:89
  813.9 12.1 %collective-permute-start.90 = (bf16[96,768]{1,0:T(8,128)(2,1)S(1)}, bf16[96,768]{1,0:T(8,128)(2,1)S(1)}, u32[]{:S(2)}, u32[]{:S(2)}) collective-permute-start(bf16[96,768]{1,0:T(8,128)(2,1)S(1)} %get-tuple-element.178), channel_id=1, source_target_pairs={{0,16},{4,20},{8,24},{12,28},{16,0},{20,4},{24,8},{28,12},{1,17},{... | collective-permute-start | bytes 442376 | tf_op jit(solution)/shard_map/ppermute | solution.py:89
  (279 other events, 2059.2 us)
where the time goes:
time: 842 us; the launch traced here: 831 us
  matrix products  228 us (27%)
  waiting for transfers between devices  181 us (21%)
  starting transfers between devices  151 us (18%)
  other arithmetic  142 us (17%)
  local copies, waits for them, and re-layouts  117 us (14%)
  between operations  12.3 us (1%)
    ppermute x35, waiting for transfers between devices, wide_flip(): return lax.ppermute(value, WD, [(src, src ^ bit) for src in range(count)])  87.2 us
    dot_general x36, matrix products, hdot(): return jnp.dot(left, right, precision=HIGH, preferred_element_type=F32)  71.3 us
    ppermute x36, starting transfers between devices, wide_move(): lax.ppermute(value, WD, shift_pairs(lax.axis_size(WD), digit, delta, keep))  70.5 us
    ppermute x35, starting transfers between devices, wide_flip(): return lax.ppermute(value, WD, [(src, src ^ bit) for src in range(count)])  59.1 us
    ppermute x36, waiting for transfers between devices, wide_move(): lax.ppermute(value, WD, shift_pairs(lax.axis_size(WD), digit, delta, keep))  52.4 us
    ppermute x32, waiting for transfers between devices, narrow_flip(): return lax.ppermute(value, NR, [(src, src ^ bit) for src in range(QN)])  41.5 us
    convert_element_type x12, other arithmetic, low(): return value.astype(BF)  32.4 us
    dot_general x2, matrix products, attention_backward(): jnp.einsum('cqhd,ckhd->chqk', grad_low, values, preferred_element_type=F32)  24.6 us
  transfers between devices with their start and end apart: 103, of which 33 were waited for; matrix products, arithmetic and copies ran while one was open for 51% of the time, Pallas kernels for 0%

commit v1 on v0

v1 whole, which is shorter than its diff:
```python
import functools
import math

import jax
import jax.numpy as jnp
from jax import lax
from jax.experimental import pallas as pl
from jax.experimental.pallas import tpu as pltpu
from jax.sharding import PartitionSpec as P

WD = "wide"
NR = "narrow"
D = 768
HD = 64
FE = 3072
DD = 384
FD = 1536
PIX = 1536
GROUPS = 3
NS_STEPS = 5
STEP = 10
QN = 4

EPS_NORM = 1e-06
TARGET_EPS = 1.0
CLIP_AT = 0.0002
MOMENTUM = 0.95
RATE_MUON = 0.15
RATE_ADAM = 0.02
RATE_VECTOR = 0.2
DECAY = 0.05
BETA_ONE = 0.9
BETA_TWO = 0.95
EPS_ADAM = 1e-12
NS_A = 3.4445
NS_B = -4.775
NS_C = 2.0315
ROOT_HALF = 0.7071067811865476
INV_ROOT_TWO_PI = 0.3989422804014327
BF = jnp.bfloat16
F32 = jnp.float32
LOG2E = 1.4426950408889634
PAIR = 2 * HD
BLOCKS = 3
PAIRS = [(i, j) for i in range(BLOCKS) for j in range(i, BLOCKS)]
VMEM_LIMIT = 56 * 2**20
COST = pl.CostEstimate(flops=1000, bytes_accessed=1000, transcendentals=0)

BLOCK = ("ln1_g", "ln1_b", "q_b", "v_b", "out_b", "ln2_g", "ln2_b", "up_b", "down_b")


def vector_layout():
    entries = []
    for side, width, hidden in (("e", D, FE), ("d", DD, FD)):
        if side == "d":
            entries += [("in_b", DD), ("mask", DD)]
        entries += [(side + name, hidden if name == "up_b" else width) for name in BLOCK]
        entries += [(side + "lnf_g", width), (side + "lnf_b", width)]
        if side == "e":
            entries += [("emb_b", D)]
    entries += [("head_b", PIX)]
    table, offset = {}, 0
    for name, extent in entries:
        table[name] = (offset, extent)
        offset += extent
    return table


def wide_digits(count):
    digits, rest, step = [], count, 1
    while rest > 1:
        radix = 2 if not digits or rest % 4 else 4
        digits.append((step, radix))
        step, rest = step * radix, rest // radix
    return digits


def shift_pairs(count, digit, delta, keep=None):
    step, radix = digit
    pairs = []
    for src in range(count):
        place = src // step % radix
        if 0 <= place + delta < radix and (keep is None or keep(place)):
            pairs.append((src, src + delta * step))
    return pairs


def wide_move(value, digit, delta, keep=None):
    return lax.ppermute(value, WD, shift_pairs(lax.axis_size(WD), digit, delta, keep))


def wide_flip(value, bit):
    count = lax.axis_size(WD)
    return lax.ppermute(value, WD, [(src, src ^ bit) for src in range(count)])


def narrow_flip(value, bit):
    return lax.ppermute(value, NR, [(src, src ^ bit) for src in range(QN)])


def place_in(digit):
    return lax.axis_index(WD) // digit[0] % digit[1]


def pick_half(value, which, axis):
    return lax.dynamic_index_in_dim(value, which, axis, keepdims=False)


def both(mine, theirs, place, axis):
    first = jnp.where(place == 0, mine, theirs)
    second = jnp.where(place == 0, theirs, mine)
    return jnp.stack([first, second], axis)


def in_order(got, place):
    odd, high = place % 2 == 1, place // 2 == 1
    got = [jnp.where(odd, got[k ^ 1], got[k]) for k in range(4)]
    return [jnp.where(high, got[k ^ 2], got[k]) for k in range(4)]


def after(value, *earlier):
    return lax.optimization_barrier((value,) + earlier)[0]


def slow_pieces(block):
    step, radix = wide_digits(lax.axis_size(WD))[-1]
    return {mask * step: wide_flip(block, mask * step) if mask else block for mask in range(radix)}


def all_pieces(pieces):
    pieces = dict(pieces)
    for step, radix in wide_digits(lax.axis_size(WD))[-2::-1]:
        others = [held for held in pieces if held]
        joined = jnp.stack([pieces[held] for held in others], 0)
        for mask in range(1, radix):
            pieces[mask * step] = wide_flip(pieces[0], mask * step)
            moved = wide_flip(joined, mask * step)
            for k, held in enumerate(others):
                pieces[held ^ mask * step] = moved[k]
    return pieces


def assemble(pieces):
    count = lax.axis_size(WD)
    shape = pieces[0].shape
    for digit in wide_digits(count):
        step, radix = digit
        place = place_in(digit)
        joined = {}
        for held in pieces:
            if held // step % radix == 0:
                group = [pieces[held ^ mask * step] for mask in range(radix)]
                if radix == 2:
                    joined[held] = both(group[0], group[1], place, 0)
                else:
                    joined[held] = jnp.stack(in_order(group, place), 0)
        pieces = joined
    return pieces[0].reshape((count,) + shape)


def tied(pieces, *earlier):
    return dict(zip(pieces, lax.optimization_barrier((tuple(pieces.values()),) + earlier)[0]))


def narrow_pair(value, bit, axis=0):
    return both(value, narrow_flip(value, bit), lax.axis_index(NR) // bit % 2, axis)


def narrow_gather(block):
    return narrow_pair(narrow_pair(block, 2), 1, 1).reshape((QN,) + block.shape)


def line_scatter(value, digit, axis):
    place = place_in(digit)
    total = pick_half(value, place, axis).astype(F32)
    for mask in range(1, digit[1]):
        sent = pick_half(value, place ^ mask, axis).astype(BF)
        total = total + wide_flip(sent, mask * digit[0]).astype(F32)
    return total


def slow_exchange(value, digit):
    place = place_in(digit)
    got = [pick_half(value, place, 0)]
    for mask in range(1, digit[1]):
        got.append(wide_flip(pick_half(value, place ^ mask, 0), mask * digit[0]))
    return jnp.stack(in_order(got, place), 0)


def ends_total(one, two, digit, targets):
    place = place_in(digit)
    total = jnp.where(place == targets[0], one, two)
    one, two = low(one), low(two)
    count = lax.axis_size(WD)
    for mask in range(1, 4):
        pairs = [
            (src, src ^ mask * digit[0])
            for src in range(count)
            if (src // digit[0] % digit[1]) ^ mask in targets
        ]
        sent = jnp.where(place ^ mask == targets[0], one, two)
        total = total + lax.ppermute(sent, WD, pairs).astype(F32)
    return total


def joined(big, small):
    rows = small.shape[1] // 2
    return jnp.concatenate([big, jnp.concatenate([small[:, :rows], small[:, rows:]], 2)], 1)


def parted(value, rows):
    small = value[:, rows:]
    width = small.shape[2] // 2
    return value[:, :rows], jnp.concatenate([small[..., :width], small[..., width:]], 1)


def joined_exchange(big, small, digit):
    return parted(slow_exchange(joined(big, small), digit), big.shape[1])


def pair_sum(value):
    return value + narrow_flip(value, 1)


def sum_all(value):
    value = pair_sum(value)
    value = value + narrow_flip(value, 2)
    bit = 1
    while bit < lax.axis_size(WD):
        value = value + wide_flip(value, bit)
        bit *= 2
    return value


def sum_tiny(value):
    me = lax.axis_index(NR)
    parts = in_order([value] + [narrow_flip(value, mask) for mask in range(1, QN)], me)
    value = (parts[0] + parts[1]) + (parts[2] + parts[3])
    for digit in wide_digits(lax.axis_size(WD)):
        if digit[1] == 2:
            value = value + wide_flip(value, digit[0])
        else:
            flips = [wide_flip(value, mask * digit[0]) for mask in range(1, 4)]
            parts = in_order([value] + flips, place_in(digit))
            value = (parts[0] + parts[1]) + (parts[2] + parts[3])
    return value


def narrow_parts(part):
    part = low(part.astype(F32) + narrow_flip(part, 1).astype(F32))
    return [part, narrow_flip(part, 2)]


def sinusoid(positions, extent):
    half_extent = extent // 2
    frequency = jnp.exp(
        jnp.arange(half_extent, dtype=F32) * (-2.0 * math.log(10000.0) / extent)
    )
    angles = positions.astype(F32)[:, None] * frequency[None, :]
    return jnp.concatenate([jnp.sin(angles), jnp.cos(angles)], axis=1)


def low(value):
    return value.astype(BF)


def mm(left, right):
    return jnp.dot(left, right, preferred_element_type=F32)


def mm_tn(left, right):
    return lax.dot_general(left, right, (((0,), (0,)), ((), ())), preferred_element_type=F32)


def mm_nt(left, right):
    return lax.dot_general(left, right, (((1,), (1,)), ((), ())), preferred_element_type=F32)


def col_sum(value):
    return jnp.sum(value, 0, keepdims=True)


def layer_norm(value, gain, bias):
    center = value - jnp.mean(value, -1, keepdims=True)
    inv = lax.rsqrt(jnp.mean(center * center, -1, keepdims=True) + EPS_NORM)
    normed = center * inv
    return (normed * gain + bias, (normed, inv))


def norm_back(grad, saved, gain):
    normed, inv = saved
    grad_n = grad * gain
    grad_in = inv * (
        grad_n
        - jnp.mean(grad_n, -1, keepdims=True)
        - normed * jnp.mean(grad_n * normed, -1, keepdims=True)
    )
    return (grad_in, col_sum(grad * normed), col_sum(grad))


def gelu_value(upper):
    return 0.5 * upper * (1.0 + lax.erf(upper * ROOT_HALF))


def gelu_slope(upper):
    return (
        0.5 * (1.0 + lax.erf(upper * ROOT_HALF))
        + upper * jnp.exp(-0.5 * upper * upper) * INV_ROOT_TWO_PI
    )


def group_targets(pix, groups):
    rows = pix.astype(F32)
    masks = [(groups == g).astype(F32)[None, :] for g in range(GROUPS)]
    per_group = pix.shape[-1] // GROUPS

    def spread(parts):
        return sum(part * mask for part, mask in zip(parts, masks))

    means = [jnp.sum(rows * mask, -1, keepdims=True) / per_group for mask in masks]
    center = rows - spread(means)
    squares = center * center
    scale = [
        lax.rsqrt(jnp.sum(squares * mask, -1, keepdims=True) / per_group + TARGET_EPS)
        for mask in masks
    ]
    return center * spread(scale)


def dot_nn(left, right):
    return jnp.dot(left, right, preferred_element_type=F32)


def dot_tn(left, right):
    return mm_tn(left, right)


def dot_nt(left, right):
    return mm_nt(left, right)


def lane_masked(value):
    lane = lax.broadcasted_iota(jnp.int32, value.shape, 1)
    zero = jnp.zeros_like(value)
    return [jnp.where(lane < HD, value, zero), jnp.where(lane < HD, zero, value)]

def attn_fwd_kernel(tile, q_ref, kv_ref, o_ref, of_ref, lse_ref, s_ref):
    queries = q_ref.shape[0]; keys = kv_ref.shape[1]
    qs = lane_masked(q_ref[...])
    scale = HD ** -0.5 * LOG2E
    def first(t, peaks):
        at = pl.ds(pl.multiple_of(t * tile, tile), tile)
        k_t = kv_ref[0, at, :]
        out = []
        for h in range(2):
            s = dot_nt(k_t, qs[h])
            s_ref[h, at, :] = s
            out.append(jnp.maximum(peaks[h], jnp.max(s, 0, keepdims=True)))
        return tuple(out)
    start = jnp.full((1, queries), -jnp.inf, F32)
    peaks = lax.fori_loop(0, keys // tile, first, (start, start))
    peaks = [p * scale for p in peaks]
    def second(t, carry):
        at = pl.ds(pl.multiple_of(t * tile, tile), tile)
        v_t = kv_ref[1, at, :]
        out = []
        for h in range(2):
            total, mixed = carry[h]
            p = jnp.exp2(s_ref[h, at, :] * scale - peaks[h])
            out.append((total + jnp.sum(p, 0, keepdims=True), mixed + dot_tn(v_t, p.astype(BF))))
        return tuple(out)
    zero = (jnp.zeros((1, queries), F32), jnp.zeros((PAIR, queries), F32))
    done = lax.fori_loop(0, keys // tile, second, (zero, zero))
    row = lax.broadcasted_iota(jnp.int32, (PAIR, queries), 0)
    mixed = jnp.where(row < HD, done[0][1] / done[0][0], done[1][1] / done[1][0]).T
    of_ref[...] = mixed
    o_ref[...] = mixed.astype(BF)
    for h in range(2):
        lse_ref[0, h : h + 1, :] = peaks[h] + jnp.log2(done[h][0])

def attention_fwd(q, kv, tile):
    queries, width = q.shape; keys = kv.shape[1]
    pairs = width // PAIR
    return pl.pallas_call(
        functools.partial(attn_fwd_kernel, tile),
        grid=(pairs,),
        in_specs=[pl.BlockSpec((queries, PAIR), lambda i: (0, i)), pl.BlockSpec((2, keys, PAIR), lambda i: (0, 0, i))],
        out_specs=[pl.BlockSpec((queries, PAIR), lambda i: (0, i)), pl.BlockSpec((queries, PAIR), lambda i: (0, i)), pl.BlockSpec((1, 2, queries), lambda i: (i, 0, 0))],
        out_shape=[jax.ShapeDtypeStruct((queries, width), BF), jax.ShapeDtypeStruct((queries, width), F32), jax.ShapeDtypeStruct((pairs, 2, queries), F32)],
        scratch_shapes=[pltpu.VMEM((2, keys, queries), F32)],
        compiler_params=pltpu.CompilerParams(vmem_limit_bytes=VMEM_LIMIT),
        cost_estimate=COST,
    )(q, kv)

def attn_bwd_kernel(tile, q_ref, kv_ref, g_ref, of_ref, lse_ref, dq_ref, dkv_ref, dqt_ref):
    queries = q_ref.shape[0]; keys = kv_ref.shape[1]
    scale = HD ** -0.5
    qs = lane_masked(q_ref[...]); gs = lane_masked(g_ref[...])
    prod = g_ref[...].astype(F32) * of_ref[...]
    which = lax.broadcasted_iota(jnp.int32, (8, PAIR), 0); lane = lax.broadcasted_iota(jnp.int32, (8, PAIR), 1)
    picks = jnp.where(lane // HD == which, 1.0, 0.0)
    deltas = lax.dot_general(picks, prod, (((1,), (1,)), ((), ())), precision=lax.Precision.HIGHEST, preferred_element_type=F32)
    dqt_ref[...] = jnp.zeros_like(dqt_ref)
    def step(t, carry):
        at = pl.ds(pl.multiple_of(t * tile, tile), tile)
        k_t = kv_ref[0, at, :]; v_t = kv_ref[1, at, :]
        dk = jnp.zeros((tile, PAIR), F32); dv = jnp.zeros((tile, PAIR), F32)
        for h in range(2):
            p = jnp.exp2(dot_nt(k_t, qs[h]) * (scale * LOG2E) - lse_ref[0, h : h + 1, :])
            dp = dot_nt(v_t, gs[h])
            ds = (p * (dp - deltas[h : h + 1, :])).astype(BF)
            dv = dv + dot_nn(p.astype(BF), gs[h])
            dk = dk + dot_nn(ds, qs[h])
            dqt_ref[h] += dot_tn(k_t, ds)
        dkv_ref[0, at, :] = (dk * scale).astype(BF)
        dkv_ref[1, at, :] = dv.astype(BF)
        return carry
    lax.fori_loop(0, keys // tile, step, 0)
    row = lax.broadcasted_iota(jnp.int32, (PAIR, queries), 0)
    dq_ref[...] = (jnp.where(row < HD, dqt_ref[0], dqt_ref[1]).T * scale).astype(BF)

def attention_bwd(q, kv, grad, mixed, lse, tile):
    queries, width = q.shape; keys = kv.shape[1]
    pairs = width // PAIR
    qspec = pl.BlockSpec((queries, PAIR), lambda i: (0, i)); kspec = pl.BlockSpec((2, keys, PAIR), lambda i: (0, 0, i))
    return pl.pallas_call(
        functools.partial(attn_bwd_kernel, tile),
        grid=(pairs,),
        in_specs=[qspec, kspec, qspec, qspec, pl.BlockSpec((1, 2, queries), lambda i: (i, 0, 0))],
        out_specs=[qspec, kspec],
        out_shape=[jax.ShapeDtypeStruct((queries, width), BF), jax.ShapeDtypeStruct((2, keys, width), BF)],
        scratch_shapes=[pltpu.VMEM((2, PAIR, queries), F32)],
        compiler_params=pltpu.CompilerParams(vmem_limit_bytes=VMEM_LIMIT),
        cost_estimate=COST,
    )(q, kv, grad, mixed, lse)


def split(value):
    high = value.astype(BF)
    return high, (value - high.astype(F32)).astype(BF)

def tile_rows(size, other, index):
    if not other:
        return slice(index * size, (index + 1) * size), slice(0, size)
    half = len(PAIRS) // 2
    at = len(PAIRS) * other + index % half * size
    return slice(at, at + size), slice(index // half * size, (index // half + 1) * size)


def slab_rows(grad, mom, factor, period, count):
    row = lax.rem(lax.broadcasted_iota(jnp.int32, (grad.shape[0], 1), 0), period)
    scale = jnp.where(row < count, factor, 0.0)
    return MOMENTUM * mom.astype(F32) + scale * grad


def gram_kernel(
    periods, counts_ref, factor_ref, big_grad, big_mom, small_grad, small_mom, keep_ref, send_ref, out_ref
):
    for k, (grad, mom) in enumerate(((big_grad, big_mom), (small_grad, small_mom))):
        rows = slab_rows(grad[...], mom[...], factor_ref[0], periods[k], counts_ref[k])
        size = rows.shape[1] // BLOCKS
        high, rest = split(rows)
        for index, (i, j) in enumerate(PAIRS):
            a, b = slice(i * size, (i + 1) * size), slice(j * size, (j + 1) * size)
            tile = dot_tn(high[:, a], high[:, b]) + (
                dot_tn(high[:, a], rest[:, b]) + dot_tn(rest[:, a], high[:, b])
            )
            at, cols = tile_rows(size, k * big_grad.shape[1] // BLOCKS, index)
            out_ref[at, cols] = tile
    cols = keep_ref.shape[1]
    first = counts_ref[2] == 0
    left, right = out_ref[:, :cols], out_ref[:, cols:]
    keep_ref[...] = jnp.where(first, left, right)
    send_ref[...] = jnp.where(first, right, left)


def packed_gram(periods, counts, factor, slabs):
    n, m = slabs[0].shape[1], slabs[2].shape[1]
    rows = len(PAIRS) * (n // BLOCKS) + len(PAIRS) // 2 * (m // BLOCKS)
    cols = n // BLOCKS
    return pl.pallas_call(
        functools.partial(gram_kernel, periods),
        in_specs=[pl.BlockSpec(memory_space=pltpu.SMEM)] * 2
        + [pl.BlockSpec(memory_space=pltpu.VMEM)] * 4,
        out_shape=[jax.ShapeDtypeStruct((rows, cols // 2), F32)] * 2,
        scratch_shapes=[pltpu.VMEM((rows, cols), F32)],
        compiler_params=pltpu.CompilerParams(vmem_limit_bytes=VMEM_LIMIT),
        cost_estimate=COST,
    )(counts, factor, *slabs)


class Square:
    def __init__(self, refs, blocks):
        self.full, self.gram, self.poly, self.prod, self.temp = refs
        self.blocks = blocks

def put(ref, rows, cols, value):
    high, rest = split(value)
    ref[0, rows, cols] = high
    ref[1, rows, cols] = rest

def product(left, right, blocks, store):
    n = left.shape[1]
    size = n // blocks
    for j in range(blocks):
        rows, cols = slice(0, (j + 1) * size), slice(j * size, (j + 1) * size)
        tile = dot_nn(left[0, rows, :], right[0, :, cols]) + (
            dot_nn(left[0, rows, :], right[1, :, cols]) + dot_nn(left[1, rows, :], right[0, :, cols])
        )
        for i in range(j + 1):
            a = slice(i * size, (i + 1) * size)
            block = tile[a]
            store(a, cols, block)
            if i != j:
                store(cols, a, block.T)

def make_poly(sq):
    n = sq.full.shape[0]
    def store(rows, cols, block):
        value = NS_C * block + NS_B * sq.full[rows, cols]
        if rows == cols:
            r = lax.broadcasted_iota(jnp.int32, block.shape, 0); c = lax.broadcasted_iota(jnp.int32, block.shape, 1)
            value = value + jnp.where(r == c, NS_A, 0.0)
        put(sq.poly, rows, cols, value)
    product(sq.gram, sq.gram, sq.blocks, store)

def next_gram(sq):
    product(sq.poly, sq.gram, sq.blocks, lambda r, c, b: put(sq.temp, r, c, b))
    def store(r, c, b):
        sq.full[r, c] = b
        put(sq.gram, r, c, b)
    product(sq.temp, sq.poly, sq.blocks, store)

def next_product(sq):
    product(sq.poly, sq.prod, sq.blocks, lambda r, c, b: put(sq.temp, r, c, b))
    sq.prod[...] = sq.temp[...]

def ortho_kernel(
    periods, counts_ref, factor_ref, mine_ref, other_ref, big_grad, big_mom, small_grad, small_mom,
    big_out, small_out, packed_ref, *refs,
):
    squares = [Square(refs[:5], BLOCKS), Square(refs[5:], 1)]
    cols = mine_ref.shape[1]
    first = counts_ref[2] == 0
    packed_ref[:, :cols] = jnp.where(first, mine_ref[...], other_ref[...])
    packed_ref[:, cols:] = jnp.where(first, other_ref[...], mine_ref[...])
    scales = []
    for sq, other in zip(squares, (0, big_grad.shape[1] // BLOCKS)):
        size = sq.full.shape[0] // BLOCKS
        r = lax.broadcasted_iota(jnp.int32, (size, size), 0)
        c = lax.broadcasted_iota(jnp.int32, (size, size), 1)
        diag = jnp.zeros((size, size), F32)
        for index, (i, j) in enumerate(PAIRS):
            if i == j:
                diag = diag + jnp.where(r == c, packed_ref[tile_rows(size, other, index)], 0.0)
        trace = jnp.sum(jnp.sum(diag, 0, keepdims=True), 1, keepdims=True)
        scale = 1.0 / (jnp.sqrt(trace) + 1e-07)
        scales.append(scale)
        for index, (i, j) in enumerate(PAIRS):
            tile = packed_ref[tile_rows(size, other, index)] * (scale * scale)
            a, b = slice(i * size, (i + 1) * size), slice(j * size, (j + 1) * size)
            sq.full[a, b] = tile
            put(sq.gram, a, b, tile)
            if i != j:
                sq.full[b, a] = tile.T
                put(sq.gram, b, a, tile.T)
    for sq in squares:
        make_poly(sq)
    for sq in squares:
        sq.prod[...] = sq.poly[...]
        next_gram(sq)
    def step(_, carry):
        for sq in squares: make_poly(sq)
        for sq in squares: next_product(sq)
        for sq in squares: next_gram(sq)
        return carry
    lax.fori_loop(1, NS_STEPS - 1, step, 0)
    for sq in squares: make_poly(sq)
    for sq in squares: next_product(sq)
    slabs = ((big_grad, big_mom, big_out), (small_grad, small_mom, small_out))
    for k, (sq, scale, (grad, mom, out)) in enumerate(zip(squares, scales, slabs)):
        rows = slab_rows(grad[...], mom[...], factor_ref[0], periods[k], counts_ref[k])
        high, rest = split(rows * scale)
        out[...] = (
            dot_nn(high, sq.prod[0]) + (dot_nn(high, sq.prod[1]) + dot_nn(rest, sq.prod[0]))
        ).astype(BF)


def orthogonal(periods, counts, factor, mine, other, slabs):
    def scratch(n):
        return [pltpu.VMEM((n, n), F32)] + [pltpu.VMEM((2, n, n), BF)] * 4

    big, small = slabs[0], slabs[2]
    return pl.pallas_call(
        functools.partial(ortho_kernel, periods),
        in_specs=[pl.BlockSpec(memory_space=pltpu.SMEM)] * 2
        + [pl.BlockSpec(memory_space=pltpu.VMEM)] * 6,
        out_shape=[jax.ShapeDtypeStruct(big.shape, BF), jax.ShapeDtypeStruct(small.shape, BF)],
        scratch_shapes=[pltpu.VMEM((mine.shape[0], 2 * mine.shape[1]), F32)]
        + scratch(big.shape[1])
        + scratch(small.shape[1]),
        compiler_params=pltpu.CompilerParams(vmem_limit_bytes=VMEM_LIMIT),
        cost_estimate=COST,
    )(counts, factor, mine, other, *slabs)


def call(kernel, outs, args, flops, smem=0):
    return pl.pallas_call(
        kernel,
        in_specs=[pl.BlockSpec(memory_space=pltpu.SMEM)] * smem
        + [pl.BlockSpec(memory_space=pltpu.VMEM)] * (len(args) - smem),
        out_specs=[pl.BlockSpec(memory_space=pltpu.VMEM)] * len(outs),
        out_shape=[jax.ShapeDtypeStruct(shape, kind) for shape, kind in outs],
        compiler_params=pltpu.CompilerParams(vmem_limit_bytes=VMEM_LIMIT),
        cost_estimate=COST,
    )(*args)


def vec_at(vec_ref, name):
    offset, extent = vector_layout()[name]
    return vec_ref[:, offset : offset + extent]


def head_masks(value):
    lane = lax.broadcasted_iota(jnp.int32, value.shape, 1) // HD
    return [jnp.where(lane == h, value, jnp.zeros_like(value)) for h in range(value.shape[1] // HD)]


def small_probs(queries, keys, vis):
    scores = dot_nt(queries, keys) * HD**-0.5
    column = lax.broadcasted_iota(jnp.int32, scores.shape, 1)
    scores = jnp.where(column < vis, scores, -jnp.inf)
    exp_scores = jnp.exp(scores - jnp.max(scores, -1, keepdims=True))
    return exp_scores / jnp.sum(exp_scores, -1, keepdims=True)


def enc_attention_kernel(
    vis, clips, start_ref, pos_ref, vec_ref, w_ref, qb_ref, vb_ref, wout_ref,
    stream_ref, hid_ref, qkv_ref, attn_ref, part_ref,
):
    stream = start_ref[...] + vec_at(vec_ref, "emb_b") + pos_ref[...]
    stream_ref[...] = stream
    hid = low(layer_norm(stream, vec_at(vec_ref, "eln1_g"), vec_at(vec_ref, "eln1_b"))[0])
    hid_ref[...] = hid
    qkv_ref[0] = low(dot_nt(hid, w_ref[0]) + qb_ref[...])
    qkv_ref[1] = low(dot_nt(hid, w_ref[1]))
    qkv_ref[2] = low(dot_nt(hid, w_ref[2]) + vb_ref[...])
    rows = stream.shape[0] // clips
    for clip in range(clips):
        at = slice(clip * rows, (clip + 1) * rows)
        keys = qkv_ref[1, at, :]
        mixed = 0.0
        for queries, values in zip(head_masks(qkv_ref[0, at, :]), head_masks(qkv_ref[2, at, :])):
            mixed = mixed + dot_nn(low(small_probs(queries, keys, vis)), values)
        attn_ref[at, :] = low(mixed)
    part_ref[...] = low(dot_nn(attn_ref[...], wout_ref[...]))


def enc_units_kernel(
    stream_ref, total_ref, more_ref, vec_ref, wup_ref, upb_ref, wdown_ref,
    middle_ref, hid_ref, upper_ref, active_ref, part_ref,
):
    middle = stream_ref[...] + (total_ref[...].astype(F32) + more_ref[...].astype(F32)) + vec_at(vec_ref, "eout_b")
    middle_ref[...] = middle
    hid = low(layer_norm(middle, vec_at(vec_ref, "eln2_g"), vec_at(vec_ref, "eln2_b"))[0])
    hid_ref[...] = hid
    upper = dot_nt(hid, wup_ref[...]) + upb_ref[...]
    upper_ref[...] = upper
    active = low(gelu_value(upper))
    active_ref[...] = active
    part_ref[...] = low(dot_nn(active, wdown_ref[...]))


def pick_matrix(own, padded, first, shown_ref):
    row = lax.broadcasted_iota(jnp.int32, (own, padded), 0) + first
    return (row == shown_ref[...]).astype(F32)


def bridge_kernel(
    own, where_ref, middle_ref, total_ref, more_ref, vec_ref, link_ref, w_ref, shown_ref, pos_ref,
    result_ref, dstream_ref, hid_ref, q_ref, kv_ref,
):
    result_ref[...] = middle_ref[...] + (total_ref[...].astype(F32) + more_ref[...].astype(F32)) + vec_at(vec_ref, "edown_b")
    padded = shown_ref.shape[1]
    mine = result_ref[pl.ds(pl.multiple_of(where_ref[0] * padded, padded), padded), :]
    final = low(layer_norm(mine, vec_at(vec_ref, "elnf_g"), vec_at(vec_ref, "elnf_b"))[0])
    latent = dot_nn(final, link_ref[...]) + vec_at(vec_ref, "in_b")
    parts = []
    for _ in range(3):
        parts.append(low(latent))
        latent = latent - parts[-1].astype(F32)
    tile = pos_ref.shape[0] // 7

    def step(t, carry):
        first = pl.multiple_of(t * tile, tile)
        at = pl.ds(first, tile)
        pick = pick_matrix(tile, padded, where_ref[1] * own + first, shown_ref)
        chosen = low(pick)
        value = (dot_nn(chosen, parts[0]) + dot_nn(chosen, parts[1])) + dot_nn(chosen, parts[2])
        hidden = 1.0 - jnp.sum(pick, -1, keepdims=True)
        value = value + hidden * vec_at(vec_ref, "mask") + pos_ref[at, :]
        dstream_ref[at, :] = value
        hid_ref[at, :] = low(
            layer_norm(value, vec_at(vec_ref, "dln1_g"), vec_at(vec_ref, "dln1_b"))[0]
        )
        return carry

    lax.fori_loop(0, 7, step, 0)
    hid = hid_ref[...]
    width = hid.shape[1]
    q_ref[...] = low(dot_nt(hid, w_ref[:width, :]) + vec_at(vec_ref, "dq_b"))
    kv_ref[0] = low(dot_nt(hid, w_ref[width : 2 * width, :]))
    kv_ref[1] = low(dot_nt(hid, w_ref[2 * width :, :]) + vec_at(vec_ref, "dv_b"))


def bridge_back_kernel(
    own, where_ref, gq_ref, gkv_ref, got_ref, hid_ref, w_ref, dstream_ref, mid_ref, vec_ref, shown_ref,
    gw_ref, latent_ref, sums_ref, hgrad_ref,
):
    width = gq_ref.shape[1]
    gk = low(gkv_ref[0].astype(F32) + got_ref[0].astype(F32))
    gv = low(gkv_ref[1].astype(F32) + got_ref[1].astype(F32))
    hid = hid_ref[...]
    hgrad = 0.0
    for k, grad in enumerate((gq_ref[...], gk, gv)):
        at = slice(k * width, (k + 1) * width)
        gw_ref[at, :] = low(dot_tn(grad, hid))
        hgrad = hgrad + dot_nn(grad, w_ref[at, :])
    sums_ref[...] = jnp.zeros_like(sums_ref)
    hgrad_ref[...] = hgrad
    sums_ref[0:1, :] = col_sum(gq_ref[...].astype(F32))
    sums_ref[1:2, :] = col_sum(gv.astype(F32))
    latent_ref[...] = jnp.zeros_like(latent_ref)
    padded = shown_ref.shape[1]
    tile = own // 7
    gain = vec_at(vec_ref, "dln1_g")

    def step(t, carry):
        first = pl.multiple_of(t * tile, tile)
        at = pl.ds(first, tile)
        saved = layer_norm(dstream_ref[at, :], gain, gain)[1]
        sgrad, gain_grad, bias_grad = norm_back(hgrad_ref[at, :], saved, gain)
        din = sgrad + mid_ref[at, :]
        pick = pick_matrix(tile, padded, where_ref[1] * own + first, shown_ref)
        hidden = 1.0 - jnp.sum(pick, -1, keepdims=True)
        sums_ref[2:3, :] += gain_grad
        sums_ref[3:4, :] += bias_grad
        sums_ref[4:5, :] += col_sum(hidden * din)
        chosen = low(pick)
        high = low(din)
        rest = low(din - high.astype(F32))
        latent_ref[...] += dot_tn(chosen, high) + dot_tn(chosen, rest)
        return carry

    lax.fori_loop(0, 7, step, 0)


def enc_units_back_kernel(
    latent_ref, result_ref, vec_ref, link_ref, wdown_ref, wup_ref, upper_ref, active_ref, hid_ref,
    glink_ref, grad_ref, gdown_ref, gup_ref, part_ref, sums_ref,
):
    sums_ref[...] = jnp.zeros_like(sums_ref)
    latent = latent_ref[...]
    gain = vec_at(vec_ref, "elnf_g")
    final, saved = layer_norm(result_ref[...], gain, vec_at(vec_ref, "elnf_b"))
    glink_ref[...] = low(dot_tn(low(final), latent))
    grad, gain_grad, bias_grad = norm_back(dot_nt(latent, link_ref[...]), saved, gain)
    grad_ref[...] = grad
    sums_ref[0:1, : latent.shape[1]] = col_sum(latent.astype(F32))
    sums_ref[1:2, :] = gain_grad
    sums_ref[2:3, :] = bias_grad
    sums_ref[3:4, :] = col_sum(grad)
    down = low(grad)
    gdown_ref[...] = low(dot_tn(active_ref[...], down))
    upper = low(dot_nt(down, wdown_ref[...]) * gelu_slope(upper_ref[...]))
    sums_ref[4:5, :] = col_sum(upper.astype(F32))
    part_ref[...] = low(dot_nn(upper, wup_ref[...]))
    gup_ref[...] = low(dot_tn(upper, hid_ref[...]))


def enc_attention_back_kernel(
    vis, clips, total_ref, more_ref, grad_ref, middle_ref, vec_ref, attn_ref, wout_ref, qkv_ref, w_ref, hid_ref,
    mid_ref, gout_ref, gqkv_ref, part_ref, sums_ref, dqkv_ref,
):
    sums_ref[...] = jnp.zeros_like(sums_ref)
    gain = vec_at(vec_ref, "eln2_g")
    saved = layer_norm(middle_ref[...], gain, gain)[1]
    mid, gain_grad, bias_grad = norm_back((total_ref[...].astype(F32) + more_ref[...].astype(F32)), saved, gain)
    mid = mid + grad_ref[...]
    mid_ref[...] = mid
    sums_ref[0:1, :] = gain_grad
    sums_ref[1:2, :] = bias_grad
    sums_ref[2:3, :] = col_sum(mid)
    out = low(mid)
    gout_ref[...] = low(dot_tn(attn_ref[...], out))
    attn_grad = low(dot_nt(out, wout_ref[...]))
    rows = mid.shape[0] // clips
    for clip in range(clips):
        at = slice(clip * rows, (clip + 1) * rows)
        queries, keys, values = (head_masks(qkv_ref[k, at, :]) for k in range(3))
        all_keys, all_values = qkv_ref[1, at, :], qkv_ref[2, at, :]
        grads = head_masks(attn_grad[at, :])
        dq = dk = dv = 0.0
        for query, key, grad in zip(queries, keys, grads):
            prob = small_probs(query, all_keys, vis)
            dprob = dot_nt(grad, all_values)
            product = prob * dprob
            dscore = low(product - prob * jnp.sum(product, -1, keepdims=True))
            dv = dv + dot_tn(low(prob), grad)
            dq = dq + dot_nn(dscore, key)
            dk = dk + dot_tn(dscore, query)
        dqkv_ref[0, at, :] = low(dq * HD**-0.5)
        dqkv_ref[1, at, :] = low(dk * HD**-0.5)
        dqkv_ref[2, at, :] = low(dv)
    width = attn_ref.shape[1]
    sums_ref[3:4, :width] = col_sum(dqkv_ref[0].astype(F32))
    sums_ref[4:5, :width] = col_sum(dqkv_ref[2].astype(F32))
    part = 0.0
    for k in range(3):
        part = part + dot_nn(dqkv_ref[k], w_ref[k])
        gqkv_ref[k] = low(dot_tn(dqkv_ref[k], hid_ref[...]))
    part_ref[...] = low(part)


def enc_start_back_kernel(total_ref, more_ref, mid_ref, stream_ref, vec_ref, pix_ref, gembed_ref, sums_ref):
    sums_ref[...] = jnp.zeros_like(sums_ref)
    gain = vec_at(vec_ref, "eln1_g")
    saved = layer_norm(stream_ref[...], gain, gain)[1]
    grad, gain_grad, bias_grad = norm_back((total_ref[...].astype(F32) + more_ref[...].astype(F32)), saved, gain)
    grad = grad + mid_ref[...]
    sums_ref[0:1, :] = gain_grad
    sums_ref[1:2, :] = bias_grad
    sums_ref[2:3, :] = col_sum(grad)
    gembed_ref[...] = low(dot_tn(pix_ref[...], low(grad)))


def group_total(keep, send):
    mine = keep + narrow_flip(send, 1)
    rows = mine.shape[0] // 2
    one, two = mine[:rows], mine[rows:]
    bits = []
    bit = 1
    while bit < wide_digits(lax.axis_size(WD))[-1][0]:
        bits.append(bit)
        bit *= 2
    for bit in bits:
        one = one + wide_flip(one, bit)
    two = two + narrow_flip(two, 2)
    one = one + narrow_flip(one, 2)
    for bit in bits:
        two = two + wide_flip(two, bit)
    mine = jnp.concatenate([one, two], 0)
    return mine, narrow_flip(mine, 1)


def adam_update(weight, first, second, gradient, rate, decay):
    first_new = BETA_ONE * first + (1.0 - BETA_ONE) * gradient
    second_new = BETA_TWO * second + (1.0 - BETA_TWO) * gradient * gradient
    direction = (
        first_new
        / (1.0 - BETA_ONE**STEP)
        / (jnp.sqrt(second_new / (1.0 - BETA_TWO**STEP)) + EPS_ADAM)
    )
    return (first_new, second_new, weight - rate * (direction + decay * weight))


def pad_rows(value, rows, axis):
    if value.shape[axis] == rows:
        return value
    widths = [(0, 0)] * value.ndim
    widths[axis] = (0, rows - value.shape[axis])
    return jnp.pad(value, widths)


def per_device(
    pixels,
    visible,
    masked,
    groups,
    enc_qkv,
    enc_qkv_mom,
    enc_out,
    enc_out_mom,
    enc_up,
    enc_up_mom,
    enc_down,
    enc_down_mom,
    dec_qkv,
    dec_qkv_mom,
    dec_out,
    dec_out_mom,
    dec_up,
    dec_up_mom,
    dec_down,
    dec_down_mom,
    embed,
    embed_m,
    embed_v,
    enc_to_dec,
    enc_to_dec_m,
    enc_to_dec_v,
    head,
    head_m,
    head_v,
    vectors,
    vectors_m,
    vectors_v,
):
    wide = lax.axis_size(WD)
    me = lax.axis_index(NR)
    half, clip = me % 2, me // 2
    slow = wide_digits(wide)[-1]
    fast = slow[0]
    plane = place_in(slow)
    clips, vis = visible.shape
    tubs = pixels.shape[1]
    own = tubs // 2

    n_up = enc_up.shape[1]
    n_q = enc_qkv.shape[2]
    n_out = enc_out.shape[0]
    n_emb = embed.shape[0] // QN
    n_link = enc_to_dec.shape[0] * DD // D // QN
    m_up = dec_up.shape[1]
    m_qkv = dec_qkv.shape[1]
    m_out = dec_out.shape[0]
    m_head = head.shape[0] * (PIX // DD)

    up_rows, down_rows = enc_up.T, enc_down
    qkv_rows = jnp.swapaxes(enc_qkv, 1, 2).reshape(3 * n_q, D)
    dqkv_rows, dup_rows = dec_qkv.T, dec_up.T
    head_rows = head.reshape(m_head, DD)
    emb_cols = lax.dynamic_slice_in_dim(embed, me * (D // QN), D // QN, 1)
    m_link = enc_to_dec.shape[0] // QN
    link_rows = lax.dynamic_slice_in_dim(enc_to_dec, me * m_link, m_link, 0)
    pack_b = jnp.concatenate([low(emb_cols).reshape(n_emb, D), low(qkv_rows), low(enc_out)], 0)
    pack_c = low(jnp.concatenate([up_rows, down_rows], 0))
    pack_d = low(
        jnp.concatenate([dup_rows, dqkv_rows, dec_out, dec_down, head_rows, link_rows], 0)
    )
    pack_d = narrow_pair(pack_d, 2)
    line_b = slow_pieces(pack_b)
    pieces_b = all_pieces(line_b)
    came = tuple(line_b.values())
    pack_c, pack_d, vis_now, _ = lax.optimization_barrier((pack_c, pack_d, visible, came))
    line_c = slow_pieces(pack_c)
    full_b = assemble(pieces_b)
    pieces_c = all_pieces(tied(line_c, full_b))
    full_c = assemble(pieces_c)
    line_d = slow_pieces(after(pack_d, tuple(pieces_c.values())))
    embed_w = full_b[:, :n_emb].reshape(PIX, D // QN)
    w_qkv = full_b[:, n_emb : n_emb + 3 * n_q].reshape(wide, 3, n_q, D)
    w_qkv = jnp.swapaxes(w_qkv, 0, 1).reshape(3, wide * n_q, D)
    w_out = full_b[:, n_emb + 3 * n_q :].reshape(wide * n_out, D)
    w_up = full_c[:, :n_up].reshape(wide * n_up, D)
    w_down = full_c[:, n_up:].reshape(wide * n_up, D)
    table = vector_layout()

    def vec_of(name):
        offset, extent = table[name]
        return vectors[offset : offset + extent]

    def share_of(name):
        offset, extent = table[name]
        share = extent // QN
        return lax.dynamic_slice_in_dim(vectors, offset + me * share, share)[None, :]

    grads = {}

    padded = -(-vis // 16) * 16
    rows = clips * padded
    shown = jnp.pad(visible, ((0, 0), (0, padded - vis)), constant_values=-1)
    vis_rows = shown.reshape(rows)
    tube_ids = jnp.arange(tubs, dtype=jnp.int32)
    vis_pix = mm(low(vis_rows[:, None] == tube_ids[None, :]), pixels[0]).astype(BF)
    vec_row = vectors[None, :]
    now_rows = jnp.pad(vis_now, ((0, 0), (0, padded - vis)), constant_values=-1).reshape(rows)
    vis_table = sinusoid(now_rows, D)
    start = mm(vis_pix, embed_w)
    start = both(start, narrow_flip(start, 2), clip, 1)
    start = both(start, narrow_flip(start, 1), half, 2).reshape(rows, D)
    units = D // QN * 4
    stream, hid1, eqkv, eattn, part = call(
        functools.partial(enc_attention_kernel, vis, clips),
        [((rows, D), F32), ((rows, D), BF), ((3, rows, D // QN), BF), ((rows, D // QN), BF), ((rows, D), BF)],
        [start, vis_table, vec_row, w_qkv, share_of("eq_b"), share_of("ev_b"), w_out],
        2 * rows * D * D,
    )
    own_pix = after(lax.dynamic_slice_in_dim(pixels[0], half * own, own, 0), part)
    targets = group_targets(own_pix, groups)
    own_pos = after(half * own + jnp.arange(own, dtype=jnp.int32), part)
    own_table = sinusoid(own_pos, DD)
    parts = narrow_parts(part)
    pieces_d = all_pieces(tied(line_d, parts[1]))
    middle, hid2, upper, active, part = call(
        enc_units_kernel,
        [((rows, D), F32), ((rows, D), BF), ((rows, units), F32), ((rows, units), BF), ((rows, D), BF)],
        [stream, *parts, vec_row, w_up, share_of("eup_b"), w_down],
        4 * rows * D * units,
    )

    parts = narrow_parts(part)
    full_d = narrow_pair(assemble(tied(pieces_d, parts[0])), 1, 2)
    at, taken = 0, []
    for extent in (m_up, m_qkv, m_out, m_up, m_head, m_link):
        taken.append(full_d[:, :, :, at : at + extent].reshape(wide * QN * extent, DD))
        at += extent
    d_up, d_qkv, d_out, d_down, d_head, link_w = taken
    d_head = d_head.reshape(DD, PIX)

    where = jnp.stack([clip, half])
    clip_shown = lax.dynamic_slice_in_dim(shown, clip, 1, 0)
    enc_result, dstream, dh1, dq, dkv = call(
        functools.partial(bridge_kernel, own),
        [((rows, D), F32), ((own, DD), F32), ((own, DD), BF), ((own, DD), BF), ((2, own, DD), BF)],
        [where, middle, *parts, vec_row, link_w, d_qkv, clip_shown, own_table],
        6 * own * DD * DD,
        1,
    )
    pick = own_pos[:, None] == clip_shown
    hidden_row = 1.0 - jnp.sum(pick.astype(F32), -1, keepdims=True)
    all_kv = both(dkv, narrow_flip(dkv, 1), half, 1).reshape(2, tubs, DD)
    def plane_rows(parts):
        return jnp.stack([pad_rows(low(part), parts[0].shape[0], 0) for part in parts], 0)

    late = lax.optimization_barrier(
        (
            (enc_up_mom, enc_qkv_mom, enc_out_mom, enc_down_mom),
            (dec_up_mom, dec_qkv_mom, dec_out_mom, dec_down_mom),
            all_kv,
        )
    )
    (up_mom, qkv_mom, out_mom, down_mom), (dup_mom, dqkv_mom, dout_mom, ddown_mom), all_kv = late
    qkv_mom = jnp.swapaxes(qkv_mom, 1, 2).reshape(3 * n_q, D)
    enc_mom, dec_mom = joined_exchange(
        plane_rows([up_mom.T, qkv_mom, out_mom, down_mom]),
        plane_rows([dup_mom.T, dqkv_mom.T, dout_mom, ddown_mom]),
        slow,
    )

    tile = next(t for t in (224, 112, 16) if tubs % t == 0)
    dattn, mixed, dlog = attention_fwd(dq, all_kv, tile)
    dattn, enc_mom, dec_mom = lax.optimization_barrier((dattn, enc_mom, dec_mom))

    dmiddle = dstream + mm(dattn, d_out) + vec_of("dout_b")
    dh2, dsaved2 = layer_norm(dmiddle, vec_of("dln2_g"), vec_of("dln2_b"))
    dh2 = low(dh2)
    dupper = mm_nt(dh2, d_up) + vec_of("dup_b")
    dactive = low(gelu_value(dupper))
    dresult = dmiddle + mm(dactive, d_down) + vec_of("ddown_b")
    hf, hsaved = layer_norm(dresult, vec_of("dlnf_g"), vec_of("dlnf_b"))
    hf = low(hf)
    predicted = mm(hf, d_head) + vec_of("head_b")
    error = (predicted - targets) * hidden_row
    loss_part = jnp.sum(error * error)
    pred_grad = error * (2.0 / (clips * wide * (tubs - vis) * PIX))

    pred_low = low(pred_grad)
    g_head = mm_tn(hf, pred_low)
    grads["head_b"] = col_sum(pred_grad)
    dgrad, grads["dlnf_g"], grads["dlnf_b"] = norm_back(
        mm_nt(pred_low, d_head), hsaved, vec_of("dlnf_g")
    )
    down_low = low(dgrad)
    g_ddown = mm_tn(dactive, down_low)
    grads["ddown_b"] = col_sum(dgrad)
    upper_low = low(mm_nt(down_low, d_down) * gelu_slope(dupper))
    g_dup = mm_tn(upper_low, dh2)
    grads["dup_b"] = col_sum(upper_low.astype(F32))
    mid_grad, grads["dln2_g"], grads["dln2_b"] = norm_back(
        mm(upper_low, d_up), dsaved2, vec_of("dln2_g")
    )
    mid_grad = mid_grad + dgrad
    out_low = low(mid_grad)
    g_dout = mm_tn(dattn, out_low)
    grads["dout_b"] = col_sum(mid_grad)
    attn_grad = low(mm_nt(out_low, d_out))
    def dec_parts(value, extent):
        return low(value).reshape(4, fast, 2, 2, extent, DD)

    def fast_scatter(value, axis):
        digits = wide_digits(wide)[:-1]
        shape = value.shape
        value = value.reshape(
            shape[:axis] + tuple(radix for _, radix in digits[::-1]) + shape[axis + 1 :]
        )
        for count, digit in enumerate(digits):
            value = line_scatter(value, digit, axis + len(digits) - 1 - count)
        return value

    def half_sum(value, place, axis, bit):
        sent = low(pick_half(value, 1 - place, axis))
        return pick_half(value, place, axis).astype(F32) + narrow_flip(sent, bit).astype(F32)

    cut = m_up - m_qkv
    p_head = dec_parts(g_head.reshape(-1, DD), m_head)
    early = jnp.stack(
        [
            dec_parts(g_dup, m_up),
            jnp.concatenate([dec_parts(g_dout, m_out), p_head[:, :, :, :, cut:]], 4),
            dec_parts(g_ddown, m_up),
        ],
        0,
    )
    early = half_sum(early, half, 4, 1)
    attn_grad, early = lax.optimization_barrier((attn_grad, early))
    early = half_sum(early, clip, 3, 2)
    gq, gkv = attention_bwd(dq, all_kv, attn_grad, mixed, dlog, tile)
    gkv, early = lax.optimization_barrier((gkv, early))
    gkv = gkv.reshape(2, 2, own, DD)
    got = narrow_flip(pick_half(gkv, 1 - half, 1), 1)
    g_dqkv, latent_part, sums, _ = call(
        functools.partial(bridge_back_kernel, own),
        [((3 * DD, DD), BF), ((padded, DD), F32), ((8, DD), F32), ((own, DD), F32)],
        [where, gq, pick_half(gkv, half, 1), got, dh1, d_qkv, dstream, mid_grad, vec_row, clip_shown],
        12 * own * DD * DD,
        1,
    )
    for row, name in enumerate(("dq_b", "dv_b", "dln1_g", "dln1_b", "mask")):
        grads[name] = sums[row]

    late = jnp.concatenate([dec_parts(g_dqkv, m_qkv), p_head[:, :, :, :, :cut]], 4)[None]
    early = fast_scatter(after(early, latent_part), 2)

    latent_pair = low(pair_sum(latent_part))
    latent_low = both(latent_pair, narrow_flip(latent_pair, 2), clip, 0).reshape(rows, DD)
    g_link, egrad, g_down, g_up, part, sums = call(
        enc_units_back_kernel,
        [((D, DD), BF), ((rows, D), F32), ((units, D), BF), ((units, D), BF), ((rows, D), BF), ((8, D), F32)],
        [latent_low, enc_result, vec_row, link_w, w_down, w_up, upper, active, hid2],
        8 * rows * D * units,
    )
    grads["in_b"] = sums[0, :DD]
    for row, name in enumerate(("elnf_g", "elnf_b", "edown_b", "eup_b")):
        grads[name] = sums[row + 1]

    def enc_parts(value, extent):
        return low(value).reshape(4, fast, extent, D).transpose(1, 0, 2, 3)

    parts = narrow_parts(part)
    g_up, g_down, late, _ = lax.optimization_barrier((g_up, g_down, late, parts[0]))
    late = half_sum(late, half, 4, 1)
    late = half_sum(after(late, parts[1]), clip, 3, 2)
    sum_up = fast_scatter(enc_parts(g_up, n_up), 0)
    sum_down = fast_scatter(enc_parts(g_down, n_up), 0)
    mid_grad, g_out, g_qkv, part, sums, _ = call(
        functools.partial(enc_attention_back_kernel, vis, clips),
        [((rows, D), F32), ((D // QN, D), BF), ((3, D // QN, D), BF), ((rows, D), BF), ((8, D), F32), ((3, rows, D // QN), BF)],
        [*parts, egrad, middle, vec_row, eattn, w_out, eqkv, w_qkv, hid1],
        4 * rows * D * D,
    )
    for row, name in enumerate(("eln2_g", "eln2_b", "eout_b")):
        grads[name] = sums[row]
    grads["eq_b"], grads["ev_b"] = sums[3, : D // QN], sums[4, : D // QN]
    parts = narrow_parts(part)
    sum_up, sum_down, _ = lax.optimization_barrier((sum_up, sum_down, parts[1]))
    ends_sum = ends_total(joined(sum_up, early[0]), joined(sum_down, early[2]), slow, (0, 3))
    g_embed, sums = call(
        enc_start_back_kernel,
        [((PIX, D), BF), ((8, D), F32)],
        [*parts, mid_grad, stream, vec_row, vis_pix],
        2 * rows * D * PIX,
    )
    for row, name in enumerate(("eln1_g", "eln1_b", "emb_b")):
        grads[name] = sums[row]
    g_embed = pick_half(g_embed.reshape(wide, QN, n_emb, D), me, 1)
    g_link = pick_half(g_link.reshape(wide, QN, n_link, D), me, 1)
    part_qkv = jnp.concatenate([enc_parts(g, n_q) for g in g_qkv], 2)
    part_rest = jnp.concatenate(
        [enc_parts(g_out, n_out), enc_parts(g_embed, n_emb), enc_parts(g_link, n_link)], 2
    )
    longer = max(part_qkv.shape[2], part_rest.shape[2])
    sum_qkv = fast_scatter(pad_rows(part_qkv, longer, 2), 0)
    sum_rest = fast_scatter(pad_rows(part_rest, longer, 2), 0)
    late = fast_scatter(late, 2)
    sum_rest, ends_sum = lax.optimization_barrier((sum_rest, ends_sum))
    middle_sum = ends_total(joined(sum_qkv, late[0]), joined(sum_rest, early[1]), slow, (1, 2))
    enc_ends, dec_ends = parted(ends_sum, n_up)
    enc_middle, dec_middle = parted(middle_sum, longer)
    middle = (plane == 1) | (plane == 2)
    enc_sum = jnp.where(middle, pad_rows(enc_middle, n_up, 1), enc_ends)
    dec_sum = jnp.where(middle, dec_middle, dec_ends)

    leading = jnp.where(me == 0, 1.0, 0.0)

    def spread(share):
        full = jnp.zeros((share.shape[0] * QN,), F32)
        return lax.dynamic_update_slice_in_dim(full, share, me * share.shape[0], 0)

    pieces = []
    for name in table:
        piece = grads[name].reshape(-1)
        if name in ("eq_b", "ev_b", "eup_b"):
            piece = spread(piece)
        elif name[0] == "e" or name == "in_b":
            piece = leading * piece
        pieces.append(piece)
    vec_total = sum_all(jnp.concatenate(pieces + [loss_part[None]]).reshape(1, -1))[0]
    loss_sum = vec_total[-1]
    vec_total = vec_total[:-1]
    squares = jnp.sum(dec_sum * dec_sum) + jnp.sum(enc_sum * enc_sum)
    square_total = sum_tiny(jnp.broadcast_to(squares, (8, 128)))[0, 0]
    grad_norm = jnp.sqrt(square_total + jnp.sum(vec_total * vec_total))
    factor = jnp.minimum(1.0, CLIP_AT / grad_norm)

    counts = jnp.asarray(
        [[n_up, m_up], [3 * n_q, m_qkv], [n_out, m_out], [n_up, m_up]], jnp.int32
    )[plane]
    counts = jnp.concatenate([counts, half[None]])
    slabs = [
        enc_sum.reshape(4 * n_up, D),
        enc_mom.reshape(4 * n_up, D),
        dec_sum.reshape(4 * m_up, DD),
        dec_mom.reshape(4 * m_up, DD),
    ]
    periods = (n_up, m_up)
    mine, other = group_total(*packed_gram(periods, counts, factor[None], slabs))
    enc_back, dec_back, _ = lax.optimization_barrier((enc_sum, dec_sum, grad_norm))
    enc_grad, dec_grad = joined_exchange(low(enc_back), low(dec_back), slow)
    enc_grad, dec_grad = enc_grad.astype(F32) * factor, dec_grad.astype(F32) * factor

    def turned(value):
        return value.T

    def same(value):
        return value

    def unqkv(value):
        return jnp.swapaxes(value.reshape(3, n_q, D), 1, 2)

    rest = enc_grad[2, n_out : n_out + n_emb + n_link]
    rest = narrow_gather(rest)
    embed_grad = rest[:, :n_emb].reshape(embed.shape)
    link_grad = rest[:, n_emb:].reshape(enc_to_dec.shape)
    head_grad = jnp.concatenate([dec_grad[1, m_qkv:], dec_grad[2, m_out:]], 0).reshape(head.shape)
    adam = []
    for weight, first, second, grad, rate, decay in [
        (embed, embed_m, embed_v, embed_grad, RATE_ADAM, DECAY),
        (enc_to_dec, enc_to_dec_m, enc_to_dec_v, link_grad, RATE_ADAM, DECAY),
        (head, head_m, head_v, head_grad, RATE_ADAM, DECAY),
        (vectors, vectors_m, vectors_v, factor * vec_total, RATE_VECTOR, 0.0),
    ]:
        adam += adam_update(weight, first, second, grad, rate, decay)
    entries = [
        (enc_qkv, enc_qkv_mom, enc_grad[1, : 3 * n_q], unqkv, 3 * D),
        (enc_out, enc_out_mom, enc_grad[2, :n_out], same, D),
        (enc_up, enc_up_mom, enc_grad[0], turned, FE),
        (enc_down, enc_down_mom, enc_grad[3], same, FE),
        (dec_qkv, dec_qkv_mom, dec_grad[1, :m_qkv], turned, 3 * DD),
        (dec_out, dec_out_mom, dec_grad[2, :m_out], same, DD),
        (dec_up, dec_up_mom, dec_grad[0], turned, FD),
        (dec_down, dec_down_mom, dec_grad[3], same, FD),
    ]
    moms = [MOMENTUM * mom + side(grad) for _, mom, grad, side, _ in entries]
    mine, moms, adam = lax.optimization_barrier((mine, moms, adam))
    enc_ortho, dec_ortho = orthogonal(periods, counts, factor[None], mine, other, slabs)
    enc_ortho, dec_ortho = joined_exchange(
        enc_ortho.reshape(4, n_up, D), dec_ortho.reshape(4, m_up, DD), slow
    )
    enc_ortho, dec_ortho = enc_ortho.astype(F32), dec_ortho.astype(F32)
    results = [loss_sum, grad_norm]
    orthos = [
        enc_ortho[1, : 3 * n_q],
        enc_ortho[2, :n_out],
        enc_ortho[0],
        enc_ortho[3],
        dec_ortho[1, :m_qkv],
        dec_ortho[2, :m_out],
        dec_ortho[0],
        dec_ortho[3],
    ]
    for (weight, _, _, side, largest), mom, part in zip(entries, moms, orthos):
        step = RATE_MUON * 0.2 * math.sqrt(largest)
        results += [weight * (1.0 - RATE_MUON * DECAY) - step * side(part), mom]
    results += adam
    return tuple(results)


def solution(mesh):
    enc, dec = (NR, WD), (WD, NR)
    muon = [P(None, None, enc), P(enc, None), P(None, enc), P(enc, None)]
    muon += [P(None, dec), P(dec, None), P(None, dec), P(dec, None)]
    pairs = [spec for spec in muon for _ in range(2)]
    adam = [P(WD, None)] * 6 + [P(dec, None)] * 3 + [P()] * 3
    in_specs = [P(WD, None, None), P(WD, None), P(WD, None), P()] + pairs + adam
    out_specs = [P(), P()] + pairs + adam
    return jax.shard_map(
        per_device,
        mesh=mesh,
        in_specs=tuple(in_specs),
        out_specs=tuple(out_specs),
        check_vma=False,
    )
```

time: 842 us -> 644 us (0.76)
  matrix products: 228 us -> 33.2 us
  Pallas kernels: 0 us -> 161 us
  starting transfers between devices: 151 us -> 93.9 us
  other arithmetic: 142 us -> 92.9 us
  local copies, waits for them, and re-layouts: 117 us -> 75.5 us
    dot_general x52 -> x0, matrix products: 165 us -> none  [the longest x36 71.3 us: hdot(): return jnp.dot(left, right, precision=HIGH, preferred_element_type=F32)]
    pallas_call x0 -> x11, Pallas kernels: none -> 161 us  [the longest x1 52.3 us: orthogonal(): pl.pallas_call(functools.partial(ortho_kernel, periods), in_specs=[pl.Blo...]
    ppermute x36 -> x6, starting transfers between devices: 70.5 us -> 13.1 us  [ends_total(): total = total + lax.ppermute(sent, WD, pairs).astype(F32)]
    convert_element_type x12 -> x13, other arithmetic: 32.4 us -> 5.84 us  [low(): return value.astype(BF)]
    reshape x15 -> x7, local copies, waits for them, and re-layouts: 27.6 us -> 8.16 us  [the longest x2 2.93 us: per_device(): full_d[:, :, :, at:at + extent].reshape(wide * QN * extent, DD)]
    slice x28 -> x19, local copies, waits for them, and re-layouts: 26.3 us -> 6.92 us  [the longest x7 1.06 us: joined(): small[:, :rows]]
    reduce_sum x17 -> x3, other arithmetic: 21.6 us -> 2.32 us  [the longest x2 2.18 us: col_sum(): return jnp.sum(value, 0, keepdims=True)]
    ppermute x36 -> x6, waiting for transfers between devices: 52.4 us -> 33.1 us  [ends_total(): total = total + lax.ppermute(sent, WD, pairs).astype(F32)]
  transfers between devices with their start and end apart: 103 -> 76, of which waited for: 33 -> 32; matrix products, arithmetic and copies ran while one was open for 51% -> 19% of each run, Pallas kernels for 0% -> 14%
where the time goes in v1:
time: 644 us; the launch traced here: 638 us
  waiting for transfers between devices  174 us (27%)
  Pallas kernels  161 us (25%)
  starting transfers between devices  93.9 us (15%)
  other arithmetic  92.9 us (14%)
  local copies, waits for them, and re-layouts  75.5 us (12%)
  matrix products  33.2 us (5%)
  between operations  7.43 us (1%)
    ppermute x39, waiting for transfers between devices, wide_flip(): return lax.ppermute(value, WD, [(src, src ^ bit) for src in range(count)])  88.2 us
    ppermute x39, starting transfers between devices, wide_flip(): return lax.ppermute(value, WD, [(src, src ^ bit) for src in range(count)])  64.3 us
    ppermute x31, waiting for transfers between devices, narrow_flip(): return lax.ppermute(value, NR, [(src, src ^ bit) for src in range(QN)])  52.5 us
    pallas_call x1, Pallas kernels, orthogonal(): pl.pallas_call(functools.partial(ortho_kernel, periods), in_specs=[pl.Blo...  52.3 us
    pallas_call x7, Pallas kernels, call(): pl.pallas_call(kernel, in_specs=[pl.BlockSpec(memory_space=pltpu.SMEM)] *...  49.6 us
    ppermute x6, waiting for transfers between devices, ends_total(): total = total + lax.ppermute(sent, WD, pairs).astype(F32)  33.1 us
    pallas_call x1, Pallas kernels, attention_bwd(): pl.pallas_call(functools.partial(attn_bwd_kernel, tile), grid=(pairs,), i...  31 us
    pallas_call x1, Pallas kernels, attention_fwd(): pl.pallas_call(functools.partial(attn_fwd_kernel, tile), grid=(pairs,), i...  23.1 us
  transfers between devices with their start and end apart: 76, of which 32 were waited for; matrix products, arithmetic and copies ran while one was open for 19% of the time, Pallas kernels for 14%

profile of v1, /device:TPU:0, one launch (start us, length us, event | category | flops | bytes accessed | tf_op | source)
XLA Modules:
  0.0 637.6 jit_solution(8808772961620376676)
XLA Ops:
  3.9 5.1 collective-permute-start
  15.1 4.4 fusion.12.pix_ref
  20.3 7.5 %collective-permute-done.2 = bf16[144,768]{1,0:T(8,128)(2,1)S(1)} collective-permute-done((bf16[144,768]{1,0:T(8,128)(2,1)S(1)}, bf16[144,768]{1,0:T(8,128)(2,1)S(1)}, u32[]{:S(2)}, u32[]{:S(2)}) %collective-permute-start.2) | collective-permute-done | bytes 221216 | tf_op jit(solution)/shard_map/ppermute | solution.py:94
  31.0 3.0 collective-permute-start.11
  35.5 8.4 %collective-permute-done.3 = bf16[3,144,768]{2,1,0:T(8,128)(2,1)S(1)} collective-permute-done((bf16[3,144,768]{2,1,0:T(8,128)(2,1)S(1)}, bf16[3,144,768]{2,1,0:T(8,128)(2,1)S(1)}, u32[]{:S(2)}, u32[]{:S(2)}) %collective-permute-start.3) | collective-permute-done | bytes 663584 | tf_op jit(solution)/shard_map/ppermute | solution.py:94
  45.5 2.4 reshape.1537
  57.8 2.2 pad_maximum_fusion.17
  66.8 3.5 collective-permute-start.17
  74.2 5.0 shard_map.535
  86.3 9.7 %collective-permute-done.18 = bf16[2,216,384]{2,1,0:T(8,128)(2,1)S(1)} collective-permute-done((bf16[2,216,384]{2,1,0:T(8,128)(2,1)S(1)}, bf16[2,216,384]{2,1,0:T(8,128)(2,1)S(1)}, u32[]{:S(2)}, u32[]{:S(2)}) %collective-permute-start.18) | collective-permute-done | bytes 331808 | tf_op jit(solution)/shard_map/ppermute | solution.py:94
  101.1 4.6 shard_map.536
  109.2 14.1 %collective-permute-done.21 = bf16[3,2,216,384]{3,2,1,0:T(8,128)(2,1)S(1)} collective-permute-done((bf16[3,2,216,384]{3,2,1,0:T(8,128)(2,1)}, bf16[3,2,216,384]{3,2,1,0:T(8,128)(2,1)S(1)}, u32[]{:S(2)}, u32[]{:S(2)}) %collective-permute-start.21) | collective-permute-done | bytes 995360 | tf_op jit(solution)/shard_map/ppermute | solution.py:94
  123.4 4.8 collective-permute-done.20
  132.2 3.0 multiply_sine_fusion
  142.8 2.1 reshape.1548.w_ref
  146.8 4.9 collective-permute-done.16.more_ref
  151.7 8.7 %shard_map.537 = (f32[320,768]{1,0:T(8,128)}, f32[784,384]{1,0:T(8,128)}, bf16[784,384]{1,0:T(8,128)(2,1)}, bf16[784,384]{1,0:T(8,128)(2,1)}, bf16[2,784,384]{2,1,0:T(8,128)(2,1)}) custom-call(s32[2]{0:T(128)} %pad_add_fusion.where_ref, f32[320,768]{1,0:T(8,128)} %get-tuple-element.148.middle_ref, bf16[320,768]{1,0:T(8,128)(2,1)} %copy-done.25, ...), custom_call_target="tpu_custom_call" | custom-call | flops 1000 | bytes 1000 | tf_op jit(solution)/shard_map/pallas_call | solution.py:608
  160.4 4.3 multiply_reduce_fusion.3
  171.5 2.3 collective-permute-start.24
  173.8 5.3 collective-permute-start.25
  180.9 2.4 reshape_reshape.3
  183.3 23.1 %shard_map.538 = (bf16[784,384]{1,0:T(8,128)(2,1)}, f32[784,384]{1,0:T(8,128)}, f32[3,2,784]{2,1,0:T(2,128)}) custom-call(bf16[784,384]{1,0:T(8,128)(2,1)} %get-tuple-element.165.q_ref, bf16[2,1568,384]{2,1,0:T(8,128)(2,1)} %bitcast.508), custom_call_target="tpu_custom_call" | custom-call | flops 1000 | bytes 1000 | tf_op jit(solution)/shard_map/pallas_call | solution.py:384
  214.9 4.8 multiply_reduce_fusion
  219.7 2.2 multiply_reduce_fusion.5
  223.0 2.8 convolution_convert_fusion
  225.8 4.1 convert_reduce_fusion
  229.8 2.9 convolution_convert_fusion.2
  232.7 2.1 multiply_reduce_fusion.6
  234.9 2.7 convolution_convert_fusion.1
  239.3 2.4 convert_element_type.388
  248.1 2.6 collective-permute-done.27
  250.7 2.4 convert_add_fusion
  255.6 31.0 %shard_map.539 = (bf16[784,384]{1,0:T(8,128)(2,1)}, bf16[2,1568,384]{2,1,0:T(8,128)(2,1)}) custom-call(bf16[784,384]{1,0:T(8,128)(2,1)} %get-tuple-element.165.q_ref, bf16[2,1568,384]{2,1,0:T(8,128)(2,1)} %bitcast.509, bf16[784,384]{1,0:T(8,128)(2,1)} %convolution_convert_fusion.3.g_ref, f32[784,384]{1,0:T(8,128)} %get-tuple-element.181.of_ref, ...), custom_call_target="tpu_custom_call" | custom-call | flops 1000 | bytes 1000 | tf_op jit(solution)/shard_map/pallas_call | solution.py:426
  290.3 2.9 collective-permute-done.29.got_ref
  294.2 10.0 %shard_map.540 = (bf16[1152,384]{1,0:T(8,128)(2,1)}, f32[160,384]{1,0:T(8,128)}, f32[8,384]{1,0:T(8,128)}, f32[784,384]{1,0:T(8,128)}) custom-call(s32[2]{0:T(128)} %pad_add_fusion.where_ref, bf16[784,384]{1,0:T(8,128)(2,1)} %get-tuple-element.183.gq_ref, bf16[2,784,384]{2,1,0:T(8,128)(2,1)} %get-tuple-element.315.gkv_ref, bf16[2,784,384]{2,1,0:T(8,128)(2,1)} %copy-done.29, ...), custom_call_target="tpu_custom_call" | custom-call | flops 1000 | bytes 1000 | tf_op jit(solution)/shard_map/pallas_call | solution.py:608
  309.8 3.9 collective-permute-done.31
  314.4 7.7 %shard_map.541 = (bf16[768,384]{1,0:T(8,128)(2,1)}, f32[320,768]{1,0:T(8,128)}, bf16[768,768]{1,0:T(8,128)(2,1)}, bf16[768,768]{1,0:T(8,128)(2,1)}, bf16[320,768]{1,0:T(8,128)(2,1)}, /*index=5*/f32[8,768]{1,0:T(8,128)}) custom-call(bf16[320,384]{1,0:T(8,128)(2,1)} %bitcast.563, f32[320,768]{1,0:T(8,128)} %get-tuple-element.189.result_ref, ...), custom_call_target="tpu_custom_call" | custom-call | flops 1000 | bytes 1000 | tf_op jit(solution)/shard_map/pallas_call | solution.py:608
  322.2 2.2 reshape.1561
  336.9 8.2 %collective-permute-done.33.more_ref = bf16[320,768]{1,0:T(8,128)(2,1)S(1)} collective-permute-done((bf16[320,768]{1,0:T(8,128)(2,1)S(1)}, bf16[320,768]{1,0:T(8,128)(2,1)S(1)}, u32[]{:S(2)}, u32[]{:S(2)}) %collective-permute-start.33) | collective-permute-done | bytes 491552 | tf_op jit(solution)/shard_map/ppermute | solution.py:98
  345.9 7.9 %shard_map.542 = (f32[320,768]{1,0:T(8,128)}, bf16[192,768]{1,0:T(8,128)(2,1)}, bf16[3,192,768]{2,1,0:T(8,128)(2,1)}, bf16[320,768]{1,0:T(8,128)(2,1)}, f32[8,768]{1,0:T(8,128)}, /*index=5*/bf16[3,320,192]{2,1,0:T(8,128)(2,1)}) custom-call(bf16[320,768]{1,0:T(8,128)(2,1)} %copy-done.27, bf16[320,768]{1,0:T(8,128)(2,1)} %copy-done.59, ...), custom_call_target="tpu_custom_call" | custom-call | flops 1000 | bytes 1000 | tf_op jit(solution)/shard_map/pallas_call | solution.py:608
  366.4 6.0 collective-permute-done.43
  378.2 8.9 %collective-permute-done.35.more_ref = bf16[320,768]{1,0:T(8,128)(2,1)S(1)} collective-permute-done((bf16[320,768]{1,0:T(8,128)(2,1)S(1)}, bf16[320,768]{1,0:T(8,128)(2,1)S(1)}, u32[]{:S(2)}, u32[]{:S(2)}) %collective-permute-start.35) | collective-permute-done | bytes 491552 | tf_op jit(solution)/shard_map/ppermute | solution.py:98
  392.0 4.1 collective-permute-start.51
  396.1 5.6 shard_map.543
  407.4 8.3 %collective-permute-done.45 = bf16[4,84,768]{2,0,1:T(4,128)(2,1)S(1)} collective-permute-done((bf16[4,84,768]{2,0,1:T(4,128)(2,1)S(1)}, bf16[4,84,768]{2,0,1:T(4,128)(2,1)S(1)}, u32[]{:S(2)}, u32[]{:S(2)}) %collective-permute-start.45) | collective-permute-done | bytes 516128 | tf_op jit(solution)/shard_map/ppermute | solution.py:94
  415.8 23.4 %collective-permute-done.49 = bf16[4,120,768]{2,1,0:T(8,128)(2,1)} collective-permute-done((bf16[4,120,768]{2,1,0:T(8,128)(2,1)}, bf16[4,120,768]{2,1,0:T(8,128)(2,1)}, u32[]{:S(2)}, u32[]{:S(2)}) %collective-permute-start.49) | collective-permute-done | bytes 737312 | tf_op jit(solution)/shard_map/ppermute | solution.py:202
  439.2 3.0 convert_add_fusion.1
  443.6 2.3 collective-permute-start.52
  447.1 2.1 collective-permute-start.53
  453.3 3.8 collective-permute-done.37
  458.8 2.9 collective-permute-done.38
  462.9 9.7 %collective-permute-done.53 = bf16[4,108,768]{2,0,1:T(4,128)(2,1)} collective-permute-done((bf16[4,108,768]{2,0,1:T(4,128)(2,1)}, bf16[4,108,768]{2,0,1:T(4,128)(2,1)}, u32[]{:S(2)}, u32[]{:S(2)}) %collective-permute-start.53) | collective-permute-done | bytes 663584 | tf_op jit(solution)/shard_map/ppermute | solution.py:202
  480.5 7.7 %collective-permute-start.40 = (f32[1,19201]{1,0:T(1,128)S(1)}, f32[1,19201]{1,0:T(1,128)S(1)}, u32[]{:S(2)}, u32[]{:S(2)}) collective-permute-start(f32[1,19201]{1,0:T(1,128)S(1)} %add.549), channel_id=1, source_target_pairs={{0,16},{4,20},{8,24},{12,28},{16,0},{20,4},{24,8},{28,12},{1,17},{... | collective-permute-start | bytes 230420 | tf_op jit(solution)/shard_map/ppermute | solution.py:94
  494.1 2.8 collective-permute-start.61
  500.9 2.4 collective-permute-start.67
  505.3 4.7 shard_map.544
  510.8 6.5 %collective-permute-done.68 = bf16[120,768]{1,0:T(8,128)(2,1)S(1)} collective-permute-done((bf16[120,768]{1,0:T(8,128)(2,1)S(1)}, bf16[120,768]{1,0:T(8,128)(2,1)S(1)}, u32[]{:S(2)}, u32[]{:S(2)}) %collective-permute-start.68) | collective-permute-done | bytes 184352 | tf_op jit(solution)/shard_map/ppermute | solution.py:94
  532.0 5.6 collective-permute-done.63
  542.6 7.5 %collective-permute-done.64 = f32[960,128]{1,0:T(8,128)S(1)} collective-permute-done((f32[960,128]{1,0:T(8,128)S(1)}, f32[960,128]{1,0:T(8,128)S(1)}, u32[]{:S(2)}, u32[]{:S(2)}) %collective-permute-start.64) | collective-permute-done | bytes 491552 | tf_op jit(solution)/shard_map/ppermute | solution.py:98
  554.9 2.6 multiply_subtract_fusion
  558.5 52.3 %shard_map.545 = (bf16[384,768]{1,0:T(8,128)(2,1)}, bf16[192,384]{1,0:T(8,128)(2,1)}) custom-call(s32[3]{0:T(128)} %pad_add_fusion.1.counts_ref, f32[1]{0:T(128)} %bitcast.155.factor_ref, f32[1920,128]{1,0:T(8,128)} %copy-done.15, f32[1920,128]{1,0:T(8,128)} %copy-done.48, f32[384,768]{1,0:T(8,128)} %bitcast.511, bf16[384,768]{1,0:T(8,128)(2,1)} %bitcast.526, ...), custom_call_target="tpu_custom_call" | custom-call | flops 1000 | bytes 1000 | tf_op jit(solution)/shard_map/pallas_call | solution.py:594
  613.1 4.3 collective-permute-start.75
  617.9 4.5 collective-permute-done.73
  622.4 7.2 %collective-permute-done.74 = bf16[120,768]{1,0:T(8,128)(2,1)S(1)} collective-permute-done((bf16[120,768]{1,0:T(8,128)(2,1)S(1)}, bf16[120,768]{1,0:T(8,128)(2,1)S(1)}, u32[]{:S(2)}, u32[]{:S(2)}) %collective-permute-start.74) | collective-permute-done | bytes 184352 | tf_op jit(solution)/shard_map/ppermute | solution.py:94
  (651 shorter events, 208.1 us)
Async XLA Ops:
  3.9 15.6 %collective-permute-start = (bf16[144,768]{1,0:T(8,128)(2,1)S(1)}, bf16[144,768]{1,0:T(8,128)(2,1)S(1)}, u32[]{:S(2)}, u32[]{:S(2)}) collective-permute-start(bf16[144,768]{1,0:T(8,128)(2,1)S(1)} %pad_maximum_fusion.42), channel_id=1, source_target_pairs={{0,24},{4,28},{8,16},{12,20},{16,8},{20,12},{24,0},{28,4},{1,25},{... | collective-permute-start | bytes 663560 | tf_op jit(solution)/shard_map/ppermute | solution.py:94
  9.0 11.3 %collective-permute-start.1 = (bf16[144,768]{1,0:T(8,128)(2,1)S(1)}, bf16[144,768]{1,0:T(8,128)(2,1)S(1)}, u32[]{:S(2)}, u32[]{:S(2)}) collective-permute-start(bf16[144,768]{1,0:T(8,128)(2,1)S(1)} %pad_maximum_fusion.42), channel_id=1, source_target_pairs={{0,8},{4,12},{8,0},{12,4},{16,24},{20,28},{24,16},{28,20},{1,9},{5... | collective-permute-start | bytes 663560 | tf_op jit(solution)/shard_map/ppermute | solution.py:94
  9.0 18.8 %collective-permute-start.2 = (bf16[144,768]{1,0:T(8,128)(2,1)S(1)}, bf16[144,768]{1,0:T(8,128)(2,1)S(1)}, u32[]{:S(2)}, u32[]{:S(2)}) collective-permute-start(bf16[144,768]{1,0:T(8,128)(2,1)S(1)} %pad_maximum_fusion.42), channel_id=1, source_target_pairs={{0,16},{4,20},{8,24},{12,28},{16,0},{20,4},{24,8},{28,12},{1,17},{... | collective-permute-start | bytes 663560 | tf_op jit(solution)/shard_map/ppermute | solution.py:94
  9.7 25.7 %collective-permute-start.4 = (bf16[144,768]{1,0:T(8,128)(2,1)S(1)}, bf16[144,768]{1,0:T(8,128)(2,1)S(1)}, u32[]{:S(2)}, u32[]{:S(2)}) collective-permute-start(bf16[144,768]{1,0:T(8,128)(2,1)S(1)} %pad_maximum_fusion.42), channel_id=1, source_target_pairs={{0,4},{4,0},{8,12},{12,8},{16,20},{20,16},{24,28},{28,24},{1,5},{5... | collective-permute-start | bytes 663560 | tf_op jit(solution)/shard_map/ppermute | solution.py:94
  13.3 16.9 %collective-permute-start.7 = (bf16[216,384]{1,0:T(8,128)(2,1)S(1)}, bf16[216,384]{1,0:T(8,128)(2,1)S(1)}, u32[]{:S(2)}, u32[]{:S(2)}) collective-permute-start(bf16[216,384]{1,0:T(8,128)(2,1)S(1)} %concatenate.364), channel_id=1, source_target_pairs={{0,2},{1,3},{2,0},{3,1},{4,6},{5,7},{6,4},{7,5},{8,10},{9,11},{10,... | collective-permute-start | bytes 497672 | tf_op jit(solution)/shard_map/ppermute | solution.py:98
  27.9 16.0 %collective-permute-start.3 = (bf16[3,144,768]{2,1,0:T(8,128)(2,1)S(1)}, bf16[3,144,768]{2,1,0:T(8,128)(2,1)S(1)}, u32[]{:S(2)}, u32[]{:S(2)}) collective-permute-start(bf16[3,144,768]{2,1,0:T(8,128)(2,1)S(1)} %pad_maximum_fusion.22), channel_id=1, source_target_pairs={{0,4},{4,0},{8,12},{12,8},{16,20},{20,16},{24,28},{28,24},{1,5},{5... | collective-permute-start | bytes 1990664 | tf_op jit(solution)/shard_map/ppermute | solution.py:94
  31.0 24.1 %collective-permute-start.10 = (bf16[192,768]{1,0:T(8,128)(2,1)}, bf16[192,768]{1,0:T(8,128)(2,1)}, u32[]{:S(2)}, u32[]{:S(2)}) collective-permute-start(bf16[192,768]{1,0:T(8,128)(2,1)} %pad_maximum_fusion.40), channel_id=1, source_target_pairs={{0,8},{4,12},{8,0},{12,4},{16,24},{20,28},{24,16},{28,20},{1,9},{5... | collective-permute-start | bytes 884744 | tf_op jit(solution)/shard_map/ppermute | solution.py:94
  31.0 24.1 %collective-permute-start.11 = (bf16[192,768]{1,0:T(8,128)(2,1)}, bf16[192,768]{1,0:T(8,128)(2,1)}, u32[]{:S(2)}, u32[]{:S(2)}) collective-permute-start(bf16[192,768]{1,0:T(8,128)(2,1)} %pad_maximum_fusion.40), channel_id=1, source_target_pairs={{0,16},{4,20},{8,24},{12,28},{16,0},{20,4},{24,8},{28,12},{1,17},{... | collective-permute-start | bytes 884744 | tf_op jit(solution)/shard_map/ppermute | solution.py:94
  34.1 21.1 %collective-permute-start.12 = (bf16[192,768]{1,0:T(8,128)(2,1)}, bf16[192,768]{1,0:T(8,128)(2,1)}, u32[]{:S(2)}, u32[]{:S(2)}) collective-permute-start(bf16[192,768]{1,0:T(8,128)(2,1)} %pad_maximum_fusion.40), channel_id=1, source_target_pairs={{0,24},{4,28},{8,16},{12,20},{16,8},{20,12},{24,0},{28,4},{1,25},{... | collective-permute-start | bytes 884744 | tf_op jit(solution)/shard_map/ppermute | solution.py:94
  49.2 7.5 %collective-permute-start.5 = (f32[320,192]{0,1:T(8,128)}, f32[320,192]{0,1:T(8,128)S(1)}, u32[]{:S(2)}, u32[]{:S(2)}) collective-permute-start(f32[320,192]{0,1:T(8,128)} %fusion.119), channel_id=1, source_target_pairs={{0,2},{1,3},{2,0},{3,1},{4,6},{5,7},{6,4},{7,5},{8,10},{9,11},{10,... | collective-permute-start | bytes 737288 | tf_op jit(solution)/shard_map/ppermute | solution.py:98
  55.1 10.9 %collective-permute-start.14 = (bf16[192,768]{1,0:T(8,128)(2,1)}, bf16[192,768]{1,0:T(8,128)(2,1)S(1)}, u32[]{:S(2)}, u32[]{:S(2)}) collective-permute-start(bf16[192,768]{1,0:T(8,128)(2,1)} %pad_maximum_fusion.40), channel_id=1, source_target_pairs={{0,4},{4,0},{8,12},{12,8},{16,20},{20,16},{24,28},{28,24},{1,5},{5... | collective-permute-start | bytes 884744 | tf_op jit(solution)/shard_map/ppermute | solution.py:94
  57.8 14.9 %collective-permute-start.6 = (f32[320,2,192]{0,2,1:T(8,128)S(1)}, f32[320,2,192]{0,2,1:T(8,128)S(1)}, u32[]{:S(2)}, u32[]{:S(2)}) collective-permute-start(f32[320,2,192]{0,2,1:T(8,128)S(1)} %pad_maximum_fusion.28), channel_id=1, source_target_pairs={{0,1},{1,0},{2,3},{3,2},{4,5},{5,4},{6,7},{7,6},{8,9},{9,8},{10,11... | collective-permute-start | bytes 1474568 | tf_op jit(solution)/shard_map/ppermute | solution.py:98
  60.0 22.4 %collective-permute-start.13 = (bf16[3,192,768]{2,1,0:T(8,128)(2,1)}, bf16[3,192,768]{2,1,0:T(8,128)(2,1)}, u32[]{:S(2)}, u32[]{:S(2)}) collective-permute-start(bf16[3,192,768]{2,1,0:T(8,128)(2,1)} %pad_maximum_fusion.17), channel_id=1, source_target_pairs={{0,4},{4,0},{8,12},{12,8},{16,20},{20,16},{24,28},{28,24},{1,5},{5... | collective-permute-start | bytes 2654216 | tf_op jit(solution)/shard_map/ppermute | solution.py:94
  66.8 19.5 %collective-permute-start.17 = (bf16[2,216,384]{2,1,0:T(8,128)(2,1)S(1)}, bf16[2,216,384]{2,1,0:T(8,128)(2,1)S(1)}, u32[]{:S(2)}, u32[]{:S(2)}) collective-permute-start(bf16[2,216,384]{2,1,0:T(8,128)(2,1)S(1)} %copy-done.28), channel_id=1, source_target_pairs={{0,8},{4,12},{8,0},{12,4},{16,24},{20,28},{24,16},{28,20},{1,9},{5... | collective-permute-start | bytes 995336 | tf_op jit(solution)/shard_map/ppermute | solution.py:94
  70.2 25.8 %collective-permute-start.18 = (bf16[2,216,384]{2,1,0:T(8,128)(2,1)S(1)}, bf16[2,216,384]{2,1,0:T(8,128)(2,1)S(1)}, u32[]{:S(2)}, u32[]{:S(2)}) collective-permute-start(bf16[2,216,384]{2,1,0:T(8,128)(2,1)S(1)} %copy-done.28), channel_id=1, source_target_pairs={{0,16},{4,20},{8,24},{12,28},{16,0},{20,4},{24,8},{28,12},{1,17},{... | collective-permute-start | bytes 995336 | tf_op jit(solution)/shard_map/ppermute | solution.py:94
  71.1 25.0 %collective-permute-start.19 = (bf16[2,216,384]{2,1,0:T(8,128)(2,1)S(1)}, bf16[2,216,384]{2,1,0:T(8,128)(2,1)S(1)}, u32[]{:S(2)}, u32[]{:S(2)}) collective-permute-start(bf16[2,216,384]{2,1,0:T(8,128)(2,1)S(1)} %copy-done.28), channel_id=1, source_target_pairs={{0,24},{4,28},{8,16},{12,20},{16,8},{20,12},{24,0},{28,4},{1,25},{... | collective-permute-start | bytes 995336 | tf_op jit(solution)/shard_map/ppermute | solution.py:94
  84.1 12.9 %collective-permute-start.9 = (bf16[320,768]{1,0:T(8,128)(2,1)S(1)}, bf16[320,768]{1,0:T(8,128)(2,1)S(1)}, u32[]{:S(2)}, u32[]{:S(2)}) collective-permute-start(bf16[320,768]{1,0:T(8,128)(2,1)S(1)} %add_convert_fusion.5.total_ref), channel_id=1, source_target_pairs={{0,2},{1,3},{2,0},{3,1},{4,6},{5,7},{6,4},{7,5},{8,10},{9,11},{10,... | collective-permute-start | bytes 1474568 | tf_op jit(solution)/shard_map/ppermute | solution.py:98
  98.1 25.2 %collective-permute-start.21 = (bf16[3,2,216,384]{3,2,1,0:T(8,128)(2,1)}, bf16[3,2,216,384]{3,2,1,0:T(8,128)(2,1)S(1)}, u32[]{:S(2)}, u32[]{:S(2)}) collective-permute-start(bf16[3,2,216,384]{3,2,1,0:T(8,128)(2,1)} %pad_maximum_fusion.13), channel_id=1, source_target_pairs={{0,4},{4,0},{8,12},{12,8},{16,20},{20,16},{24,28},{28,24},{1,5},{5... | collective-permute-start | bytes 2985992 | tf_op jit(solution)/shard_map/ppermute | solution.py:94
  105.7 22.5 %collective-permute-start.20 = (bf16[2,216,384]{2,1,0:T(8,128)(2,1)S(1)}, bf16[2,216,384]{2,1,0:T(8,128)(2,1)S(1)}, u32[]{:S(2)}, u32[]{:S(2)}) collective-permute-start(bf16[2,216,384]{2,1,0:T(8,128)(2,1)S(1)} %copy-done.28), channel_id=1, source_target_pairs={{0,4},{4,0},{8,12},{12,8},{16,20},{20,16},{24,28},{28,24},{1,5},{5... | collective-permute-start | bytes 995336 | tf_op jit(solution)/shard_map/ppermute | solution.py:94
  129.6 9.8 %collective-permute-start.22 = (bf16[8,2,216,384]{3,2,1,0:T(8,128)(2,1)S(1)}, bf16[8,2,216,384]{3,2,1,0:T(8,128)(2,1)S(1)}, u32[]{:S(2)}, u32[]{:S(2)}) collective-permute-start(bf16[8,2,216,384]{3,2,1,0:T(8,128)(2,1)S(1)} %bitcast.516), channel_id=1, source_target_pairs={{0,1},{1,0},{2,3},{3,2},{4,5},{5,4},{6,7},{7,6},{8,9},{9,8},{10,11... | collective-permute-start | bytes 7962632 | tf_op jit(solution)/shard_map/ppermute | solution.py:98
  137.9 13.8 %collective-permute-start.16 = (bf16[320,768]{1,0:T(8,128)(2,1)S(1)}, bf16[320,768]{1,0:T(8,128)(2,1)}, u32[]{:S(2)}, u32[]{:S(2)}) collective-permute-start(bf16[320,768]{1,0:T(8,128)(2,1)S(1)} %add_convert_fusion.4.total_ref), channel_id=1, source_target_pairs={{0,2},{1,3},{2,0},{3,1},{4,6},{5,7},{6,4},{7,5},{8,10},{9,11},{10,... | collective-permute-start | bytes 1474568 | tf_op jit(solution)/shard_map/ppermute | solution.py:98
  171.5 34.9 %collective-permute-start.24 = (bf16[120,768]{1,0:T(8,128)(2,1)}, bf16[120,768]{1,0:T(8,128)(2,1)}, u32[]{:S(2)}, u32[]{:S(2)}) collective-permute-start(bf16[120,768]{1,0:T(8,128)(2,1)} %get-tuple-element.387), channel_id=1, source_target_pairs={{0,24},{4,28},{8,16},{12,20},{16,8},{20,12},{24,0},{28,4},{1,25},{... | collective-permute-start | bytes 552968 | tf_op jit(solution)/shard_map/ppermute | solution.py:94
  173.8 32.7 %collective-permute-start.25 = (bf16[120,768]{1,0:T(8,128)(2,1)}, bf16[120,768]{1,0:T(8,128)(2,1)}, u32[]{:S(2)}, u32[]{:S(2)}) collective-permute-start(bf16[120,768]{1,0:T(8,128)(2,1)} %get-tuple-element.386), channel_id=1, source_target_pairs={{0,16},{4,20},{8,24},{12,28},{16,0},{20,4},{24,8},{28,12},{1,17},{... | collective-permute-start | bytes 552968 | tf_op jit(solution)/shard_map/ppermute | solution.py:94
  179.0 27.4 %collective-permute-start.26 = (bf16[120,768]{1,0:T(8,128)(2,1)}, bf16[120,768]{1,0:T(8,128)(2,1)}, u32[]{:S(2)}, u32[]{:S(2)}) collective-permute-start(bf16[120,768]{1,0:T(8,128)(2,1)} %get-tuple-element.385), channel_id=1, source_target_pairs={{0,8},{4,12},{8,0},{12,4},{16,24},{20,28},{24,16},{28,20},{1,9},{5... | collective-permute-start | bytes 552968 | tf_op jit(solution)/shard_map/ppermute | solution.py:94
  254.2 32.5 %collective-permute-start.28 = (bf16[3,4,2,48,384]{4,3,1,0,2:T(8,128)(2,1)}, bf16[3,4,2,48,384]{4,3,1,0,2:T(8,128)(2,1)S(1)}, u32[]{:S(2)}, u32[]{:S(2)}) collective-permute-start(bf16[3,4,2,48,384]{4,3,1,0,2:T(8,128)(2,1)} %fusion.29), channel_id=1, source_target_pairs={{0,2},{1,3},{2,0},{3,1},{4,6},{5,7},{6,4},{7,5},{8,10},{9,11},{10,... | collective-permute-start | bytes 2654216 | tf_op jit(solution)/shard_map/ppermute | solution.py:98
  307.7 21.6 %collective-permute-start.48 = (bf16[3,4,48,384]{3,2,1,0:T(8,128)(2,1)}, bf16[3,4,48,384]{3,2,1,0:T(8,128)(2,1)S(1)}, u32[]{:S(2)}, u32[]{:S(2)}) collective-permute-start(bf16[3,4,48,384]{3,2,1,0:T(8,128)(2,1)} %fusion.32), channel_id=1, source_target_pairs={{0,4},{4,0},{8,12},{12,8},{16,20},{20,16},{24,28},{28,24},{1,5},{5... | collective-permute-start | bytes 1327112 | tf_op jit(solution)/shard_map/ppermute | solution.py:94
  322.2 7.3 %collective-permute-start.32 = (bf16[320,768]{1,0:T(8,128)(2,1)}, bf16[320,768]{1,0:T(8,128)(2,1)}, u32[]{:S(2)}, u32[]{:S(2)}) collective-permute-start(bf16[320,768]{1,0:T(8,128)(2,1)} %get-tuple-element.193), channel_id=1, source_target_pairs={{0,1},{1,0},{2,3},{3,2},{4,5},{5,4},{6,7},{7,6},{8,9},{9,8},{10,11... | collective-permute-start | bytes 1474568 | tf_op jit(solution)/shard_map/ppermute | solution.py:98
  331.5 13.6 %collective-permute-start.33 = (bf16[320,768]{1,0:T(8,128)(2,1)S(1)}, bf16[320,768]{1,0:T(8,128)(2,1)S(1)}, u32[]{:S(2)}, u32[]{:S(2)}) collective-permute-start(bf16[320,768]{1,0:T(8,128)(2,1)S(1)} %add_convert_fusion.3.total_ref), channel_id=1, source_target_pairs={{0,2},{1,3},{2,0},{3,1},{4,6},{5,7},{6,4},{7,5},{8,10},{9,11},{10,... | collective-permute-start | bytes 1474568 | tf_op jit(solution)/shard_map/ppermute | solution.py:98
  333.1 29.6 %collective-permute-start.42 = (bf16[1,4,2,2,48,384]{5,4,1,2,3,0:T(8,128)(2,1)}, bf16[1,4,2,2,48,384]{5,4,1,2,3,0:T(8,128)(2,1)S(1)}, u32[]{:S(2)}, u32[]{:S(2)}) collective-permute-start(bf16[1,4,2,2,48,384]{5,4,1,2,3,0:T(8,128)(2,1)} %dynamic-slice_bitcast_fusion.6), channel_id=1, source_target_pairs={{0,1},{1,0},{2,3},{3,2},{4,5},{5,4},{6,7},{7,6},{8,9},{9,8},{10,11... | collective-permute-start | bytes 1769480 | tf_op jit(solution)/shard_map/ppermute | solution.py:98
  334.0 29.5 %collective-permute-start.47 = (bf16[4,96,768]{2,1,0:T(8,128)(2,1)}, bf16[4,96,768]{2,1,0:T(8,128)(2,1)}, u32[]{:S(2)}, u32[]{:S(2)}) collective-permute-start(bf16[4,96,768]{2,1,0:T(8,128)(2,1)} %dynamic-slice_bitcast_fusion.4), channel_id=1, source_target_pairs={{0,4},{4,0},{8,12},{12,8},{16,20},{20,16},{24,28},{28,24},{1,5},{5... | collective-permute-start | bytes 1769480 | tf_op jit(solution)/shard_map/ppermute | solution.py:94
  336.4 28.8 %collective-permute-start.46 = (bf16[4,96,768]{2,1,0:T(8,128)(2,1)}, bf16[4,96,768]{2,1,0:T(8,128)(2,1)}, u32[]{:S(2)}, u32[]{:S(2)}) collective-permute-start(bf16[4,96,768]{2,1,0:T(8,128)(2,1)} %dynamic-slice_bitcast_fusion.5), channel_id=1, source_target_pairs={{0,4},{4,0},{8,12},{12,8},{16,20},{20,16},{24,28},{28,24},{1,5},{5... | collective-permute-start | bytes 1769480 | tf_op jit(solution)/shard_map/ppermute | solution.py:94
  357.3 17.7 %collective-permute-start.41 = (bf16[4,84,768]{2,0,1:T(4,128)(2,1)}, bf16[4,84,768]{2,0,1:T(4,128)(2,1)}, u32[]{:S(2)}, u32[]{:S(2)}) collective-permute-start(bf16[4,84,768]{2,0,1:T(4,128)(2,1)} %copy.167), channel_id=1, source_target_pairs={{0,4},{4,0},{8,12},{12,8},{16,20},{20,16},{24,28},{28,24},{1,5},{5... | collective-permute-start | bytes 1548296 | tf_op jit(solution)/shard_map/ppermute | solution.py:94
  358.8 14.3 %collective-permute-start.34 = (bf16[320,768]{1,0:T(8,128)(2,1)}, bf16[320,768]{1,0:T(8,128)(2,1)}, u32[]{:S(2)}, u32[]{:S(2)}) collective-permute-start(bf16[320,768]{1,0:T(8,128)(2,1)} %get-tuple-element.198), channel_id=1, source_target_pairs={{0,1},{1,0},{2,3},{3,2},{4,5},{5,4},{6,7},{7,6},{8,9},{9,8},{10,11... | collective-permute-start | bytes 1474568 | tf_op jit(solution)/shard_map/ppermute | solution.py:98
  362.9 9.5 %collective-permute-start.43 = (bf16[1,4,2,48,384]{4,3,1,2,0:T(8,128)(2,1)S(1)}, bf16[1,4,2,48,384]{4,3,1,2,0:T(8,128)(2,1)S(1)}, u32[]{:S(2)}, u32[]{:S(2)}) collective-permute-start(bf16[1,4,2,48,384]{4,3,1,2,0:T(8,128)(2,1)S(1)} %fusion.37), channel_id=1, source_target_pairs={{0,2},{1,3},{2,0},{3,1},{4,6},{5,7},{6,4},{7,5},{8,10},{9,11},{10,... | collective-permute-start | bytes 884744 | tf_op jit(solution)/shard_map/ppermute | solution.py:98
  372.5 5.6 collective-permute-start.44
  374.4 12.7 %collective-permute-start.35 = (bf16[320,768]{1,0:T(8,128)(2,1)S(1)}, bf16[320,768]{1,0:T(8,128)(2,1)S(1)}, u32[]{:S(2)}, u32[]{:S(2)}) collective-permute-start(bf16[320,768]{1,0:T(8,128)(2,1)S(1)} %add_convert_fusion.2.total_ref), channel_id=1, source_target_pairs={{0,2},{1,3},{2,0},{3,1},{4,6},{5,7},{6,4},{7,5},{8,10},{9,11},{10,... | collective-permute-start | bytes 1474568 | tf_op jit(solution)/shard_map/ppermute | solution.py:98
  388.3 50.8 %collective-permute-start.49 = (bf16[4,120,768]{2,1,0:T(8,128)(2,1)}, bf16[4,120,768]{2,1,0:T(8,128)(2,1)}, u32[]{:S(2)}, u32[]{:S(2)}) collective-permute-start(bf16[4,120,768]{2,1,0:T(8,128)(2,1)} %get-tuple-element.306), channel_id=1, source_target_pairs={{8,0},{12,4},{16,24},{20,28},{9,1},{13,5},{17,25},{21,29},{10,2},{... | collective-permute-start | bytes 2211848 | tf_op jit(solution)/shard_map/ppermute | solution.py:202
  389.6 49.5 %collective-permute-start.50 = (bf16[4,120,768]{2,1,0:T(8,128)(2,1)S(1)}, bf16[4,120,768]{2,1,0:T(8,128)(2,1)}, u32[]{:S(2)}, u32[]{:S(2)}) collective-permute-start(bf16[4,120,768]{2,1,0:T(8,128)(2,1)S(1)} %get-tuple-element.307), channel_id=1, source_target_pairs={{8,24},{12,28},{16,0},{20,4},{9,25},{13,29},{17,1},{21,5},{10,26},... | collective-permute-start | bytes 2211848 | tf_op jit(solution)/shard_map/ppermute | solution.py:202
  392.0 47.2 %collective-permute-start.51 = (bf16[4,120,768]{2,1,0:T(8,128)(2,1)}, bf16[4,120,768]{2,1,0:T(8,128)(2,1)}, u32[]{:S(2)}, u32[]{:S(2)}) collective-permute-start(bf16[4,120,768]{2,1,0:T(8,128)(2,1)} %broadcast_select_fusion), channel_id=1, source_target_pairs={{0,24},{4,28},{24,0},{28,4},{1,25},{5,29},{25,1},{29,5},{2,26},{6,... | collective-permute-start | bytes 2211848 | tf_op jit(solution)/shard_map/ppermute | solution.py:202
  403.6 12.1 %collective-permute-start.45 = (bf16[4,84,768]{2,0,1:T(4,128)(2,1)S(1)}, bf16[4,84,768]{2,0,1:T(4,128)(2,1)S(1)}, u32[]{:S(2)}, u32[]{:S(2)}) collective-permute-start(bf16[4,84,768]{2,0,1:T(4,128)(2,1)S(1)} %copy.176), channel_id=1, source_target_pairs={{0,4},{4,0},{8,12},{12,8},{16,20},{20,16},{24,28},{28,24},{1,5},{5... | collective-permute-start | bytes 1548296 | tf_op jit(solution)/shard_map/ppermute | solution.py:94
  407.3 45.3 %collective-permute-start.36 = (f32[1,19201]{1,0:T(1,128)S(1)}, f32[1,19201]{1,0:T(1,128)S(1)}, u32[]{:S(2)}, u32[]{:S(2)}) collective-permute-start(f32[1,19201]{1,0:T(1,128)S(1)} %reshape.1556), channel_id=1, source_target_pairs={{0,1},{1,0},{2,3},{3,2},{4,5},{5,4},{6,7},{7,6},{8,9},{9,8},{10,11... | collective-permute-start | bytes 230420 | tf_op jit(solution)/shard_map/ppermute | solution.py:98
  443.6 19.3 %collective-permute-start.52 = (bf16[4,108,768]{2,0,1:T(4,128)(2,1)}, bf16[4,108,768]{2,0,1:T(4,128)(2,1)}, u32[]{:S(2)}, u32[]{:S(2)}) collective-permute-start(bf16[4,108,768]{2,0,1:T(4,128)(2,1)} %copy.180), channel_id=1, source_target_pairs={{0,8},{4,12},{24,16},{28,20},{1,9},{5,13},{25,17},{29,21},{2,10},{... | collective-permute-start | bytes 1990664 | tf_op jit(solution)/shard_map/ppermute | solution.py:202
  447.1 25.5 %collective-permute-start.53 = (bf16[4,108,768]{2,0,1:T(4,128)(2,1)}, bf16[4,108,768]{2,0,1:T(4,128)(2,1)}, u32[]{:S(2)}, u32[]{:S(2)}) collective-permute-start(bf16[4,108,768]{2,0,1:T(4,128)(2,1)} %copy.182), channel_id=1, source_target_pairs={{0,16},{4,20},{24,8},{28,12},{1,17},{5,21},{25,9},{29,13},{2,18},{... | collective-permute-start | bytes 1990664 | tf_op jit(solution)/shard_map/ppermute | solution.py:202
  450.6 22.0 %collective-permute-start.54 = (bf16[4,108,768]{2,0,1:T(4,128)(2,1)}, bf16[4,108,768]{2,0,1:T(4,128)(2,1)}, u32[]{:S(2)}, u32[]{:S(2)}) collective-permute-start(bf16[4,108,768]{2,0,1:T(4,128)(2,1)} %copy.184), channel_id=1, source_target_pairs={{8,16},{12,20},{16,8},{20,12},{9,17},{13,21},{17,9},{21,13},{10,18... | collective-permute-start | bytes 1990664 | tf_op jit(solution)/shard_map/ppermute | solution.py:202
  461.8 18.6 %collective-permute-start.39 = (f32[1,19201]{1,0:T(1,128)S(1)}, f32[1,19201]{1,0:T(1,128)S(1)}, u32[]{:S(2)}, u32[]{:S(2)}) collective-permute-start(f32[1,19201]{1,0:T(1,128)S(1)} %add.548), channel_id=1, source_target_pairs={{0,8},{4,12},{8,0},{12,4},{16,24},{20,28},{24,16},{28,20},{1,9},{5... | collective-permute-start | bytes 230420 | tf_op jit(solution)/shard_map/ppermute | solution.py:94
  477.8 10.4 %collective-permute-start.55 = (f32[8,128]{1,0:T(8,128)S(1)}, f32[8,128]{1,0:T(8,128)S(1)}, u32[]{:S(2)}, u32[]{:S(2)}) collective-permute-start(f32[8,128]{1,0:T(8,128)S(1)} %broadcast_in_dim.25), channel_id=1, source_target_pairs={{0,3},{1,2},{2,1},{3,0},{4,7},{5,6},{6,5},{7,4},{8,11},{9,10},{10,... | collective-permute-start | bytes 12296 | tf_op jit(solution)/shard_map/ppermute | solution.py:98
  477.9 10.3 %collective-permute-start.56 = (f32[8,128]{1,0:T(8,128)S(1)}, f32[8,128]{1,0:T(8,128)S(1)}, u32[]{:S(2)}, u32[]{:S(2)}) collective-permute-start(f32[8,128]{1,0:T(8,128)S(1)} %broadcast_in_dim.25), channel_id=1, source_target_pairs={{0,2},{1,3},{2,0},{3,1},{4,6},{5,7},{6,4},{7,5},{8,10},{9,11},{10,... | collective-permute-start | bytes 12296 | tf_op jit(solution)/shard_map/ppermute | solution.py:98
  478.5 9.7 %collective-permute-start.57 = (f32[8,128]{1,0:T(8,128)S(1)}, f32[8,128]{1,0:T(8,128)S(1)}, u32[]{:S(2)}, u32[]{:S(2)}) collective-permute-start(f32[8,128]{1,0:T(8,128)S(1)} %broadcast_in_dim.25), channel_id=1, source_target_pairs={{0,1},{1,0},{2,3},{3,2},{4,5},{5,4},{6,7},{7,6},{8,9},{9,8},{10,11... | collective-permute-start | bytes 12296 | tf_op jit(solution)/shard_map/ppermute | solution.py:98
  480.5 11.8 %collective-permute-start.40 = (f32[1,19201]{1,0:T(1,128)S(1)}, f32[1,19201]{1,0:T(1,128)S(1)}, u32[]{:S(2)}, u32[]{:S(2)}) collective-permute-start(f32[1,19201]{1,0:T(1,128)S(1)} %add.549), channel_id=1, source_target_pairs={{0,16},{4,20},{8,24},{12,28},{16,0},{20,4},{24,8},{28,12},{1,17},{... | collective-permute-start | bytes 230420 | tf_op jit(solution)/shard_map/ppermute | solution.py:94
  492.4 5.5 collective-permute-start.59
  500.9 9.9 %collective-permute-start.67 = (bf16[120,768]{1,0:T(8,128)(2,1)S(1)}, bf16[120,768]{1,0:T(8,128)(2,1)S(1)}, u32[]{:S(2)}, u32[]{:S(2)}) collective-permute-start(bf16[120,768]{1,0:T(8,128)(2,1)S(1)} %get-tuple-element.384), channel_id=1, source_target_pairs={{0,24},{4,28},{8,16},{12,20},{16,8},{20,12},{24,0},{28,4},{1,25},{... | collective-permute-start | bytes 552968 | tf_op jit(solution)/shard_map/ppermute | solution.py:94
  503.3 14.0 %collective-permute-start.68 = (bf16[120,768]{1,0:T(8,128)(2,1)S(1)}, bf16[120,768]{1,0:T(8,128)(2,1)S(1)}, u32[]{:S(2)}, u32[]{:S(2)}) collective-permute-start(bf16[120,768]{1,0:T(8,128)(2,1)S(1)} %get-tuple-element.383), channel_id=1, source_target_pairs={{0,16},{4,20},{8,24},{12,28},{16,0},{20,4},{24,8},{28,12},{1,17},{... | collective-permute-start | bytes 552968 | tf_op jit(solution)/shard_map/ppermute | solution.py:94
  504.4 12.9 %collective-permute-start.69 = (bf16[120,768]{1,0:T(8,128)(2,1)S(1)}, bf16[120,768]{1,0:T(8,128)(2,1)S(1)}, u32[]{:S(2)}, u32[]{:S(2)}) collective-permute-start(bf16[120,768]{1,0:T(8,128)(2,1)S(1)} %get-tuple-element.382), channel_id=1, source_target_pairs={{0,8},{4,12},{8,0},{12,4},{16,24},{20,28},{24,16},{28,20},{1,9},{5... | collective-permute-start | bytes 552968 | tf_op jit(solution)/shard_map/ppermute | solution.py:94
  510.1 14.1 %collective-permute-start.62 = (f32[1920,128]{1,0:T(8,128)}, f32[1920,128]{1,0:T(8,128)S(1)}, u32[]{:S(2)}, u32[]{:S(2)}) collective-permute-start(f32[1920,128]{1,0:T(8,128)} %get-tuple-element.224), channel_id=1, source_target_pairs={{0,1},{1,0},{2,3},{3,2},{4,5},{5,4},{6,7},{7,6},{8,9},{9,8},{10,11... | collective-permute-start | bytes 2949128 | tf_op jit(solution)/shard_map/ppermute | solution.py:98
  520.4 21.0 %collective-permute-start.70 = (f32[60,768]{1,0:T(8,128)}, f32[60,768]{1,0:T(8,128)}, u32[]{:S(2)}, u32[]{:S(2)}) collective-permute-start(f32[60,768]{1,0:T(8,128)} %slice_bitcast_fusion.14), channel_id=1, source_target_pairs={{0,2},{1,3},{2,0},{3,1},{4,6},{5,7},{6,4},{7,5},{8,10},{9,11},{10,... | collective-permute-start | bytes 552968 | tf_op jit(solution)/shard_map/ppermute | solution.py:98
  525.3 12.4 %collective-permute-start.63 = (f32[960,128]{1,0:T(8,128)}, f32[960,128]{1,0:T(8,128)S(1)}, u32[]{:S(2)}, u32[]{:S(2)}) collective-permute-start(f32[960,128]{1,0:T(8,128)} %get-tuple-element.359), channel_id=1, source_target_pairs={{0,4},{4,0},{8,12},{12,8},{16,20},{20,16},{24,28},{28,24},{1,5},{5... | collective-permute-start | bytes 1474568 | tf_op jit(solution)/shard_map/ppermute | solution.py:94
  526.8 12.1 %collective-permute-start.65 = (f32[960,128]{1,0:T(8,128)}, f32[960,128]{1,0:T(8,128)S(1)}, u32[]{:S(2)}, u32[]{:S(2)}) collective-permute-start(f32[960,128]{1,0:T(8,128)} %get-tuple-element.360), channel_id=1, source_target_pairs={{0,2},{1,3},{2,0},{3,1},{4,6},{5,7},{6,4},{7,5},{8,10},{9,11},{10,... | collective-permute-start | bytes 1474568 | tf_op jit(solution)/shard_map/ppermute | solution.py:98
  539.0 11.1 %collective-permute-start.64 = (f32[960,128]{1,0:T(8,128)S(1)}, f32[960,128]{1,0:T(8,128)S(1)}, u32[]{:S(2)}, u32[]{:S(2)}) collective-permute-start(f32[960,128]{1,0:T(8,128)S(1)} %get-tuple-element.357), channel_id=1, source_target_pairs={{0,2},{1,3},{2,0},{3,1},{4,6},{5,7},{6,4},{7,5},{8,10},{9,11},{10,... | collective-permute-start | bytes 1474568 | tf_op jit(solution)/shard_map/ppermute | solution.py:98
  540.3 10.7 %collective-permute-start.66 = (f32[960,128]{1,0:T(8,128)S(1)}, f32[960,128]{1,0:T(8,128)S(1)}, u32[]{:S(2)}, u32[]{:S(2)}) collective-permute-start(f32[960,128]{1,0:T(8,128)S(1)} %get-tuple-element.358), channel_id=1, source_target_pairs={{0,4},{4,0},{8,12},{12,8},{16,20},{20,16},{24,28},{28,24},{1,5},{5... | collective-permute-start | bytes 1474568 | tf_op jit(solution)/shard_map/ppermute | solution.py:94
  542.5 9.5 %collective-permute-start.71 = (f32[2,60,768]{2,1,0:T(8,128)S(1)}, f32[2,60,768]{2,1,0:T(8,128)S(1)}, u32[]{:S(2)}, u32[]{:S(2)}) collective-permute-start(f32[2,60,768]{2,1,0:T(8,128)S(1)} %pad_maximum_fusion.38), channel_id=1, source_target_pairs={{0,1},{1,0},{2,3},{3,2},{4,5},{5,4},{6,7},{7,6},{8,9},{9,8},{10,11... | collective-permute-start | bytes 1105928 | tf_op jit(solution)/shard_map/ppermute | solution.py:98
  551.2 6.3 collective-permute-start.72
  612.9 9.5 %collective-permute-start.73 = (bf16[120,768]{1,0:T(8,128)(2,1)S(1)}, bf16[120,768]{1,0:T(8,128)(2,1)S(1)}, u32[]{:S(2)}, u32[]{:S(2)}) collective-permute-start(bf16[120,768]{1,0:T(8,128)(2,1)S(1)} %get-tuple-element.381), channel_id=1, source_target_pairs={{0,24},{4,28},{8,16},{12,20},{16,8},{20,12},{24,0},{28,4},{1,25},{... | collective-permute-start | bytes 552968 | tf_op jit(solution)/shard_map/ppermute | solution.py:94
  613.0 16.6 %collective-permute-start.74 = (bf16[120,768]{1,0:T(8,128)(2,1)S(1)}, bf16[120,768]{1,0:T(8,128)(2,1)S(1)}, u32[]{:S(2)}, u32[]{:S(2)}) collective-permute-start(bf16[120,768]{1,0:T(8,128)(2,1)S(1)} %get-tuple-element.380), channel_id=1, source_target_pairs={{0,16},{4,20},{8,24},{12,28},{16,0},{20,4},{24,8},{28,12},{1,17},{... | collective-permute-start | bytes 552968 | tf_op jit(solution)/shard_map/ppermute | solution.py:94
  613.1 16.5 %collective-permute-start.75 = (bf16[120,768]{1,0:T(8,128)(2,1)S(1)}, bf16[120,768]{1,0:T(8,128)(2,1)S(1)}, u32[]{:S(2)}, u32[]{:S(2)}) collective-permute-start(bf16[120,768]{1,0:T(8,128)(2,1)S(1)} %get-tuple-element.379), channel_id=1, source_target_pairs={{0,8},{4,12},{8,0},{12,4},{16,24},{20,28},{24,16},{28,20},{1,9},{5... | collective-permute-start | bytes 552968 | tf_op jit(solution)/shard_map/ppermute | solution.py:94
  (130 other events, 854.4 us)

commit v2 on v1

--- a/solution.py
+++ b/solution.py
@@ -44,7 +44,7 @@
 BLOCKS = 3
 PAIRS = [(i, j) for i in range(BLOCKS) for j in range(i, BLOCKS)]
 VMEM_LIMIT = 56 * 2**20
-COST = pl.CostEstimate(flops=1000, bytes_accessed=1000, transcendentals=0)
+COST = pl.CostEstimate(flops=2000000000, bytes_accessed=1000, transcendentals=0)
 
 BLOCK = ("ln1_g", "ln1_b", "q_b", "v_b", "out_b", "ln2_g", "ln2_b", "up_b", "down_b")
 
@@ -1000,7 +1000,7 @@
     )
 
     parts = narrow_parts(part)
-    full_d = narrow_pair(assemble(tied(pieces_d, parts[0])), 1, 2)
+    full_d = narrow_pair(assemble(tied(pieces_d, parts[1])), 1, 2)
     at, taken = 0, []
     for extent in (m_up, m_qkv, m_out, m_up, m_head, m_link):
         taken.append(full_d[:, :, :, at : at + extent].reshape(wide * QN * extent, DD))
@@ -1130,6 +1130,8 @@
         [latent_low, enc_result, vec_row, link_w, w_down, w_up, upper, active, hid2],
         8 * rows * D * units,
     )
+    parts = narrow_parts(part)
+    g_link, sums, _ = lax.optimization_barrier((g_link, sums, parts[1]))
     grads["in_b"] = sums[0, :DD]
     for row, name in enumerate(("elnf_g", "elnf_b", "edown_b", "eup_b")):
         grads[name] = sums[row + 1]
@@ -1137,10 +1139,8 @@
     def enc_parts(value, extent):
         return low(value).reshape(4, fast, extent, D).transpose(1, 0, 2, 3)
 
-    parts = narrow_parts(part)
     g_up, g_down, late, _ = lax.optimization_barrier((g_up, g_down, late, parts[0]))
     late = half_sum(late, half, 4, 1)
-    late = half_sum(after(late, parts[1]), clip, 3, 2)
     sum_up = fast_scatter(enc_parts(g_up, n_up), 0)
     sum_down = fast_scatter(enc_parts(g_down, n_up), 0)
     mid_grad, g_out, g_qkv, part, sums, _ = call(
@@ -1153,7 +1153,6 @@
         grads[name] = sums[row]
     grads["eq_b"], grads["ev_b"] = sums[3, : D // QN], sums[4, : D // QN]
     parts = narrow_parts(part)
-    sum_up, sum_down, _ = lax.optimization_barrier((sum_up, sum_down, parts[1]))
     ends_sum = ends_total(joined(sum_up, early[0]), joined(sum_down, early[2]), slow, (0, 3))
     g_embed, sums = call(
         enc_start_back_kernel,
@@ -1172,8 +1171,7 @@
     longer = max(part_qkv.shape[2], part_rest.shape[2])
     sum_qkv = fast_scatter(pad_rows(part_qkv, longer, 2), 0)
     sum_rest = fast_scatter(pad_rows(part_rest, longer, 2), 0)
-    late = fast_scatter(late, 2)
-    sum_rest, ends_sum = lax.optimization_barrier((sum_rest, ends_sum))
+    late = fast_scatter(half_sum(after(late, parts[1]), clip, 3, 2), 2)
     middle_sum = ends_total(joined(sum_qkv, late[0]), joined(sum_rest, early[1]), slow, (1, 2))
     enc_ends, dec_ends = parted(ends_sum, n_up)
     enc_middle, dec_middle = parted(middle_sum, longer)

time: 644 us -> 594 us (0.922)
  waiting for transfers between devices: 174 us -> 150 us
  local copies, waits for them, and re-layouts: 75.5 us -> 55.9 us
  other arithmetic: 92.9 us -> 82.3 us
    ppermute x6, waiting for transfers between devices: 33.1 us -> 15 us  [ends_total(): total = total + lax.ppermute(sent, WD, pairs).astype(F32)]
    ppermute x31, waiting for transfers between devices: 52.5 us -> 45.3 us  [narrow_flip(): return lax.ppermute(value, NR, [(src, src ^ bit) for src in range(QN)])]
    unnamed x260 -> x210, local copies, waits for them, and re-layouts: 14.8 us -> 12.2 us
  transfers between devices with their start and end apart: 76 -> 76, of which waited for: 32 -> 32; matrix products, arithmetic and copies ran while one was open for 19% -> 17% of each run, Pallas kernels for 14% -> 15%
where the time goes in v2:
time: 594 us; the launch traced here: 583 us
  Pallas kernels  161 us (27%)
  waiting for transfers between devices  150 us (25%)
  starting transfers between devices  92.6 us (16%)
  other arithmetic  82.3 us (14%)
  local copies, waits for them, and re-layouts  55.9 us (9%)
  matrix products  34.4 us (6%)
  between operations  7.19 us (1%)
    ppermute x39, waiting for transfers between devices, wide_flip(): return lax.ppermute(value, WD, [(src, src ^ bit) for src in range(count)])  89.6 us
    ppermute x39, starting transfers between devices, wide_flip(): return lax.ppermute(value, WD, [(src, src ^ bit) for src in range(count)])  61.9 us
    pallas_call x1, Pallas kernels, orthogonal(): pl.pallas_call(functools.partial(ortho_kernel, periods), in_specs=[pl.Blo...  52.2 us
    pallas_call x7, Pallas kernels, call(): pl.pallas_call(kernel, in_specs=[pl.BlockSpec(memory_space=pltpu.SMEM)] *...  49.9 us
    ppermute x31, waiting for transfers between devices, narrow_flip(): return lax.ppermute(value, NR, [(src, src ^ bit) for src in range(QN)])  45.3 us
    pallas_call x1, Pallas kernels, attention_bwd(): pl.pallas_call(functools.partial(attn_bwd_kernel, tile), grid=(pairs,), i...  31 us
    pallas_call x1, Pallas kernels, attention_fwd(): pl.pallas_call(functools.partial(attn_fwd_kernel, tile), grid=(pairs,), i...  23.1 us
    ppermute x31, starting transfers between devices, narrow_flip(): return lax.ppermute(value, NR, [(src, src ^ bit) for src in range(QN)])  16.9 us
  transfers between devices with their start and end apart: 76, of which 32 were waited for; matrix products, arithmetic and copies ran while one was open for 17% of the time, Pallas kernels for 15%

profile of v2, /device:TPU:0, one launch (start us, length us, event | category | flops | bytes accessed | tf_op | source)
XLA Modules:
  0.0 583.3 jit_solution(2768879373235263461)
XLA Ops:
  4.6 5.0 collective-permute-start
  16.5 5.4 fusion.12.pix_ref
  24.4 4.3 collective-permute-done.2
  30.5 3.0 collective-permute-start.11
  36.6 8.2 %collective-permute-done.3 = bf16[3,144,768]{2,1,0:T(8,128)(2,1)S(1)} collective-permute-done((bf16[3,144,768]{2,1,0:T(8,128)(2,1)S(1)}, bf16[3,144,768]{2,1,0:T(8,128)(2,1)S(1)}, u32[]{:S(2)}, u32[]{:S(2)}) %collective-permute-start.3) | collective-permute-done | bytes 663584 | tf_op jit(solution)/shard_map/ppermute | solution.py:94
  51.4 3.0 collective-permute-done.11
  55.6 2.2 pad_maximum_fusion.17
  62.2 4.8 collective-permute-start.17
  71.9 5.0 shard_map.535
  76.8 3.6 collective-permute-done.13
  86.9 5.9 %collective-permute-done.18 = bf16[2,216,384]{2,1,0:T(8,128)(2,1)S(1)} collective-permute-done((bf16[2,216,384]{2,1,0:T(8,128)(2,1)S(1)}, bf16[2,216,384]{2,1,0:T(8,128)(2,1)S(1)}, u32[]{:S(2)}, u32[]{:S(2)}) %collective-permute-start.18) | collective-permute-done | bytes 331808 | tf_op jit(solution)/shard_map/ppermute | solution.py:94
  92.8 3.7 collective-permute-done.9.more_ref
  98.6 5.0 shard_map.536
  103.6 2.1 collective-permute-done.15
  109.4 13.3 %collective-permute-done.21 = bf16[3,2,216,384]{3,2,1,0:T(8,128)(2,1)S(1)} collective-permute-done((bf16[3,2,216,384]{3,2,1,0:T(8,128)(2,1)}, bf16[3,2,216,384]{3,2,1,0:T(8,128)(2,1)S(1)}, u32[]{:S(2)}, u32[]{:S(2)}) %collective-permute-start.21) | collective-permute-done | bytes 995360 | tf_op jit(solution)/shard_map/ppermute | solution.py:94
  122.9 5.0 collective-permute-done.20
  131.0 2.9 multiply_sine_fusion
  139.9 2.1 reshape.1548.w_ref
  142.0 8.7 %shard_map.537 = (f32[320,768]{1,0:T(8,128)}, f32[784,384]{1,0:T(8,128)}, bf16[784,384]{1,0:T(8,128)(2,1)}, bf16[784,384]{1,0:T(8,128)(2,1)}, bf16[2,784,384]{2,1,0:T(8,128)(2,1)}) custom-call(s32[2]{0:T(128)} %pad_add_fusion.where_ref, f32[320,768]{1,0:T(8,128)} %get-tuple-element.146.middle_ref, bf16[320,768]{1,0:T(8,128)(2,1)} %copy-done.38, ...), custom_call_target="tpu_custom_call" | custom-call | flops 2000000000 | bytes 1000 | tf_op jit(solution)/shard_map/pallas_call | solution.py:608
  151.0 4.3 multiply_reduce_fusion.3
  155.6 3.5 pad_maximum_fusion.7
  159.1 2.5 reshape_reshape.3
  166.3 1.8 collective-permute-start.24
  168.2 3.4 collective-permute-start.25
  171.6 23.1 %shard_map.538 = (bf16[784,384]{1,0:T(8,128)(2,1)}, f32[784,384]{1,0:T(8,128)}, f32[3,2,784]{2,1,0:T(2,128)}) custom-call(bf16[784,384]{1,0:T(8,128)(2,1)} %get-tuple-element.163.q_ref, bf16[2,1568,384]{2,1,0:T(8,128)(2,1)} %bitcast.519), custom_call_target="tpu_custom_call" | custom-call | flops 2000000000 | bytes 1000 | tf_op jit(solution)/shard_map/pallas_call | solution.py:384
  202.0 4.8 multiply_reduce_fusion
  209.0 2.8 convolution_convert_fusion
  211.8 4.1 convert_reduce_fusion
  215.9 3.0 convolution_convert_fusion.2
  218.8 2.1 multiply_reduce_fusion.6
  229.6 2.8 convolution_convert_fusion.3.g_ref
  233.6 1.9 convert_add_fusion
  237.1 31.0 %shard_map.539 = (bf16[784,384]{1,0:T(8,128)(2,1)}, bf16[2,1568,384]{2,1,0:T(8,128)(2,1)}) custom-call(bf16[784,384]{1,0:T(8,128)(2,1)} %get-tuple-element.163.q_ref, bf16[2,1568,384]{2,1,0:T(8,128)(2,1)} %bitcast.520, bf16[784,384]{1,0:T(8,128)(2,1)} %convolution_convert_fusion.3.g_ref, f32[784,384]{1,0:T(8,128)} %get-tuple-element.179.of_ref, ...), custom_call_target="tpu_custom_call" | custom-call | flops 2000000000 | bytes 1000 | tf_op jit(solution)/shard_map/pallas_call | solution.py:426
  271.1 2.9 collective-permute-done.29.got_ref
  275.0 10.0 %shard_map.540 = (bf16[1152,384]{1,0:T(8,128)(2,1)}, f32[160,384]{1,0:T(8,128)}, f32[8,384]{1,0:T(8,128)}, f32[784,384]{1,0:T(8,128)}) custom-call(s32[2]{0:T(128)} %pad_add_fusion.where_ref, bf16[784,384]{1,0:T(8,128)(2,1)} %get-tuple-element.181.gq_ref, bf16[2,784,384]{2,1,0:T(8,128)(2,1)} %get-tuple-element.311.gkv_ref, bf16[2,784,384]{2,1,0:T(8,128)(2,1)} %copy-done.86, ...), custom_call_target="tpu_custom_call" | custom-call | flops 2000000000 | bytes 1000 | tf_op jit(solution)/shard_map/pallas_call | solution.py:608
  285.2 2.3 reshape.1557
  290.0 4.5 collective-permute-done.31
  295.3 7.7 %shard_map.541 = (bf16[768,384]{1,0:T(8,128)(2,1)}, f32[320,768]{1,0:T(8,128)}, bf16[768,768]{1,0:T(8,128)(2,1)}, bf16[768,768]{1,0:T(8,128)(2,1)}, bf16[320,768]{1,0:T(8,128)(2,1)}, /*index=5*/f32[8,768]{1,0:T(8,128)}) custom-call(bf16[320,384]{1,0:T(8,128)(2,1)} %bitcast.570, f32[320,768]{1,0:T(8,128)} %get-tuple-element.187.result_ref, ...), custom_call_target="tpu_custom_call" | custom-call | flops 2000000000 | bytes 1000 | tf_op jit(solution)/shard_map/pallas_call | solution.py:608
  303.2 1.8 collective-permute-done.32
  310.4 8.1 %collective-permute-done.33.more_ref = bf16[320,768]{1,0:T(8,128)(2,1)S(1)} collective-permute-done((bf16[320,768]{1,0:T(8,128)(2,1)S(1)}, bf16[320,768]{1,0:T(8,128)(2,1)S(1)}, u32[]{:S(2)}, u32[]{:S(2)}) %collective-permute-start.33) | collective-permute-done | bytes 491552 | tf_op jit(solution)/shard_map/ppermute | solution.py:98
  319.3 7.9 %shard_map.542 = (f32[320,768]{1,0:T(8,128)}, bf16[192,768]{1,0:T(8,128)(2,1)}, bf16[3,192,768]{2,1,0:T(8,128)(2,1)}, bf16[320,768]{1,0:T(8,128)(2,1)}, f32[8,768]{1,0:T(8,128)}, /*index=5*/bf16[3,320,192]{2,1,0:T(8,128)(2,1)}) custom-call(bf16[320,768]{1,0:T(8,128)(2,1)} %copy-done.40, bf16[320,768]{1,0:T(8,128)(2,1)} %copy-done.87, ...), custom_call_target="tpu_custom_call" | custom-call | flops 2000000000 | bytes 1000 | tf_op jit(solution)/shard_map/pallas_call | solution.py:608
  331.0 2.1 reshape.1561
  345.1 4.7 collective-permute-start.54
  354.1 10.4 %collective-permute-done.35.more_ref = bf16[320,768]{1,0:T(8,128)(2,1)S(1)} collective-permute-done((bf16[320,768]{1,0:T(8,128)(2,1)S(1)}, bf16[320,768]{1,0:T(8,128)(2,1)S(1)}, u32[]{:S(2)}, u32[]{:S(2)}) %collective-permute-start.35) | collective-permute-done | bytes 491552 | tf_op jit(solution)/shard_map/ppermute | solution.py:98
  365.3 5.6 shard_map.543
  376.8 12.1 %collective-permute-done.44 = bf16[1,4,48,384]{3,2,1,0:T(8,128)(2,1)S(1)} collective-permute-done((bf16[1,4,48,384]{3,2,1,0:T(8,128)(2,1)S(1)}, bf16[1,4,48,384]{3,2,1,0:T(8,128)(2,1)S(1)}, u32[]{:S(2)}, u32[]{:S(2)}) %collective-permute-start.44) | collective-permute-done | bytes 147488 | tf_op jit(solution)/shard_map/ppermute | solution.py:94
  389.7 3.5 collective-permute-start.47
  394.2 2.4 collective-permute-start.48
  398.3 1.9 convert_add_fusion.1
  403.4 3.1 collective-permute-done.38
  408.4 14.3 %collective-permute-done.48 = bf16[4,108,768]{2,0,1:T(4,128)(2,1)S(1)} collective-permute-done((bf16[4,108,768]{2,0,1:T(4,128)(2,1)S(1)}, bf16[4,108,768]{2,0,1:T(4,128)(2,1)S(1)}, u32[]{:S(2)}, u32[]{:S(2)}) %collective-permute-start.48) | collective-permute-done | bytes 663584 | tf_op jit(solution)/shard_map/ppermute | solution.py:202
  428.9 6.5 %collective-permute-start.40 = (f32[1,19201]{1,0:T(1,128)S(1)}, f32[1,19201]{1,0:T(1,128)S(1)}, u32[]{:S(2)}, u32[]{:S(2)}) collective-permute-start(f32[1,19201]{1,0:T(1,128)S(1)} %add.549), channel_id=1, source_target_pairs={{0,16},{4,20},{8,24},{12,28},{16,0},{20,4},{24,8},{28,12},{1,17},{... | collective-permute-start | bytes 230420 | tf_op jit(solution)/shard_map/ppermute | solution.py:94
  437.4 2.2 collective-permute-done.40
  441.5 2.7 collective-permute-start.61
  448.1 2.4 collective-permute-start.67
  452.6 4.8 shard_map.544
  458.1 6.5 %collective-permute-done.68 = bf16[120,768]{1,0:T(8,128)(2,1)S(1)} collective-permute-done((bf16[120,768]{1,0:T(8,128)(2,1)S(1)}, bf16[120,768]{1,0:T(8,128)(2,1)S(1)}, u32[]{:S(2)}, u32[]{:S(2)}) %collective-permute-start.68) | collective-permute-done | bytes 184352 | tf_op jit(solution)/shard_map/ppermute | solution.py:94
  475.9 9.3 %collective-permute-done.63 = f32[960,128]{1,0:T(8,128)S(1)} collective-permute-done((f32[960,128]{1,0:T(8,128)}, f32[960,128]{1,0:T(8,128)S(1)}, u32[]{:S(2)}, u32[]{:S(2)}) %collective-permute-start.63) | collective-permute-done | bytes 491552 | tf_op jit(solution)/shard_map/ppermute | solution.py:94
  490.9 7.4 %collective-permute-done.64 = f32[960,128]{1,0:T(8,128)S(1)} collective-permute-done((f32[960,128]{1,0:T(8,128)S(1)}, f32[960,128]{1,0:T(8,128)S(1)}, u32[]{:S(2)}, u32[]{:S(2)}) %collective-permute-start.64) | collective-permute-done | bytes 491552 | tf_op jit(solution)/shard_map/ppermute | solution.py:98
  501.0 1.9 multiply_subtract_fusion.2
  504.3 52.2 %shard_map.545 = (bf16[384,768]{1,0:T(8,128)(2,1)}, bf16[192,384]{1,0:T(8,128)(2,1)}) custom-call(s32[3]{0:T(128)} %pad_add_fusion.1.counts_ref, f32[1]{0:T(128)} %bitcast.155.factor_ref, f32[1920,128]{1,0:T(8,128)} %copy-done.31, f32[1920,128]{1,0:T(8,128)} %collective-permute-done.72.other_ref, f32[384,768]{1,0:T(8,128)} %bitcast.515, ...), custom_call_target="tpu_custom_call" | custom-call | flops 2000000000 | bytes 1000 | tf_op jit(solution)/shard_map/pallas_call | solution.py:594
  559.5 3.6 collective-permute-start.75
  563.7 4.5 collective-permute-done.73
  568.2 7.2 %collective-permute-done.74 = bf16[120,768]{1,0:T(8,128)(2,1)S(1)} collective-permute-done((bf16[120,768]{1,0:T(8,128)(2,1)S(1)}, bf16[120,768]{1,0:T(8,128)(2,1)S(1)}, u32[]{:S(2)}, u32[]{:S(2)}) %collective-permute-start.74) | collective-permute-done | bytes 184352 | tf_op jit(solution)/shard_map/ppermute | solution.py:94
  (601 shorter events, 175.7 us)
Async XLA Ops:
  4.6 19.8 %collective-permute-start = (bf16[144,768]{1,0:T(8,128)(2,1)}, bf16[144,768]{1,0:T(8,128)(2,1)S(1)}, u32[]{:S(2)}, u32[]{:S(2)}) collective-permute-start(bf16[144,768]{1,0:T(8,128)(2,1)} %pad_maximum_fusion.42), channel_id=1, source_target_pairs={{0,24},{4,28},{8,16},{12,20},{16,8},{20,12},{24,0},{28,4},{1,25},{... | collective-permute-start | bytes 663560 | tf_op jit(solution)/shard_map/ppermute | solution.py:94
  9.7 14.7 %collective-permute-start.1 = (bf16[144,768]{1,0:T(8,128)(2,1)}, bf16[144,768]{1,0:T(8,128)(2,1)S(1)}, u32[]{:S(2)}, u32[]{:S(2)}) collective-permute-start(bf16[144,768]{1,0:T(8,128)(2,1)} %pad_maximum_fusion.42), channel_id=1, source_target_pairs={{0,8},{4,12},{8,0},{12,4},{16,24},{20,28},{24,16},{28,20},{1,9},{5... | collective-permute-start | bytes 663560 | tf_op jit(solution)/shard_map/ppermute | solution.py:94
  9.7 19.0 %collective-permute-start.2 = (bf16[144,768]{1,0:T(8,128)(2,1)}, bf16[144,768]{1,0:T(8,128)(2,1)S(1)}, u32[]{:S(2)}, u32[]{:S(2)}) collective-permute-start(bf16[144,768]{1,0:T(8,128)(2,1)} %pad_maximum_fusion.42), channel_id=1, source_target_pairs={{0,16},{4,20},{8,24},{12,28},{16,0},{20,4},{24,8},{28,12},{1,17},{... | collective-permute-start | bytes 663560 | tf_op jit(solution)/shard_map/ppermute | solution.py:94
  10.2 25.3 %collective-permute-start.4 = (bf16[144,768]{1,0:T(8,128)(2,1)}, bf16[144,768]{1,0:T(8,128)(2,1)}, u32[]{:S(2)}, u32[]{:S(2)}) collective-permute-start(bf16[144,768]{1,0:T(8,128)(2,1)} %pad_maximum_fusion.42), channel_id=1, source_target_pairs={{0,4},{4,0},{8,12},{12,8},{16,20},{20,16},{24,28},{28,24},{1,5},{5... | collective-permute-start | bytes 663560 | tf_op jit(solution)/shard_map/ppermute | solution.py:94
  14.0 16.3 %collective-permute-start.7 = (bf16[216,384]{1,0:T(8,128)(2,1)S(1)}, bf16[216,384]{1,0:T(8,128)(2,1)S(1)}, u32[]{:S(2)}, u32[]{:S(2)}) collective-permute-start(bf16[216,384]{1,0:T(8,128)(2,1)S(1)} %concatenate.364), channel_id=1, source_target_pairs={{0,2},{1,3},{2,0},{3,1},{4,6},{5,7},{6,4},{7,5},{8,10},{9,11},{10,... | collective-permute-start | bytes 497672 | tf_op jit(solution)/shard_map/ppermute | solution.py:98
  28.8 16.0 %collective-permute-start.3 = (bf16[3,144,768]{2,1,0:T(8,128)(2,1)S(1)}, bf16[3,144,768]{2,1,0:T(8,128)(2,1)S(1)}, u32[]{:S(2)}, u32[]{:S(2)}) collective-permute-start(bf16[3,144,768]{2,1,0:T(8,128)(2,1)S(1)} %pad_maximum_fusion.22), channel_id=1, source_target_pairs={{0,4},{4,0},{8,12},{12,8},{16,20},{20,16},{24,28},{28,24},{1,5},{5... | collective-permute-start | bytes 1990664 | tf_op jit(solution)/shard_map/ppermute | solution.py:94
  30.4 21.0 %collective-permute-start.10 = (bf16[192,768]{1,0:T(8,128)(2,1)}, bf16[192,768]{1,0:T(8,128)(2,1)}, u32[]{:S(2)}, u32[]{:S(2)}) collective-permute-start(bf16[192,768]{1,0:T(8,128)(2,1)} %pad_maximum_fusion.40), channel_id=1, source_target_pairs={{0,8},{4,12},{8,0},{12,4},{16,24},{20,28},{24,16},{28,20},{1,9},{5... | collective-permute-start | bytes 884744 | tf_op jit(solution)/shard_map/ppermute | solution.py:94
  30.5 23.9 %collective-permute-start.11 = (bf16[192,768]{1,0:T(8,128)(2,1)}, bf16[192,768]{1,0:T(8,128)(2,1)}, u32[]{:S(2)}, u32[]{:S(2)}) collective-permute-start(bf16[192,768]{1,0:T(8,128)(2,1)} %pad_maximum_fusion.40), channel_id=1, source_target_pairs={{0,16},{4,20},{8,24},{12,28},{16,0},{20,4},{24,8},{28,12},{1,17},{... | collective-permute-start | bytes 884744 | tf_op jit(solution)/shard_map/ppermute | solution.py:94
  33.5 20.9 %collective-permute-start.12 = (bf16[192,768]{1,0:T(8,128)(2,1)}, bf16[192,768]{1,0:T(8,128)(2,1)}, u32[]{:S(2)}, u32[]{:S(2)}) collective-permute-start(bf16[192,768]{1,0:T(8,128)(2,1)} %pad_maximum_fusion.40), channel_id=1, source_target_pairs={{0,24},{4,28},{8,16},{12,20},{16,8},{20,12},{24,0},{28,4},{1,25},{... | collective-permute-start | bytes 884744 | tf_op jit(solution)/shard_map/ppermute | solution.py:94
  48.1 7.3 %collective-permute-start.5 = (f32[320,192]{0,1:T(8,128)S(1)}, f32[320,192]{0,1:T(8,128)S(1)}, u32[]{:S(2)}, u32[]{:S(2)}) collective-permute-start(f32[320,192]{0,1:T(8,128)S(1)} %fusion.117), channel_id=1, source_target_pairs={{0,2},{1,3},{2,0},{3,1},{4,6},{5,7},{6,4},{7,5},{8,10},{9,11},{10,... | collective-permute-start | bytes 737288 | tf_op jit(solution)/shard_map/ppermute | solution.py:98
  54.4 7.7 %collective-permute-start.14 = (bf16[192,768]{1,0:T(8,128)(2,1)}, bf16[192,768]{1,0:T(8,128)(2,1)S(1)}, u32[]{:S(2)}, u32[]{:S(2)}) collective-permute-start(bf16[192,768]{1,0:T(8,128)(2,1)} %pad_maximum_fusion.40), channel_id=1, source_target_pairs={{0,4},{4,0},{8,12},{12,8},{16,20},{20,16},{24,28},{28,24},{1,5},{5... | collective-permute-start | bytes 884744 | tf_op jit(solution)/shard_map/ppermute | solution.py:94
  55.5 14.8 %collective-permute-start.6 = (f32[320,2,192]{0,2,1:T(8,128)S(1)}, f32[320,2,192]{0,2,1:T(8,128)S(1)}, u32[]{:S(2)}, u32[]{:S(2)}) collective-permute-start(f32[320,2,192]{0,2,1:T(8,128)S(1)} %pad_maximum_fusion.28), channel_id=1, source_target_pairs={{0,1},{1,0},{2,3},{3,2},{4,5},{5,4},{6,7},{7,6},{8,9},{9,8},{10,11... | collective-permute-start | bytes 1474568 | tf_op jit(solution)/shard_map/ppermute | solution.py:98
  57.8 22.7 %collective-permute-start.13 = (bf16[3,192,768]{2,1,0:T(8,128)(2,1)}, bf16[3,192,768]{2,1,0:T(8,128)(2,1)}, u32[]{:S(2)}, u32[]{:S(2)}) collective-permute-start(bf16[3,192,768]{2,1,0:T(8,128)(2,1)} %pad_maximum_fusion.17), channel_id=1, source_target_pairs={{0,4},{4,0},{8,12},{12,8},{16,20},{20,16},{24,28},{28,24},{1,5},{5... | collective-permute-start | bytes 2654216 | tf_op jit(solution)/shard_map/ppermute | solution.py:94
  62.2 24.7 %collective-permute-start.17 = (bf16[2,216,384]{2,1,0:T(8,128)(2,1)S(1)}, bf16[2,216,384]{2,1,0:T(8,128)(2,1)S(1)}, u32[]{:S(2)}, u32[]{:S(2)}) collective-permute-start(bf16[2,216,384]{2,1,0:T(8,128)(2,1)S(1)} %pad_maximum_fusion.39), channel_id=1, source_target_pairs={{0,8},{4,12},{8,0},{12,4},{16,24},{20,28},{24,16},{28,20},{1,9},{5... | collective-permute-start | bytes 995336 | tf_op jit(solution)/shard_map/ppermute | solution.py:94
  66.9 25.9 %collective-permute-start.18 = (bf16[2,216,384]{2,1,0:T(8,128)(2,1)S(1)}, bf16[2,216,384]{2,1,0:T(8,128)(2,1)S(1)}, u32[]{:S(2)}, u32[]{:S(2)}) collective-permute-start(bf16[2,216,384]{2,1,0:T(8,128)(2,1)S(1)} %pad_maximum_fusion.39), channel_id=1, source_target_pairs={{0,16},{4,20},{8,24},{12,28},{16,0},{20,4},{24,8},{28,12},{1,17},{... | collective-permute-start | bytes 995336 | tf_op jit(solution)/shard_map/ppermute | solution.py:94
  67.5 25.2 %collective-permute-start.19 = (bf16[2,216,384]{2,1,0:T(8,128)(2,1)S(1)}, bf16[2,216,384]{2,1,0:T(8,128)(2,1)S(1)}, u32[]{:S(2)}, u32[]{:S(2)}) collective-permute-start(bf16[2,216,384]{2,1,0:T(8,128)(2,1)S(1)} %pad_maximum_fusion.39), channel_id=1, source_target_pairs={{0,24},{4,28},{8,16},{12,20},{16,8},{20,12},{24,0},{28,4},{1,25},{... | collective-permute-start | bytes 995336 | tf_op jit(solution)/shard_map/ppermute | solution.py:94
  76.8 5.6 collective-permute-start.8
  83.4 13.1 %collective-permute-start.9 = (bf16[320,768]{1,0:T(8,128)(2,1)S(1)}, bf16[320,768]{1,0:T(8,128)(2,1)S(1)}, u32[]{:S(2)}, u32[]{:S(2)}) collective-permute-start(bf16[320,768]{1,0:T(8,128)(2,1)S(1)} %add_convert_fusion.5.total_ref), channel_id=1, source_target_pairs={{0,2},{1,3},{2,0},{3,1},{4,6},{5,7},{6,4},{7,5},{8,10},{9,11},{10,... | collective-permute-start | bytes 1474568 | tf_op jit(solution)/shard_map/ppermute | solution.py:98
  97.6 25.2 %collective-permute-start.21 = (bf16[3,2,216,384]{3,2,1,0:T(8,128)(2,1)}, bf16[3,2,216,384]{3,2,1,0:T(8,128)(2,1)S(1)}, u32[]{:S(2)}, u32[]{:S(2)}) collective-permute-start(bf16[3,2,216,384]{3,2,1,0:T(8,128)(2,1)} %pad_maximum_fusion.13), channel_id=1, source_target_pairs={{0,4},{4,0},{8,12},{12,8},{16,20},{20,16},{24,28},{28,24},{1,5},{5... | collective-permute-start | bytes 2985992 | tf_op jit(solution)/shard_map/ppermute | solution.py:94
  106.9 21.0 %collective-permute-start.16 = (bf16[320,768]{1,0:T(8,128)(2,1)S(1)}, bf16[320,768]{1,0:T(8,128)(2,1)}, u32[]{:S(2)}, u32[]{:S(2)}) collective-permute-start(bf16[320,768]{1,0:T(8,128)(2,1)S(1)} %add_convert_fusion.4.total_ref), channel_id=1, source_target_pairs={{0,2},{1,3},{2,0},{3,1},{4,6},{5,7},{6,4},{7,5},{8,10},{9,11},{10,... | collective-permute-start | bytes 1474568 | tf_op jit(solution)/shard_map/ppermute | solution.py:98
  108.4 19.5 %collective-permute-start.20 = (bf16[2,216,384]{2,1,0:T(8,128)(2,1)S(1)}, bf16[2,216,384]{2,1,0:T(8,128)(2,1)S(1)}, u32[]{:S(2)}, u32[]{:S(2)}) collective-permute-start(bf16[2,216,384]{2,1,0:T(8,128)(2,1)S(1)} %pad_maximum_fusion.39), channel_id=1, source_target_pairs={{0,4},{4,0},{8,12},{12,8},{16,20},{20,16},{24,28},{28,24},{1,5},{5... | collective-permute-start | bytes 995336 | tf_op jit(solution)/shard_map/ppermute | solution.py:94
  129.3 7.1 %collective-permute-start.22 = (bf16[8,2,216,384]{3,2,1,0:T(8,128)(2,1)S(1)}, bf16[8,2,216,384]{3,2,1,0:T(8,128)(2,1)S(1)}, u32[]{:S(2)}, u32[]{:S(2)}) collective-permute-start(bf16[8,2,216,384]{3,2,1,0:T(8,128)(2,1)S(1)} %bitcast.508), channel_id=1, source_target_pairs={{0,1},{1,0},{2,3},{3,2},{4,5},{5,4},{6,7},{7,6},{8,9},{9,8},{10,11... | collective-permute-start | bytes 7962632 | tf_op jit(solution)/shard_map/ppermute | solution.py:98
  150.8 10.8 %collective-permute-start.23 = (bf16[2,784,384]{2,1,0:T(8,128)(2,1)}, bf16[2,784,384]{2,1,0:T(8,128)(2,1)}, u32[]{:S(2)}, u32[]{:S(2)}) collective-permute-start(bf16[2,784,384]{2,1,0:T(8,128)(2,1)} %get-tuple-element.164), channel_id=1, source_target_pairs={{0,1},{1,0},{2,3},{3,2},{4,5},{5,4},{6,7},{7,6},{8,9},{9,8},{10,11... | collective-permute-start | bytes 3612680 | tf_op jit(solution)/shard_map/ppermute | solution.py:98
  166.3 28.3 %collective-permute-start.24 = (bf16[120,768]{1,0:T(8,128)(2,1)S(1)}, bf16[120,768]{1,0:T(8,128)(2,1)S(1)}, u32[]{:S(2)}, u32[]{:S(2)}) collective-permute-start(bf16[120,768]{1,0:T(8,128)(2,1)S(1)} %get-tuple-element.383), channel_id=1, source_target_pairs={{0,24},{4,28},{8,16},{12,20},{16,8},{20,12},{24,0},{28,4},{1,25},{... | collective-permute-start | bytes 552968 | tf_op jit(solution)/shard_map/ppermute | solution.py:94
  168.2 26.5 %collective-permute-start.25 = (bf16[120,768]{1,0:T(8,128)(2,1)S(1)}, bf16[120,768]{1,0:T(8,128)(2,1)S(1)}, u32[]{:S(2)}, u32[]{:S(2)}) collective-permute-start(bf16[120,768]{1,0:T(8,128)(2,1)S(1)} %get-tuple-element.382), channel_id=1, source_target_pairs={{0,16},{4,20},{8,24},{12,28},{16,0},{20,4},{24,8},{28,12},{1,17},{... | collective-permute-start | bytes 552968 | tf_op jit(solution)/shard_map/ppermute | solution.py:94
  171.5 23.1 %collective-permute-start.26 = (bf16[120,768]{1,0:T(8,128)(2,1)S(1)}, bf16[120,768]{1,0:T(8,128)(2,1)S(1)}, u32[]{:S(2)}, u32[]{:S(2)}) collective-permute-start(bf16[120,768]{1,0:T(8,128)(2,1)S(1)} %get-tuple-element.381), channel_id=1, source_target_pairs={{0,8},{4,12},{8,0},{12,4},{16,24},{20,28},{24,16},{28,20},{1,9},{5... | collective-permute-start | bytes 552968 | tf_op jit(solution)/shard_map/ppermute | solution.py:94
  235.6 32.5 %collective-permute-start.28 = (bf16[3,4,2,48,384]{4,3,1,0,2:T(8,128)(2,1)S(1)}, bf16[3,4,2,48,384]{4,3,1,0,2:T(8,128)(2,1)S(1)}, u32[]{:S(2)}, u32[]{:S(2)}) collective-permute-start(bf16[3,4,2,48,384]{4,3,1,0,2:T(8,128)(2,1)S(1)} %fusion.28), channel_id=1, source_target_pairs={{0,2},{1,3},{2,0},{3,1},{4,6},{5,7},{6,4},{7,5},{8,10},{9,11},{10,... | collective-permute-start | bytes 2654216 | tf_op jit(solution)/shard_map/ppermute | solution.py:98
  287.6 15.4 %collective-permute-start.46 = (bf16[3,4,48,384]{3,2,1,0:T(8,128)(2,1)S(1)}, bf16[3,4,48,384]{3,2,1,0:T(8,128)(2,1)S(1)}, u32[]{:S(2)}, u32[]{:S(2)}) collective-permute-start(bf16[3,4,48,384]{3,2,1,0:T(8,128)(2,1)S(1)} %fusion.31), channel_id=1, source_target_pairs={{0,4},{4,0},{8,12},{12,8},{16,20},{20,16},{24,28},{28,24},{1,5},{5... | collective-permute-start | bytes 1327112 | tf_op jit(solution)/shard_map/ppermute | solution.py:94
  305.1 13.3 %collective-permute-start.33 = (bf16[320,768]{1,0:T(8,128)(2,1)S(1)}, bf16[320,768]{1,0:T(8,128)(2,1)S(1)}, u32[]{:S(2)}, u32[]{:S(2)}) collective-permute-start(bf16[320,768]{1,0:T(8,128)(2,1)S(1)} %add_convert_fusion.3.total_ref), channel_id=1, source_target_pairs={{0,2},{1,3},{2,0},{3,1},{4,6},{5,7},{6,4},{7,5},{8,10},{9,11},{10,... | collective-permute-start | bytes 1474568 | tf_op jit(solution)/shard_map/ppermute | solution.py:98
  306.7 44.5 %collective-permute-start.42 = (bf16[1,4,2,2,48,384]{5,4,1,2,3,0:T(8,128)(2,1)}, bf16[1,4,2,2,48,384]{5,4,1,2,3,0:T(8,128)(2,1)}, u32[]{:S(2)}, u32[]{:S(2)}) collective-permute-start(bf16[1,4,2,2,48,384]{5,4,1,2,3,0:T(8,128)(2,1)} %dynamic-slice_bitcast_fusion.6), channel_id=1, source_target_pairs={{0,1},{1,0},{2,3},{3,2},{4,5},{5,4},{6,7},{7,6},{8,9},{9,8},{10,11... | collective-permute-start | bytes 1769480 | tf_op jit(solution)/shard_map/ppermute | solution.py:98
  307.5 29.9 %collective-permute-start.51 = (bf16[4,96,768]{2,1,0:T(8,128)(2,1)}, bf16[4,96,768]{2,1,0:T(8,128)(2,1)}, u32[]{:S(2)}, u32[]{:S(2)}) collective-permute-start(bf16[4,96,768]{2,1,0:T(8,128)(2,1)} %dynamic-slice_bitcast_fusion.4), channel_id=1, source_target_pairs={{0,4},{4,0},{8,12},{12,8},{16,20},{20,16},{24,28},{28,24},{1,5},{5... | collective-permute-start | bytes 1769480 | tf_op jit(solution)/shard_map/ppermute | solution.py:94
  309.0 29.8 %collective-permute-start.50 = (bf16[4,96,768]{2,1,0:T(8,128)(2,1)}, bf16[4,96,768]{2,1,0:T(8,128)(2,1)}, u32[]{:S(2)}, u32[]{:S(2)}) collective-permute-start(bf16[4,96,768]{2,1,0:T(8,128)(2,1)} %dynamic-slice_bitcast_fusion.5), channel_id=1, source_target_pairs={{0,4},{4,0},{8,12},{12,8},{16,20},{20,16},{24,28},{28,24},{1,5},{5... | collective-permute-start | bytes 1769480 | tf_op jit(solution)/shard_map/ppermute | solution.py:94
  329.6 23.4 %collective-permute-start.41 = (bf16[4,84,768]{2,0,1:T(4,128)(2,1)}, bf16[4,84,768]{2,0,1:T(4,128)(2,1)}, u32[]{:S(2)}, u32[]{:S(2)}) collective-permute-start(bf16[4,84,768]{2,0,1:T(4,128)(2,1)} %copy.167), channel_id=1, source_target_pairs={{0,4},{4,0},{8,12},{12,8},{16,20},{20,16},{24,28},{28,24},{1,5},{5... | collective-permute-start | bytes 1548296 | tf_op jit(solution)/shard_map/ppermute | solution.py:94
  330.2 14.9 %collective-permute-start.34 = (bf16[320,768]{1,0:T(8,128)(2,1)}, bf16[320,768]{1,0:T(8,128)(2,1)}, u32[]{:S(2)}, u32[]{:S(2)}) collective-permute-start(bf16[320,768]{1,0:T(8,128)(2,1)} %get-tuple-element.196), channel_id=1, source_target_pairs={{0,1},{1,0},{2,3},{3,2},{4,5},{5,4},{6,7},{7,6},{8,9},{9,8},{10,11... | collective-permute-start | bytes 1474568 | tf_op jit(solution)/shard_map/ppermute | solution.py:98
  341.5 52.7 %collective-permute-start.52 = (bf16[4,120,768]{2,1,0:T(8,128)(2,1)}, bf16[4,120,768]{2,1,0:T(8,128)(2,1)}, u32[]{:S(2)}, u32[]{:S(2)}) collective-permute-start(bf16[4,120,768]{2,1,0:T(8,128)(2,1)} %get-tuple-element.302), channel_id=1, source_target_pairs={{8,0},{12,4},{16,24},{20,28},{9,1},{13,5},{17,25},{21,29},{10,2},{... | collective-permute-start | bytes 2211848 | tf_op jit(solution)/shard_map/ppermute | solution.py:202
  342.8 54.6 %collective-permute-start.53 = (bf16[4,120,768]{2,1,0:T(8,128)(2,1)}, bf16[4,120,768]{2,1,0:T(8,128)(2,1)}, u32[]{:S(2)}, u32[]{:S(2)}) collective-permute-start(bf16[4,120,768]{2,1,0:T(8,128)(2,1)} %get-tuple-element.303), channel_id=1, source_target_pairs={{8,24},{12,28},{16,0},{20,4},{9,25},{13,29},{17,1},{21,5},{10,26},... | collective-permute-start | bytes 2211848 | tf_op jit(solution)/shard_map/ppermute | solution.py:202
  345.1 53.1 %collective-permute-start.54 = (bf16[4,120,768]{2,1,0:T(8,128)(2,1)}, bf16[4,120,768]{2,1,0:T(8,128)(2,1)}, u32[]{:S(2)}, u32[]{:S(2)}) collective-permute-start(bf16[4,120,768]{2,1,0:T(8,128)(2,1)} %broadcast_select_fusion), channel_id=1, source_target_pairs={{0,24},{4,28},{24,0},{28,4},{1,25},{5,29},{25,1},{29,5},{2,26},{6,... | collective-permute-start | bytes 2211848 | tf_op jit(solution)/shard_map/ppermute | solution.py:202
  351.1 13.4 %collective-permute-start.35 = (bf16[320,768]{1,0:T(8,128)(2,1)S(1)}, bf16[320,768]{1,0:T(8,128)(2,1)S(1)}, u32[]{:S(2)}, u32[]{:S(2)}) collective-permute-start(bf16[320,768]{1,0:T(8,128)(2,1)S(1)} %add_convert_fusion.2.total_ref), channel_id=1, source_target_pairs={{0,2},{1,3},{2,0},{3,1},{4,6},{5,7},{6,4},{7,5},{8,10},{9,11},{10,... | collective-permute-start | bytes 1474568 | tf_op jit(solution)/shard_map/ppermute | solution.py:98
  364.6 10.5 %collective-permute-start.43 = (bf16[1,4,2,48,384]{4,3,1,2,0:T(8,128)(2,1)S(1)}, bf16[1,4,2,48,384]{4,3,1,2,0:T(8,128)(2,1)S(1)}, u32[]{:S(2)}, u32[]{:S(2)}) collective-permute-start(bf16[1,4,2,48,384]{4,3,1,2,0:T(8,128)(2,1)S(1)} %fusion.36), channel_id=1, source_target_pairs={{0,2},{1,3},{2,0},{3,1},{4,6},{5,7},{6,4},{7,5},{8,10},{9,11},{10,... | collective-permute-start | bytes 884744 | tf_op jit(solution)/shard_map/ppermute | solution.py:98
  372.5 16.5 %collective-permute-start.45 = (bf16[4,84,768]{2,0,1:T(4,128)(2,1)S(1)}, bf16[4,84,768]{2,0,1:T(4,128)(2,1)S(1)}, u32[]{:S(2)}, u32[]{:S(2)}) collective-permute-start(bf16[4,84,768]{2,0,1:T(4,128)(2,1)S(1)} %copy.176), channel_id=1, source_target_pairs={{0,4},{4,0},{8,12},{12,8},{16,20},{20,16},{24,28},{28,24},{1,5},{5... | collective-permute-start | bytes 1548296 | tf_op jit(solution)/shard_map/ppermute | solution.py:94
  375.3 13.7 %collective-permute-start.44 = (bf16[1,4,48,384]{3,2,1,0:T(8,128)(2,1)S(1)}, bf16[1,4,48,384]{3,2,1,0:T(8,128)(2,1)S(1)}, u32[]{:S(2)}, u32[]{:S(2)}) collective-permute-start(bf16[1,4,48,384]{3,2,1,0:T(8,128)(2,1)S(1)} %fusion.57), channel_id=1, source_target_pairs={{0,4},{4,0},{8,12},{12,8},{16,20},{20,16},{24,28},{28,24},{1,5},{5... | collective-permute-start | bytes 442376 | tf_op jit(solution)/shard_map/ppermute | solution.py:94
  388.9 7.7 %collective-permute-start.36 = (f32[1,19201]{1,0:T(1,128)S(1)}, f32[1,19201]{1,0:T(1,128)S(1)}, u32[]{:S(2)}, u32[]{:S(2)}) collective-permute-start(f32[1,19201]{1,0:T(1,128)S(1)} %reshape.1556), channel_id=1, source_target_pairs={{0,1},{1,0},{2,3},{3,2},{4,5},{5,4},{6,7},{7,6},{8,9},{9,8},{10,11... | collective-permute-start | bytes 230420 | tf_op jit(solution)/shard_map/ppermute | solution.py:98
  389.7 18.7 %collective-permute-start.47 = (bf16[4,108,768]{2,0,1:T(4,128)(2,1)S(1)}, bf16[4,108,768]{2,0,1:T(4,128)(2,1)S(1)}, u32[]{:S(2)}, u32[]{:S(2)}) collective-permute-start(bf16[4,108,768]{2,0,1:T(4,128)(2,1)S(1)} %copy.178), channel_id=1, source_target_pairs={{0,8},{4,12},{24,16},{28,20},{1,9},{5,13},{25,17},{29,21},{2,10},{... | collective-permute-start | bytes 1990664 | tf_op jit(solution)/shard_map/ppermute | solution.py:202
  394.2 28.5 %collective-permute-start.48 = (bf16[4,108,768]{2,0,1:T(4,128)(2,1)S(1)}, bf16[4,108,768]{2,0,1:T(4,128)(2,1)S(1)}, u32[]{:S(2)}, u32[]{:S(2)}) collective-permute-start(bf16[4,108,768]{2,0,1:T(4,128)(2,1)S(1)} %copy.180), channel_id=1, source_target_pairs={{0,16},{4,20},{24,8},{28,12},{1,17},{5,21},{25,9},{29,13},{2,18},{... | collective-permute-start | bytes 1990664 | tf_op jit(solution)/shard_map/ppermute | solution.py:202
  396.6 26.1 %collective-permute-start.49 = (bf16[4,108,768]{2,0,1:T(4,128)(2,1)S(1)}, bf16[4,108,768]{2,0,1:T(4,128)(2,1)S(1)}, u32[]{:S(2)}, u32[]{:S(2)}) collective-permute-start(bf16[4,108,768]{2,0,1:T(4,128)(2,1)S(1)} %copy.182), channel_id=1, source_target_pairs={{8,16},{12,20},{16,8},{20,12},{9,17},{13,21},{17,9},{21,13},{10,18... | collective-permute-start | bytes 1990664 | tf_op jit(solution)/shard_map/ppermute | solution.py:202
  406.5 22.3 %collective-permute-start.39 = (f32[1,19201]{1,0:T(1,128)S(1)}, f32[1,19201]{1,0:T(1,128)S(1)}, u32[]{:S(2)}, u32[]{:S(2)}) collective-permute-start(f32[1,19201]{1,0:T(1,128)S(1)} %add.548), channel_id=1, source_target_pairs={{0,8},{4,12},{8,0},{12,4},{16,24},{20,28},{24,16},{28,20},{1,9},{5... | collective-permute-start | bytes 230420 | tf_op jit(solution)/shard_map/ppermute | solution.py:94
  426.2 9.2 %collective-permute-start.55 = (f32[8,128]{1,0:T(8,128)S(1)}, f32[8,128]{1,0:T(8,128)S(1)}, u32[]{:S(2)}, u32[]{:S(2)}) collective-permute-start(f32[8,128]{1,0:T(8,128)S(1)} %broadcast_in_dim.25), channel_id=1, source_target_pairs={{0,3},{1,2},{2,1},{3,0},{4,7},{5,6},{6,5},{7,4},{8,11},{9,10},{10,... | collective-permute-start | bytes 12296 | tf_op jit(solution)/shard_map/ppermute | solution.py:98
  426.3 9.1 %collective-permute-start.56 = (f32[8,128]{1,0:T(8,128)S(1)}, f32[8,128]{1,0:T(8,128)S(1)}, u32[]{:S(2)}, u32[]{:S(2)}) collective-permute-start(f32[8,128]{1,0:T(8,128)S(1)} %broadcast_in_dim.25), channel_id=1, source_target_pairs={{0,2},{1,3},{2,0},{3,1},{4,6},{5,7},{6,4},{7,5},{8,10},{9,11},{10,... | collective-permute-start | bytes 12296 | tf_op jit(solution)/shard_map/ppermute | solution.py:98
  427.4 8.0 %collective-permute-start.57 = (f32[8,128]{1,0:T(8,128)S(1)}, f32[8,128]{1,0:T(8,128)S(1)}, u32[]{:S(2)}, u32[]{:S(2)}) collective-permute-start(f32[8,128]{1,0:T(8,128)S(1)} %broadcast_in_dim.25), channel_id=1, source_target_pairs={{0,1},{1,0},{2,3},{3,2},{4,5},{5,4},{6,7},{7,6},{8,9},{9,8},{10,11... | collective-permute-start | bytes 12296 | tf_op jit(solution)/shard_map/ppermute | solution.py:98
  428.9 10.7 %collective-permute-start.40 = (f32[1,19201]{1,0:T(1,128)S(1)}, f32[1,19201]{1,0:T(1,128)S(1)}, u32[]{:S(2)}, u32[]{:S(2)}) collective-permute-start(f32[1,19201]{1,0:T(1,128)S(1)} %add.549), channel_id=1, source_target_pairs={{0,16},{4,20},{8,24},{12,28},{16,0},{20,4},{24,8},{28,12},{1,17},{... | collective-permute-start | bytes 230420 | tf_op jit(solution)/shard_map/ppermute | solution.py:94
  439.7 5.5 collective-permute-start.59
  448.1 10.0 %collective-permute-start.67 = (bf16[120,768]{1,0:T(8,128)(2,1)S(1)}, bf16[120,768]{1,0:T(8,128)(2,1)S(1)}, u32[]{:S(2)}, u32[]{:S(2)}) collective-permute-start(bf16[120,768]{1,0:T(8,128)(2,1)S(1)} %get-tuple-element.380), channel_id=1, source_target_pairs={{0,24},{4,28},{8,16},{12,20},{16,8},{20,12},{24,0},{28,4},{1,25},{... | collective-permute-start | bytes 552968 | tf_op jit(solution)/shard_map/ppermute | solution.py:94
  450.6 14.0 %collective-permute-start.68 = (bf16[120,768]{1,0:T(8,128)(2,1)S(1)}, bf16[120,768]{1,0:T(8,128)(2,1)S(1)}, u32[]{:S(2)}, u32[]{:S(2)}) collective-permute-start(bf16[120,768]{1,0:T(8,128)(2,1)S(1)} %get-tuple-element.379), channel_id=1, source_target_pairs={{0,16},{4,20},{8,24},{12,28},{16,0},{20,4},{24,8},{28,12},{1,17},{... | collective-permute-start | bytes 552968 | tf_op jit(solution)/shard_map/ppermute | solution.py:94
  451.7 12.9 %collective-permute-start.69 = (bf16[120,768]{1,0:T(8,128)(2,1)S(1)}, bf16[120,768]{1,0:T(8,128)(2,1)S(1)}, u32[]{:S(2)}, u32[]{:S(2)}) collective-permute-start(bf16[120,768]{1,0:T(8,128)(2,1)S(1)} %get-tuple-element.378), channel_id=1, source_target_pairs={{0,8},{4,12},{8,0},{12,4},{16,24},{20,28},{24,16},{28,20},{1,9},{5... | collective-permute-start | bytes 552968 | tf_op jit(solution)/shard_map/ppermute | solution.py:94
  457.4 14.3 %collective-permute-start.62 = (f32[1920,128]{1,0:T(8,128)}, f32[1920,128]{1,0:T(8,128)S(1)}, u32[]{:S(2)}, u32[]{:S(2)}) collective-permute-start(f32[1920,128]{1,0:T(8,128)} %get-tuple-element.220), channel_id=1, source_target_pairs={{0,1},{1,0},{2,3},{3,2},{4,5},{5,4},{6,7},{7,6},{8,9},{9,8},{10,11... | collective-permute-start | bytes 2949128 | tf_op jit(solution)/shard_map/ppermute | solution.py:98
  467.7 22.2 %collective-permute-start.70 = (f32[60,768]{1,0:T(8,128)}, f32[60,768]{1,0:T(8,128)}, u32[]{:S(2)}, u32[]{:S(2)}) collective-permute-start(f32[60,768]{1,0:T(8,128)} %slice_bitcast_fusion.14), channel_id=1, source_target_pairs={{0,2},{1,3},{2,0},{3,1},{4,6},{5,7},{6,4},{7,5},{8,10},{9,11},{10,... | collective-permute-start | bytes 552968 | tf_op jit(solution)/shard_map/ppermute | solution.py:98
  472.9 12.3 %collective-permute-start.63 = (f32[960,128]{1,0:T(8,128)}, f32[960,128]{1,0:T(8,128)S(1)}, u32[]{:S(2)}, u32[]{:S(2)}) collective-permute-start(f32[960,128]{1,0:T(8,128)} %get-tuple-element.355), channel_id=1, source_target_pairs={{0,4},{4,0},{8,12},{12,8},{16,20},{20,16},{24,28},{28,24},{1,5},{5... | collective-permute-start | bytes 1474568 | tf_op jit(solution)/shard_map/ppermute | solution.py:94
  474.1 12.1 %collective-permute-start.65 = (f32[960,128]{1,0:T(8,128)}, f32[960,128]{1,0:T(8,128)}, u32[]{:S(2)}, u32[]{:S(2)}) collective-permute-start(f32[960,128]{1,0:T(8,128)} %get-tuple-element.356), channel_id=1, source_target_pairs={{0,2},{1,3},{2,0},{3,1},{4,6},{5,7},{6,4},{7,5},{8,10},{9,11},{10,... | collective-permute-start | bytes 1474568 | tf_op jit(solution)/shard_map/ppermute | solution.py:98
  487.4 10.9 %collective-permute-start.64 = (f32[960,128]{1,0:T(8,128)S(1)}, f32[960,128]{1,0:T(8,128)S(1)}, u32[]{:S(2)}, u32[]{:S(2)}) collective-permute-start(f32[960,128]{1,0:T(8,128)S(1)} %get-tuple-element.353), channel_id=1, source_target_pairs={{0,2},{1,3},{2,0},{3,1},{4,6},{5,7},{6,4},{7,5},{8,10},{9,11},{10,... | collective-permute-start | bytes 1474568 | tf_op jit(solution)/shard_map/ppermute | solution.py:98
  488.4 10.6 %collective-permute-start.66 = (f32[960,128]{1,0:T(8,128)S(1)}, f32[960,128]{1,0:T(8,128)S(1)}, u32[]{:S(2)}, u32[]{:S(2)}) collective-permute-start(f32[960,128]{1,0:T(8,128)S(1)} %get-tuple-element.354), channel_id=1, source_target_pairs={{0,4},{4,0},{8,12},{12,8},{16,20},{20,16},{24,28},{28,24},{1,5},{5... | collective-permute-start | bytes 1474568 | tf_op jit(solution)/shard_map/ppermute | solution.py:94
  490.8 9.1 %collective-permute-start.71 = (f32[2,60,768]{2,1,0:T(8,128)S(1)}, f32[2,60,768]{2,1,0:T(8,128)S(1)}, u32[]{:S(2)}, u32[]{:S(2)}) collective-permute-start(f32[2,60,768]{2,1,0:T(8,128)S(1)} %pad_maximum_fusion.38), channel_id=1, source_target_pairs={{0,1},{1,0},{2,3},{3,2},{4,5},{5,4},{6,7},{7,6},{8,9},{9,8},{10,11... | collective-permute-start | bytes 1105928 | tf_op jit(solution)/shard_map/ppermute | solution.py:98
  558.7 9.5 %collective-permute-start.73 = (bf16[120,768]{1,0:T(8,128)(2,1)S(1)}, bf16[120,768]{1,0:T(8,128)(2,1)S(1)}, u32[]{:S(2)}, u32[]{:S(2)}) collective-permute-start(bf16[120,768]{1,0:T(8,128)(2,1)S(1)} %get-tuple-element.377), channel_id=1, source_target_pairs={{0,24},{4,28},{8,16},{12,20},{16,8},{20,12},{24,0},{28,4},{1,25},{... | collective-permute-start | bytes 552968 | tf_op jit(solution)/shard_map/ppermute | solution.py:94
  559.5 15.8 %collective-permute-start.74 = (bf16[120,768]{1,0:T(8,128)(2,1)S(1)}, bf16[120,768]{1,0:T(8,128)(2,1)S(1)}, u32[]{:S(2)}, u32[]{:S(2)}) collective-permute-start(bf16[120,768]{1,0:T(8,128)(2,1)S(1)} %get-tuple-element.376), channel_id=1, source_target_pairs={{0,16},{4,20},{8,24},{12,28},{16,0},{20,4},{24,8},{28,12},{1,17},{... | collective-permute-start | bytes 552968 | tf_op jit(solution)/shard_map/ppermute | solution.py:94
  559.5 15.8 %collective-permute-start.75 = (bf16[120,768]{1,0:T(8,128)(2,1)S(1)}, bf16[120,768]{1,0:T(8,128)(2,1)S(1)}, u32[]{:S(2)}, u32[]{:S(2)}) collective-permute-start(bf16[120,768]{1,0:T(8,128)(2,1)S(1)} %get-tuple-element.375), channel_id=1, source_target_pairs={{0,8},{4,12},{8,0},{12,4},{16,24},{20,28},{24,16},{28,20},{1,9},{5... | collective-permute-start | bytes 552968 | tf_op jit(solution)/shard_map/ppermute | solution.py:94
  (105 other events, 529.8 us)

commit v3 on v2

--- a/solution.py
+++ b/solution.py
@@ -539,7 +539,7 @@
     periods, counts_ref, factor_ref, mine_ref, other_ref, big_grad, big_mom, small_grad, small_mom,
     big_out, small_out, packed_ref, *refs,
 ):
-    squares = [Square(refs[:5], BLOCKS), Square(refs[5:], 1)]
+    squares = [Square(refs[:5], BLOCKS), Square(refs[5:], BLOCKS)]
     cols = mine_ref.shape[1]
     first = counts_ref[2] == 0
     packed_ref[:, :cols] = jnp.where(first, mine_ref[...], other_ref[...])
@@ -1038,7 +1038,7 @@
         slow,
     )
 
-    tile = next(t for t in (224, 112, 16) if tubs % t == 0)
+    tile = next(t for t in (784, 224, 112, 16) if tubs % t == 0)
     dattn, mixed, dlog = attention_fwd(dq, all_kv, tile)
     dattn, enc_mom, dec_mom = lax.optimization_barrier((dattn, enc_mom, dec_mom))
 

time: 594 us -> 585 us (0.985)
  Pallas kernels: 161 us -> 152 us
  transfers between devices with their start and end apart: 76 -> 76, of which waited for: 32 -> 32; matrix products, arithmetic and copies ran while one was open for 17% -> 18% of each run, Pallas kernels for 15% -> 14%
where the time goes in v3:
time: 585 us; the launch traced here: 574 us
  Pallas kernels  152 us (26%)
  waiting for transfers between devices  150 us (26%)
  starting transfers between devices  92.1 us (16%)
  other arithmetic  82.3 us (14%)
  local copies, waits for them, and re-layouts  56.1 us (10%)
  matrix products  34.2 us (6%)
  between operations  7.15 us (1%)
    ppermute x39, waiting for transfers between devices, wide_flip(): return lax.ppermute(value, WD, [(src, src ^ bit) for src in range(count)])  89.5 us
    ppermute x39, starting transfers between devices, wide_flip(): return lax.ppermute(value, WD, [(src, src ^ bit) for src in range(count)])  62 us
    pallas_call x1, Pallas kernels, orthogonal(): pl.pallas_call(functools.partial(ortho_kernel, periods), in_specs=[pl.Blo...  50.9 us
    pallas_call x7, Pallas kernels, call(): pl.pallas_call(kernel, in_specs=[pl.BlockSpec(memory_space=pltpu.SMEM)] *...  50.2 us
    ppermute x31, waiting for transfers between devices, narrow_flip(): return lax.ppermute(value, NR, [(src, src ^ bit) for src in range(QN)])  45.6 us
    pallas_call x1, Pallas kernels, attention_bwd(): pl.pallas_call(functools.partial(attn_bwd_kernel, tile), grid=(pairs,), i...  29 us
    pallas_call x1, Pallas kernels, attention_fwd(): pl.pallas_call(functools.partial(attn_fwd_kernel, tile), grid=(pairs,), i...  17.4 us
    ppermute x31, starting transfers between devices, narrow_flip(): return lax.ppermute(value, NR, [(src, src ^ bit) for src in range(QN)])  16.6 us
  transfers between devices with their start and end apart: 76, of which 32 were waited for; matrix products, arithmetic and copies ran while one was open for 18% of the time, Pallas kernels for 14%

profile of v3, /device:TPU:0, one launch (start us, length us, event | category | flops | bytes accessed | tf_op | source)
XLA Modules:
  0.0 574.2 jit_solution(8453274151211169400)
XLA Ops:
  4.6 5.0 collective-permute-start
  16.5 5.4 fusion.12.pix_ref
  24.4 4.3 collective-permute-done.2
  30.5 3.0 collective-permute-start.11
  36.6 8.2 %collective-permute-done.3 = bf16[3,144,768]{2,1,0:T(8,128)(2,1)S(1)} collective-permute-done((bf16[3,144,768]{2,1,0:T(8,128)(2,1)S(1)}, bf16[3,144,768]{2,1,0:T(8,128)(2,1)S(1)}, u32[]{:S(2)}, u32[]{:S(2)}) %collective-permute-start.3) | collective-permute-done | bytes 663584 | tf_op jit(solution)/shard_map/ppermute | solution.py:94
  51.4 3.0 collective-permute-done.11
  55.6 2.2 pad_maximum_fusion.17
  62.2 4.8 collective-permute-start.17
  71.9 5.0 shard_map.535
  76.8 3.6 collective-permute-done.13
  86.9 5.9 %collective-permute-done.18 = bf16[2,216,384]{2,1,0:T(8,128)(2,1)S(1)} collective-permute-done((bf16[2,216,384]{2,1,0:T(8,128)(2,1)S(1)}, bf16[2,216,384]{2,1,0:T(8,128)(2,1)S(1)}, u32[]{:S(2)}, u32[]{:S(2)}) %collective-permute-start.18) | collective-permute-done | bytes 331808 | tf_op jit(solution)/shard_map/ppermute | solution.py:94
  92.8 3.7 collective-permute-done.9.more_ref
  98.6 5.1 shard_map.536
  103.7 2.1 collective-permute-done.15
  109.5 13.3 %collective-permute-done.21 = bf16[3,2,216,384]{3,2,1,0:T(8,128)(2,1)S(1)} collective-permute-done((bf16[3,2,216,384]{3,2,1,0:T(8,128)(2,1)}, bf16[3,2,216,384]{3,2,1,0:T(8,128)(2,1)S(1)}, u32[]{:S(2)}, u32[]{:S(2)}) %collective-permute-start.21) | collective-permute-done | bytes 995360 | tf_op jit(solution)/shard_map/ppermute | solution.py:94
  122.9 5.0 collective-permute-done.20
  131.0 2.9 multiply_sine_fusion
  139.9 2.1 reshape.1548.w_ref
  142.0 8.9 %shard_map.537 = (f32[320,768]{1,0:T(8,128)}, f32[784,384]{1,0:T(8,128)}, bf16[784,384]{1,0:T(8,128)(2,1)}, bf16[784,384]{1,0:T(8,128)(2,1)}, bf16[2,784,384]{2,1,0:T(8,128)(2,1)}) custom-call(s32[2]{0:T(128)} %pad_add_fusion.where_ref, f32[320,768]{1,0:T(8,128)} %get-tuple-element.146.middle_ref, bf16[320,768]{1,0:T(8,128)(2,1)} %copy-done.38, ...), custom_call_target="tpu_custom_call" | custom-call | flops 2000000000 | bytes 1000 | tf_op jit(solution)/shard_map/pallas_call | solution.py:608
  151.2 4.3 multiply_reduce_fusion.3
  155.8 3.5 pad_maximum_fusion.7
  159.3 2.5 reshape_reshape.3
  166.5 1.8 collective-permute-start.24
  168.3 3.4 collective-permute-start.25
  171.7 17.4 %shard_map.538 = (bf16[784,384]{1,0:T(8,128)(2,1)}, f32[784,384]{1,0:T(8,128)}, f32[3,2,784]{2,1,0:T(2,128)}) custom-call(bf16[784,384]{1,0:T(8,128)(2,1)} %get-tuple-element.163.q_ref, bf16[2,1568,384]{2,1,0:T(8,128)(2,1)} %bitcast.519), custom_call_target="tpu_custom_call" | custom-call | flops 2000000000 | bytes 1000 | tf_op jit(solution)/shard_map/pallas_call | solution.py:384
  196.5 4.8 multiply_reduce_fusion
  203.5 2.8 convolution_convert_fusion
  206.3 3.9 convert_reduce_fusion
  210.1 3.0 convolution_convert_fusion.2
  213.1 2.1 multiply_reduce_fusion.6
  223.8 2.8 convolution_convert_fusion.3.g_ref
  227.8 1.9 convert_add_fusion
  231.3 29.0 %shard_map.539 = (bf16[784,384]{1,0:T(8,128)(2,1)}, bf16[2,1568,384]{2,1,0:T(8,128)(2,1)}) custom-call(bf16[784,384]{1,0:T(8,128)(2,1)} %get-tuple-element.163.q_ref, bf16[2,1568,384]{2,1,0:T(8,128)(2,1)} %bitcast.520, bf16[784,384]{1,0:T(8,128)(2,1)} %convolution_convert_fusion.3.g_ref, f32[784,384]{1,0:T(8,128)} %get-tuple-element.179.of_ref, ...), custom_call_target="tpu_custom_call" | custom-call | flops 2000000000 | bytes 1000 | tf_op jit(solution)/shard_map/pallas_call | solution.py:426
  263.3 2.9 collective-permute-done.29.got_ref
  267.3 10.0 %shard_map.540 = (bf16[1152,384]{1,0:T(8,128)(2,1)}, f32[160,384]{1,0:T(8,128)}, f32[8,384]{1,0:T(8,128)}, f32[784,384]{1,0:T(8,128)}) custom-call(s32[2]{0:T(128)} %pad_add_fusion.where_ref, bf16[784,384]{1,0:T(8,128)(2,1)} %get-tuple-element.181.gq_ref, bf16[2,784,384]{2,1,0:T(8,128)(2,1)} %get-tuple-element.311.gkv_ref, bf16[2,784,384]{2,1,0:T(8,128)(2,1)} %copy-done.86, ...), custom_call_target="tpu_custom_call" | custom-call | flops 2000000000 | bytes 1000 | tf_op jit(solution)/shard_map/pallas_call | solution.py:608
  277.4 2.5 reshape.1557
  282.5 4.5 collective-permute-done.31
  287.7 7.7 %shard_map.541 = (bf16[768,384]{1,0:T(8,128)(2,1)}, f32[320,768]{1,0:T(8,128)}, bf16[768,768]{1,0:T(8,128)(2,1)}, bf16[768,768]{1,0:T(8,128)(2,1)}, bf16[320,768]{1,0:T(8,128)(2,1)}, /*index=5*/f32[8,768]{1,0:T(8,128)}) custom-call(bf16[320,384]{1,0:T(8,128)(2,1)} %bitcast.570, f32[320,768]{1,0:T(8,128)} %get-tuple-element.187.result_ref, ...), custom_call_target="tpu_custom_call" | custom-call | flops 2000000000 | bytes 1000 | tf_op jit(solution)/shard_map/pallas_call | solution.py:608
  302.9 8.1 %collective-permute-done.33.more_ref = bf16[320,768]{1,0:T(8,128)(2,1)S(1)} collective-permute-done((bf16[320,768]{1,0:T(8,128)(2,1)S(1)}, bf16[320,768]{1,0:T(8,128)(2,1)S(1)}, u32[]{:S(2)}, u32[]{:S(2)}) %collective-permute-start.33) | collective-permute-done | bytes 491552 | tf_op jit(solution)/shard_map/ppermute | solution.py:98
  311.7 7.9 %shard_map.542 = (f32[320,768]{1,0:T(8,128)}, bf16[192,768]{1,0:T(8,128)(2,1)}, bf16[3,192,768]{2,1,0:T(8,128)(2,1)}, bf16[320,768]{1,0:T(8,128)(2,1)}, f32[8,768]{1,0:T(8,128)}, /*index=5*/bf16[3,320,192]{2,1,0:T(8,128)(2,1)}) custom-call(bf16[320,768]{1,0:T(8,128)(2,1)} %copy-done.40, bf16[320,768]{1,0:T(8,128)(2,1)} %copy-done.87, ...), custom_call_target="tpu_custom_call" | custom-call | flops 2000000000 | bytes 1000 | tf_op jit(solution)/shard_map/pallas_call | solution.py:608
  323.5 2.1 reshape.1561
  337.6 4.4 collective-permute-start.54
  346.4 10.4 %collective-permute-done.35.more_ref = bf16[320,768]{1,0:T(8,128)(2,1)S(1)} collective-permute-done((bf16[320,768]{1,0:T(8,128)(2,1)S(1)}, bf16[320,768]{1,0:T(8,128)(2,1)S(1)}, u32[]{:S(2)}, u32[]{:S(2)}) %collective-permute-start.35) | collective-permute-done | bytes 491552 | tf_op jit(solution)/shard_map/ppermute | solution.py:98
  357.6 5.6 shard_map.543
  369.0 12.1 %collective-permute-done.44 = bf16[1,4,48,384]{3,2,1,0:T(8,128)(2,1)S(1)} collective-permute-done((bf16[1,4,48,384]{3,2,1,0:T(8,128)(2,1)S(1)}, bf16[1,4,48,384]{3,2,1,0:T(8,128)(2,1)S(1)}, u32[]{:S(2)}, u32[]{:S(2)}) %collective-permute-start.44) | collective-permute-done | bytes 147488 | tf_op jit(solution)/shard_map/ppermute | solution.py:94
  381.9 3.5 collective-permute-start.47
  386.7 2.4 collective-permute-start.48
  390.5 1.9 convert_add_fusion.1
  392.4 1.9 collective-permute-done.37
  395.8 3.0 collective-permute-done.38
  400.6 14.3 %collective-permute-done.48 = bf16[4,108,768]{2,0,1:T(4,128)(2,1)S(1)} collective-permute-done((bf16[4,108,768]{2,0,1:T(4,128)(2,1)S(1)}, bf16[4,108,768]{2,0,1:T(4,128)(2,1)S(1)}, u32[]{:S(2)}, u32[]{:S(2)}) %collective-permute-start.48) | collective-permute-done | bytes 663584 | tf_op jit(solution)/shard_map/ppermute | solution.py:202
  421.1 6.5 %collective-permute-start.40 = (f32[1,19201]{1,0:T(1,128)S(1)}, f32[1,19201]{1,0:T(1,128)S(1)}, u32[]{:S(2)}, u32[]{:S(2)}) collective-permute-start(f32[1,19201]{1,0:T(1,128)S(1)} %add.549), channel_id=1, source_target_pairs={{0,16},{4,20},{8,24},{12,28},{16,0},{20,4},{24,8},{28,12},{1,17},{... | collective-permute-start | bytes 230420 | tf_op jit(solution)/shard_map/ppermute | solution.py:94
  429.6 2.2 collective-permute-done.40
  433.7 2.7 collective-permute-start.61
  440.3 2.4 collective-permute-start.67
  444.8 4.8 shard_map.544
  450.3 6.4 %collective-permute-done.68 = bf16[120,768]{1,0:T(8,128)(2,1)S(1)} collective-permute-done((bf16[120,768]{1,0:T(8,128)(2,1)S(1)}, bf16[120,768]{1,0:T(8,128)(2,1)S(1)}, u32[]{:S(2)}, u32[]{:S(2)}) %collective-permute-start.68) | collective-permute-done | bytes 184352 | tf_op jit(solution)/shard_map/ppermute | solution.py:94
  468.2 9.3 %collective-permute-done.63 = f32[960,128]{1,0:T(8,128)S(1)} collective-permute-done((f32[960,128]{1,0:T(8,128)}, f32[960,128]{1,0:T(8,128)S(1)}, u32[]{:S(2)}, u32[]{:S(2)}) %collective-permute-start.63) | collective-permute-done | bytes 491552 | tf_op jit(solution)/shard_map/ppermute | solution.py:94
  483.1 7.4 %collective-permute-done.64 = f32[960,128]{1,0:T(8,128)S(1)} collective-permute-done((f32[960,128]{1,0:T(8,128)S(1)}, f32[960,128]{1,0:T(8,128)S(1)}, u32[]{:S(2)}, u32[]{:S(2)}) %collective-permute-start.64) | collective-permute-done | bytes 491552 | tf_op jit(solution)/shard_map/ppermute | solution.py:98
  493.2 1.9 multiply_subtract_fusion.2
  496.6 50.9 %shard_map.545 = (bf16[384,768]{1,0:T(8,128)(2,1)}, bf16[192,384]{1,0:T(8,128)(2,1)}) custom-call(s32[3]{0:T(128)} %pad_add_fusion.1.counts_ref, f32[1]{0:T(128)} %bitcast.155.factor_ref, f32[1920,128]{1,0:T(8,128)} %copy-done.31, f32[1920,128]{1,0:T(8,128)} %collective-permute-done.72.other_ref, f32[384,768]{1,0:T(8,128)} %bitcast.515, ...), custom_call_target="tpu_custom_call" | custom-call | flops 2000000000 | bytes 1000 | tf_op jit(solution)/shard_map/pallas_call | solution.py:594
  550.4 3.6 collective-permute-start.75
  554.6 4.5 collective-permute-done.73
  559.0 7.2 %collective-permute-done.74 = bf16[120,768]{1,0:T(8,128)(2,1)S(1)} collective-permute-done((bf16[120,768]{1,0:T(8,128)(2,1)S(1)}, bf16[120,768]{1,0:T(8,128)(2,1)S(1)}, u32[]{:S(2)}, u32[]{:S(2)}) %collective-permute-start.74) | collective-permute-done | bytes 184352 | tf_op jit(solution)/shard_map/ppermute | solution.py:94
  (601 shorter events, 175.7 us)
Async XLA Ops:
  4.6 19.8 %collective-permute-start = (bf16[144,768]{1,0:T(8,128)(2,1)}, bf16[144,768]{1,0:T(8,128)(2,1)S(1)}, u32[]{:S(2)}, u32[]{:S(2)}) collective-permute-start(bf16[144,768]{1,0:T(8,128)(2,1)} %pad_maximum_fusion.42), channel_id=1, source_target_pairs={{0,24},{4,28},{8,16},{12,20},{16,8},{20,12},{24,0},{28,4},{1,25},{... | collective-permute-start | bytes 663560 | tf_op jit(solution)/shard_map/ppermute | solution.py:94
  9.7 14.7 %collective-permute-start.1 = (bf16[144,768]{1,0:T(8,128)(2,1)}, bf16[144,768]{1,0:T(8,128)(2,1)S(1)}, u32[]{:S(2)}, u32[]{:S(2)}) collective-permute-start(bf16[144,768]{1,0:T(8,128)(2,1)} %pad_maximum_fusion.42), channel_id=1, source_target_pairs={{0,8},{4,12},{8,0},{12,4},{16,24},{20,28},{24,16},{28,20},{1,9},{5... | collective-permute-start | bytes 663560 | tf_op jit(solution)/shard_map/ppermute | solution.py:94
  9.7 19.0 %collective-permute-start.2 = (bf16[144,768]{1,0:T(8,128)(2,1)}, bf16[144,768]{1,0:T(8,128)(2,1)S(1)}, u32[]{:S(2)}, u32[]{:S(2)}) collective-permute-start(bf16[144,768]{1,0:T(8,128)(2,1)} %pad_maximum_fusion.42), channel_id=1, source_target_pairs={{0,16},{4,20},{8,24},{12,28},{16,0},{20,4},{24,8},{28,12},{1,17},{... | collective-permute-start | bytes 663560 | tf_op jit(solution)/shard_map/ppermute | solution.py:94
  10.2 25.3 %collective-permute-start.4 = (bf16[144,768]{1,0:T(8,128)(2,1)}, bf16[144,768]{1,0:T(8,128)(2,1)}, u32[]{:S(2)}, u32[]{:S(2)}) collective-permute-start(bf16[144,768]{1,0:T(8,128)(2,1)} %pad_maximum_fusion.42), channel_id=1, source_target_pairs={{0,4},{4,0},{8,12},{12,8},{16,20},{20,16},{24,28},{28,24},{1,5},{5... | collective-permute-start | bytes 663560 | tf_op jit(solution)/shard_map/ppermute | solution.py:94
  14.0 16.3 %collective-permute-start.7 = (bf16[216,384]{1,0:T(8,128)(2,1)S(1)}, bf16[216,384]{1,0:T(8,128)(2,1)S(1)}, u32[]{:S(2)}, u32[]{:S(2)}) collective-permute-start(bf16[216,384]{1,0:T(8,128)(2,1)S(1)} %concatenate.364), channel_id=1, source_target_pairs={{0,2},{1,3},{2,0},{3,1},{4,6},{5,7},{6,4},{7,5},{8,10},{9,11},{10,... | collective-permute-start | bytes 497672 | tf_op jit(solution)/shard_map/ppermute | solution.py:98
  28.8 16.0 %collective-permute-start.3 = (bf16[3,144,768]{2,1,0:T(8,128)(2,1)S(1)}, bf16[3,144,768]{2,1,0:T(8,128)(2,1)S(1)}, u32[]{:S(2)}, u32[]{:S(2)}) collective-permute-start(bf16[3,144,768]{2,1,0:T(8,128)(2,1)S(1)} %pad_maximum_fusion.22), channel_id=1, source_target_pairs={{0,4},{4,0},{8,12},{12,8},{16,20},{20,16},{24,28},{28,24},{1,5},{5... | collective-permute-start | bytes 1990664 | tf_op jit(solution)/shard_map/ppermute | solution.py:94
  30.4 21.0 %collective-permute-start.10 = (bf16[192,768]{1,0:T(8,128)(2,1)}, bf16[192,768]{1,0:T(8,128)(2,1)}, u32[]{:S(2)}, u32[]{:S(2)}) collective-permute-start(bf16[192,768]{1,0:T(8,128)(2,1)} %pad_maximum_fusion.40), channel_id=1, source_target_pairs={{0,8},{4,12},{8,0},{12,4},{16,24},{20,28},{24,16},{28,20},{1,9},{5... | collective-permute-start | bytes 884744 | tf_op jit(solution)/shard_map/ppermute | solution.py:94
  30.5 23.9 %collective-permute-start.11 = (bf16[192,768]{1,0:T(8,128)(2,1)}, bf16[192,768]{1,0:T(8,128)(2,1)}, u32[]{:S(2)}, u32[]{:S(2)}) collective-permute-start(bf16[192,768]{1,0:T(8,128)(2,1)} %pad_maximum_fusion.40), channel_id=1, source_target_pairs={{0,16},{4,20},{8,24},{12,28},{16,0},{20,4},{24,8},{28,12},{1,17},{... | collective-permute-start | bytes 884744 | tf_op jit(solution)/shard_map/ppermute | solution.py:94
  33.5 20.9 %collective-permute-start.12 = (bf16[192,768]{1,0:T(8,128)(2,1)}, bf16[192,768]{1,0:T(8,128)(2,1)}, u32[]{:S(2)}, u32[]{:S(2)}) collective-permute-start(bf16[192,768]{1,0:T(8,128)(2,1)} %pad_maximum_fusion.40), channel_id=1, source_target_pairs={{0,24},{4,28},{8,16},{12,20},{16,8},{20,12},{24,0},{28,4},{1,25},{... | collective-permute-start | bytes 884744 | tf_op jit(solution)/shard_map/ppermute | solution.py:94
  48.1 7.3 %collective-permute-start.5 = (f32[320,192]{0,1:T(8,128)S(1)}, f32[320,192]{0,1:T(8,128)S(1)}, u32[]{:S(2)}, u32[]{:S(2)}) collective-permute-start(f32[320,192]{0,1:T(8,128)S(1)} %fusion.117), channel_id=1, source_target_pairs={{0,2},{1,3},{2,0},{3,1},{4,6},{5,7},{6,4},{7,5},{8,10},{9,11},{10,... | collective-permute-start | bytes 737288 | tf_op jit(solution)/shard_map/ppermute | solution.py:98
  54.4 7.7 %collective-permute-start.14 = (bf16[192,768]{1,0:T(8,128)(2,1)}, bf16[192,768]{1,0:T(8,128)(2,1)S(1)}, u32[]{:S(2)}, u32[]{:S(2)}) collective-permute-start(bf16[192,768]{1,0:T(8,128)(2,1)} %pad_maximum_fusion.40), channel_id=1, source_target_pairs={{0,4},{4,0},{8,12},{12,8},{16,20},{20,16},{24,28},{28,24},{1,5},{5... | collective-permute-start | bytes 884744 | tf_op jit(solution)/shard_map/ppermute | solution.py:94
  55.5 14.8 %collective-permute-start.6 = (f32[320,2,192]{0,2,1:T(8,128)S(1)}, f32[320,2,192]{0,2,1:T(8,128)S(1)}, u32[]{:S(2)}, u32[]{:S(2)}) collective-permute-start(f32[320,2,192]{0,2,1:T(8,128)S(1)} %pad_maximum_fusion.28), channel_id=1, source_target_pairs={{0,1},{1,0},{2,3},{3,2},{4,5},{5,4},{6,7},{7,6},{8,9},{9,8},{10,11... | collective-permute-start | bytes 1474568 | tf_op jit(solution)/shard_map/ppermute | solution.py:98
  57.8 22.7 %collective-permute-start.13 = (bf16[3,192,768]{2,1,0:T(8,128)(2,1)}, bf16[3,192,768]{2,1,0:T(8,128)(2,1)}, u32[]{:S(2)}, u32[]{:S(2)}) collective-permute-start(bf16[3,192,768]{2,1,0:T(8,128)(2,1)} %pad_maximum_fusion.17), channel_id=1, source_target_pairs={{0,4},{4,0},{8,12},{12,8},{16,20},{20,16},{24,28},{28,24},{1,5},{5... | collective-permute-start | bytes 2654216 | tf_op jit(solution)/shard_map/ppermute | solution.py:94
  62.2 24.7 %collective-permute-start.17 = (bf16[2,216,384]{2,1,0:T(8,128)(2,1)S(1)}, bf16[2,216,384]{2,1,0:T(8,128)(2,1)S(1)}, u32[]{:S(2)}, u32[]{:S(2)}) collective-permute-start(bf16[2,216,384]{2,1,0:T(8,128)(2,1)S(1)} %pad_maximum_fusion.39), channel_id=1, source_target_pairs={{0,8},{4,12},{8,0},{12,4},{16,24},{20,28},{24,16},{28,20},{1,9},{5... | collective-permute-start | bytes 995336 | tf_op jit(solution)/shard_map/ppermute | solution.py:94
  66.9 25.9 %collective-permute-start.18 = (bf16[2,216,384]{2,1,0:T(8,128)(2,1)S(1)}, bf16[2,216,384]{2,1,0:T(8,128)(2,1)S(1)}, u32[]{:S(2)}, u32[]{:S(2)}) collective-permute-start(bf16[2,216,384]{2,1,0:T(8,128)(2,1)S(1)} %pad_maximum_fusion.39), channel_id=1, source_target_pairs={{0,16},{4,20},{8,24},{12,28},{16,0},{20,4},{24,8},{28,12},{1,17},{... | collective-permute-start | bytes 995336 | tf_op jit(solution)/shard_map/ppermute | solution.py:94
  67.5 25.2 %collective-permute-start.19 = (bf16[2,216,384]{2,1,0:T(8,128)(2,1)S(1)}, bf16[2,216,384]{2,1,0:T(8,128)(2,1)S(1)}, u32[]{:S(2)}, u32[]{:S(2)}) collective-permute-start(bf16[2,216,384]{2,1,0:T(8,128)(2,1)S(1)} %pad_maximum_fusion.39), channel_id=1, source_target_pairs={{0,24},{4,28},{8,16},{12,20},{16,8},{20,12},{24,0},{28,4},{1,25},{... | collective-permute-start | bytes 995336 | tf_op jit(solution)/shard_map/ppermute | solution.py:94
  76.8 5.6 collective-permute-start.8
  83.4 13.1 %collective-permute-start.9 = (bf16[320,768]{1,0:T(8,128)(2,1)S(1)}, bf16[320,768]{1,0:T(8,128)(2,1)S(1)}, u32[]{:S(2)}, u32[]{:S(2)}) collective-permute-start(bf16[320,768]{1,0:T(8,128)(2,1)S(1)} %add_convert_fusion.5.total_ref), channel_id=1, source_target_pairs={{0,2},{1,3},{2,0},{3,1},{4,6},{5,7},{6,4},{7,5},{8,10},{9,11},{10,... | collective-permute-start | bytes 1474568 | tf_op jit(solution)/shard_map/ppermute | solution.py:98
  97.6 25.2 %collective-permute-start.21 = (bf16[3,2,216,384]{3,2,1,0:T(8,128)(2,1)}, bf16[3,2,216,384]{3,2,1,0:T(8,128)(2,1)S(1)}, u32[]{:S(2)}, u32[]{:S(2)}) collective-permute-start(bf16[3,2,216,384]{3,2,1,0:T(8,128)(2,1)} %pad_maximum_fusion.13), channel_id=1, source_target_pairs={{0,4},{4,0},{8,12},{12,8},{16,20},{20,16},{24,28},{28,24},{1,5},{5... | collective-permute-start | bytes 2985992 | tf_op jit(solution)/shard_map/ppermute | solution.py:94
  106.9 20.9 %collective-permute-start.16 = (bf16[320,768]{1,0:T(8,128)(2,1)S(1)}, bf16[320,768]{1,0:T(8,128)(2,1)}, u32[]{:S(2)}, u32[]{:S(2)}) collective-permute-start(bf16[320,768]{1,0:T(8,128)(2,1)S(1)} %add_convert_fusion.4.total_ref), channel_id=1, source_target_pairs={{0,2},{1,3},{2,0},{3,1},{4,6},{5,7},{6,4},{7,5},{8,10},{9,11},{10,... | collective-permute-start | bytes 1474568 | tf_op jit(solution)/shard_map/ppermute | solution.py:98
  108.5 19.4 %collective-permute-start.20 = (bf16[2,216,384]{2,1,0:T(8,128)(2,1)S(1)}, bf16[2,216,384]{2,1,0:T(8,128)(2,1)S(1)}, u32[]{:S(2)}, u32[]{:S(2)}) collective-permute-start(bf16[2,216,384]{2,1,0:T(8,128)(2,1)S(1)} %pad_maximum_fusion.39), channel_id=1, source_target_pairs={{0,4},{4,0},{8,12},{12,8},{16,20},{20,16},{24,28},{28,24},{1,5},{5... | collective-permute-start | bytes 995336 | tf_op jit(solution)/shard_map/ppermute | solution.py:94
  129.3 7.1 %collective-permute-start.22 = (bf16[8,2,216,384]{3,2,1,0:T(8,128)(2,1)S(1)}, bf16[8,2,216,384]{3,2,1,0:T(8,128)(2,1)S(1)}, u32[]{:S(2)}, u32[]{:S(2)}) collective-permute-start(bf16[8,2,216,384]{3,2,1,0:T(8,128)(2,1)S(1)} %bitcast.508), channel_id=1, source_target_pairs={{0,1},{1,0},{2,3},{3,2},{4,5},{5,4},{6,7},{7,6},{8,9},{9,8},{10,11... | collective-permute-start | bytes 7962632 | tf_op jit(solution)/shard_map/ppermute | solution.py:98
  151.0 10.8 %collective-permute-start.23 = (bf16[2,784,384]{2,1,0:T(8,128)(2,1)}, bf16[2,784,384]{2,1,0:T(8,128)(2,1)}, u32[]{:S(2)}, u32[]{:S(2)}) collective-permute-start(bf16[2,784,384]{2,1,0:T(8,128)(2,1)} %get-tuple-element.164), channel_id=1, source_target_pairs={{0,1},{1,0},{2,3},{3,2},{4,5},{5,4},{6,7},{7,6},{8,9},{9,8},{10,11... | collective-permute-start | bytes 3612680 | tf_op jit(solution)/shard_map/ppermute | solution.py:98
  166.5 22.6 %collective-permute-start.24 = (bf16[120,768]{1,0:T(8,128)(2,1)S(1)}, bf16[120,768]{1,0:T(8,128)(2,1)S(1)}, u32[]{:S(2)}, u32[]{:S(2)}) collective-permute-start(bf16[120,768]{1,0:T(8,128)(2,1)S(1)} %get-tuple-element.383), channel_id=1, source_target_pairs={{0,24},{4,28},{8,16},{12,20},{16,8},{20,12},{24,0},{28,4},{1,25},{... | collective-permute-start | bytes 552968 | tf_op jit(solution)/shard_map/ppermute | solution.py:94
  168.3 20.8 %collective-permute-start.25 = (bf16[120,768]{1,0:T(8,128)(2,1)S(1)}, bf16[120,768]{1,0:T(8,128)(2,1)S(1)}, u32[]{:S(2)}, u32[]{:S(2)}) collective-permute-start(bf16[120,768]{1,0:T(8,128)(2,1)S(1)} %get-tuple-element.382), channel_id=1, source_target_pairs={{0,16},{4,20},{8,24},{12,28},{16,0},{20,4},{24,8},{28,12},{1,17},{... | collective-permute-start | bytes 552968 | tf_op jit(solution)/shard_map/ppermute | solution.py:94
  171.7 17.4 %collective-permute-start.26 = (bf16[120,768]{1,0:T(8,128)(2,1)S(1)}, bf16[120,768]{1,0:T(8,128)(2,1)S(1)}, u32[]{:S(2)}, u32[]{:S(2)}) collective-permute-start(bf16[120,768]{1,0:T(8,128)(2,1)S(1)} %get-tuple-element.381), channel_id=1, source_target_pairs={{0,8},{4,12},{8,0},{12,4},{16,24},{20,28},{24,16},{28,20},{1,9},{5... | collective-permute-start | bytes 552968 | tf_op jit(solution)/shard_map/ppermute | solution.py:94
  229.8 30.5 %collective-permute-start.28 = (bf16[3,4,2,48,384]{4,3,1,0,2:T(8,128)(2,1)S(1)}, bf16[3,4,2,48,384]{4,3,1,0,2:T(8,128)(2,1)S(1)}, u32[]{:S(2)}, u32[]{:S(2)}) collective-permute-start(bf16[3,4,2,48,384]{4,3,1,0,2:T(8,128)(2,1)S(1)} %fusion.28), channel_id=1, source_target_pairs={{0,2},{1,3},{2,0},{3,1},{4,6},{5,7},{6,4},{7,5},{8,10},{9,11},{10,... | collective-permute-start | bytes 2654216 | tf_op jit(solution)/shard_map/ppermute | solution.py:98
  280.0 15.4 %collective-permute-start.46 = (bf16[3,4,48,384]{3,2,1,0:T(8,128)(2,1)S(1)}, bf16[3,4,48,384]{3,2,1,0:T(8,128)(2,1)S(1)}, u32[]{:S(2)}, u32[]{:S(2)}) collective-permute-start(bf16[3,4,48,384]{3,2,1,0:T(8,128)(2,1)S(1)} %fusion.31), channel_id=1, source_target_pairs={{0,4},{4,0},{8,12},{12,8},{16,20},{20,16},{24,28},{28,24},{1,5},{5... | collective-permute-start | bytes 1327112 | tf_op jit(solution)/shard_map/ppermute | solution.py:94
  297.6 13.3 %collective-permute-start.33 = (bf16[320,768]{1,0:T(8,128)(2,1)S(1)}, bf16[320,768]{1,0:T(8,128)(2,1)S(1)}, u32[]{:S(2)}, u32[]{:S(2)}) collective-permute-start(bf16[320,768]{1,0:T(8,128)(2,1)S(1)} %add_convert_fusion.3.total_ref), channel_id=1, source_target_pairs={{0,2},{1,3},{2,0},{3,1},{4,6},{5,7},{6,4},{7,5},{8,10},{9,11},{10,... | collective-permute-start | bytes 1474568 | tf_op jit(solution)/shard_map/ppermute | solution.py:98
  299.1 44.2 %collective-permute-start.42 = (bf16[1,4,2,2,48,384]{5,4,1,2,3,0:T(8,128)(2,1)}, bf16[1,4,2,2,48,384]{5,4,1,2,3,0:T(8,128)(2,1)}, u32[]{:S(2)}, u32[]{:S(2)}) collective-permute-start(bf16[1,4,2,2,48,384]{5,4,1,2,3,0:T(8,128)(2,1)} %dynamic-slice_bitcast_fusion.6), channel_id=1, source_target_pairs={{0,1},{1,0},{2,3},{3,2},{4,5},{5,4},{6,7},{7,6},{8,9},{9,8},{10,11... | collective-permute-start | bytes 1769480 | tf_op jit(solution)/shard_map/ppermute | solution.py:98
  300.0 29.9 %collective-permute-start.51 = (bf16[4,96,768]{2,1,0:T(8,128)(2,1)}, bf16[4,96,768]{2,1,0:T(8,128)(2,1)}, u32[]{:S(2)}, u32[]{:S(2)}) collective-permute-start(bf16[4,96,768]{2,1,0:T(8,128)(2,1)} %dynamic-slice_bitcast_fusion.4), channel_id=1, source_target_pairs={{0,4},{4,0},{8,12},{12,8},{16,20},{20,16},{24,28},{28,24},{1,5},{5... | collective-permute-start | bytes 1769480 | tf_op jit(solution)/shard_map/ppermute | solution.py:94
  301.5 29.8 %collective-permute-start.50 = (bf16[4,96,768]{2,1,0:T(8,128)(2,1)}, bf16[4,96,768]{2,1,0:T(8,128)(2,1)}, u32[]{:S(2)}, u32[]{:S(2)}) collective-permute-start(bf16[4,96,768]{2,1,0:T(8,128)(2,1)} %dynamic-slice_bitcast_fusion.5), channel_id=1, source_target_pairs={{0,4},{4,0},{8,12},{12,8},{16,20},{20,16},{24,28},{28,24},{1,5},{5... | collective-permute-start | bytes 1769480 | tf_op jit(solution)/shard_map/ppermute | solution.py:94
  322.1 23.1 %collective-permute-start.41 = (bf16[4,84,768]{2,0,1:T(4,128)(2,1)}, bf16[4,84,768]{2,0,1:T(4,128)(2,1)}, u32[]{:S(2)}, u32[]{:S(2)}) collective-permute-start(bf16[4,84,768]{2,0,1:T(4,128)(2,1)} %copy.167), channel_id=1, source_target_pairs={{0,4},{4,0},{8,12},{12,8},{16,20},{20,16},{24,28},{28,24},{1,5},{5... | collective-permute-start | bytes 1548296 | tf_op jit(solution)/shard_map/ppermute | solution.py:94
  322.7 14.9 %collective-permute-start.34 = (bf16[320,768]{1,0:T(8,128)(2,1)}, bf16[320,768]{1,0:T(8,128)(2,1)}, u32[]{:S(2)}, u32[]{:S(2)}) collective-permute-start(bf16[320,768]{1,0:T(8,128)(2,1)} %get-tuple-element.196), channel_id=1, source_target_pairs={{0,1},{1,0},{2,3},{3,2},{4,5},{5,4},{6,7},{7,6},{8,9},{9,8},{10,11... | collective-permute-start | bytes 1474568 | tf_op jit(solution)/shard_map/ppermute | solution.py:98
  334.0 52.7 %collective-permute-start.52 = (bf16[4,120,768]{2,1,0:T(8,128)(2,1)}, bf16[4,120,768]{2,1,0:T(8,128)(2,1)}, u32[]{:S(2)}, u32[]{:S(2)}) collective-permute-start(bf16[4,120,768]{2,1,0:T(8,128)(2,1)} %get-tuple-element.302), channel_id=1, source_target_pairs={{8,0},{12,4},{16,24},{20,28},{9,1},{13,5},{17,25},{21,29},{10,2},{... | collective-permute-start | bytes 2211848 | tf_op jit(solution)/shard_map/ppermute | solution.py:202
  335.3 54.6 %collective-permute-start.53 = (bf16[4,120,768]{2,1,0:T(8,128)(2,1)}, bf16[4,120,768]{2,1,0:T(8,128)(2,1)}, u32[]{:S(2)}, u32[]{:S(2)}) collective-permute-start(bf16[4,120,768]{2,1,0:T(8,128)(2,1)} %get-tuple-element.303), channel_id=1, source_target_pairs={{8,24},{12,28},{16,0},{20,4},{9,25},{13,29},{17,1},{21,5},{10,26},... | collective-permute-start | bytes 2211848 | tf_op jit(solution)/shard_map/ppermute | solution.py:202
  337.6 52.9 %collective-permute-start.54 = (bf16[4,120,768]{2,1,0:T(8,128)(2,1)}, bf16[4,120,768]{2,1,0:T(8,128)(2,1)}, u32[]{:S(2)}, u32[]{:S(2)}) collective-permute-start(bf16[4,120,768]{2,1,0:T(8,128)(2,1)} %broadcast_select_fusion), channel_id=1, source_target_pairs={{0,24},{4,28},{24,0},{28,4},{1,25},{5,29},{25,1},{29,5},{2,26},{6,... | collective-permute-start | bytes 2211848 | tf_op jit(solution)/shard_map/ppermute | solution.py:202
  343.4 13.4 %collective-permute-start.35 = (bf16[320,768]{1,0:T(8,128)(2,1)S(1)}, bf16[320,768]{1,0:T(8,128)(2,1)S(1)}, u32[]{:S(2)}, u32[]{:S(2)}) collective-permute-start(bf16[320,768]{1,0:T(8,128)(2,1)S(1)} %add_convert_fusion.2.total_ref), channel_id=1, source_target_pairs={{0,2},{1,3},{2,0},{3,1},{4,6},{5,7},{6,4},{7,5},{8,10},{9,11},{10,... | collective-permute-start | bytes 1474568 | tf_op jit(solution)/shard_map/ppermute | solution.py:98
  356.8 10.6 %collective-permute-start.43 = (bf16[1,4,2,48,384]{4,3,1,2,0:T(8,128)(2,1)S(1)}, bf16[1,4,2,48,384]{4,3,1,2,0:T(8,128)(2,1)S(1)}, u32[]{:S(2)}, u32[]{:S(2)}) collective-permute-start(bf16[1,4,2,48,384]{4,3,1,2,0:T(8,128)(2,1)S(1)} %fusion.36), channel_id=1, source_target_pairs={{0,2},{1,3},{2,0},{3,1},{4,6},{5,7},{6,4},{7,5},{8,10},{9,11},{10,... | collective-permute-start | bytes 884744 | tf_op jit(solution)/shard_map/ppermute | solution.py:98
  364.8 16.5 %collective-permute-start.45 = (bf16[4,84,768]{2,0,1:T(4,128)(2,1)S(1)}, bf16[4,84,768]{2,0,1:T(4,128)(2,1)S(1)}, u32[]{:S(2)}, u32[]{:S(2)}) collective-permute-start(bf16[4,84,768]{2,0,1:T(4,128)(2,1)S(1)} %copy.176), channel_id=1, source_target_pairs={{0,4},{4,0},{8,12},{12,8},{16,20},{20,16},{24,28},{28,24},{1,5},{5... | collective-permute-start | bytes 1548296 | tf_op jit(solution)/shard_map/ppermute | solution.py:94
  367.5 13.7 %collective-permute-start.44 = (bf16[1,4,48,384]{3,2,1,0:T(8,128)(2,1)S(1)}, bf16[1,4,48,384]{3,2,1,0:T(8,128)(2,1)S(1)}, u32[]{:S(2)}, u32[]{:S(2)}) collective-permute-start(bf16[1,4,48,384]{3,2,1,0:T(8,128)(2,1)S(1)} %fusion.57), channel_id=1, source_target_pairs={{0,4},{4,0},{8,12},{12,8},{16,20},{20,16},{24,28},{28,24},{1,5},{5... | collective-permute-start | bytes 442376 | tf_op jit(solution)/shard_map/ppermute | solution.py:94
  381.2 7.9 %collective-permute-start.36 = (f32[1,19201]{1,0:T(1,128)S(1)}, f32[1,19201]{1,0:T(1,128)S(1)}, u32[]{:S(2)}, u32[]{:S(2)}) collective-permute-start(f32[1,19201]{1,0:T(1,128)S(1)} %reshape.1556), channel_id=1, source_target_pairs={{0,1},{1,0},{2,3},{3,2},{4,5},{5,4},{6,7},{7,6},{8,9},{9,8},{10,11... | collective-permute-start | bytes 230420 | tf_op jit(solution)/shard_map/ppermute | solution.py:98
  381.9 18.7 %collective-permute-start.47 = (bf16[4,108,768]{2,0,1:T(4,128)(2,1)S(1)}, bf16[4,108,768]{2,0,1:T(4,128)(2,1)S(1)}, u32[]{:S(2)}, u32[]{:S(2)}) collective-permute-start(bf16[4,108,768]{2,0,1:T(4,128)(2,1)S(1)} %copy.178), channel_id=1, source_target_pairs={{0,8},{4,12},{24,16},{28,20},{1,9},{5,13},{25,17},{29,21},{2,10},{... | collective-permute-start | bytes 1990664 | tf_op jit(solution)/shard_map/ppermute | solution.py:202
  386.7 28.2 %collective-permute-start.48 = (bf16[4,108,768]{2,0,1:T(4,128)(2,1)S(1)}, bf16[4,108,768]{2,0,1:T(4,128)(2,1)S(1)}, u32[]{:S(2)}, u32[]{:S(2)}) collective-permute-start(bf16[4,108,768]{2,0,1:T(4,128)(2,1)S(1)} %copy.180), channel_id=1, source_target_pairs={{0,16},{4,20},{24,8},{28,12},{1,17},{5,21},{25,9},{29,13},{2,18},{... | collective-permute-start | bytes 1990664 | tf_op jit(solution)/shard_map/ppermute | solution.py:202
  389.1 25.8 %collective-permute-start.49 = (bf16[4,108,768]{2,0,1:T(4,128)(2,1)S(1)}, bf16[4,108,768]{2,0,1:T(4,128)(2,1)S(1)}, u32[]{:S(2)}, u32[]{:S(2)}) collective-permute-start(bf16[4,108,768]{2,0,1:T(4,128)(2,1)S(1)} %copy.182), channel_id=1, source_target_pairs={{8,16},{12,20},{16,8},{20,12},{9,17},{13,21},{17,9},{21,13},{10,18... | collective-permute-start | bytes 1990664 | tf_op jit(solution)/shard_map/ppermute | solution.py:202
  399.0 22.1 %collective-permute-start.39 = (f32[1,19201]{1,0:T(1,128)S(1)}, f32[1,19201]{1,0:T(1,128)S(1)}, u32[]{:S(2)}, u32[]{:S(2)}) collective-permute-start(f32[1,19201]{1,0:T(1,128)S(1)} %add.548), channel_id=1, source_target_pairs={{0,8},{4,12},{8,0},{12,4},{16,24},{20,28},{24,16},{28,20},{1,9},{5... | collective-permute-start | bytes 230420 | tf_op jit(solution)/shard_map/ppermute | solution.py:94
  418.4 9.2 %collective-permute-start.55 = (f32[8,128]{1,0:T(8,128)S(1)}, f32[8,128]{1,0:T(8,128)S(1)}, u32[]{:S(2)}, u32[]{:S(2)}) collective-permute-start(f32[8,128]{1,0:T(8,128)S(1)} %broadcast_in_dim.25), channel_id=1, source_target_pairs={{0,3},{1,2},{2,1},{3,0},{4,7},{5,6},{6,5},{7,4},{8,11},{9,10},{10,... | collective-permute-start | bytes 12296 | tf_op jit(solution)/shard_map/ppermute | solution.py:98
  418.5 9.1 %collective-permute-start.56 = (f32[8,128]{1,0:T(8,128)S(1)}, f32[8,128]{1,0:T(8,128)S(1)}, u32[]{:S(2)}, u32[]{:S(2)}) collective-permute-start(f32[8,128]{1,0:T(8,128)S(1)} %broadcast_in_dim.25), channel_id=1, source_target_pairs={{0,2},{1,3},{2,0},{3,1},{4,6},{5,7},{6,4},{7,5},{8,10},{9,11},{10,... | collective-permute-start | bytes 12296 | tf_op jit(solution)/shard_map/ppermute | solution.py:98
  419.7 8.0 %collective-permute-start.57 = (f32[8,128]{1,0:T(8,128)S(1)}, f32[8,128]{1,0:T(8,128)S(1)}, u32[]{:S(2)}, u32[]{:S(2)}) collective-permute-start(f32[8,128]{1,0:T(8,128)S(1)} %broadcast_in_dim.25), channel_id=1, source_target_pairs={{0,1},{1,0},{2,3},{3,2},{4,5},{5,4},{6,7},{7,6},{8,9},{9,8},{10,11... | collective-permute-start | bytes 12296 | tf_op jit(solution)/shard_map/ppermute | solution.py:98
  421.1 10.7 %collective-permute-start.40 = (f32[1,19201]{1,0:T(1,128)S(1)}, f32[1,19201]{1,0:T(1,128)S(1)}, u32[]{:S(2)}, u32[]{:S(2)}) collective-permute-start(f32[1,19201]{1,0:T(1,128)S(1)} %add.549), channel_id=1, source_target_pairs={{0,16},{4,20},{8,24},{12,28},{16,0},{20,4},{24,8},{28,12},{1,17},{... | collective-permute-start | bytes 230420 | tf_op jit(solution)/shard_map/ppermute | solution.py:94
  431.9 5.5 collective-permute-start.59
  440.3 10.0 %collective-permute-start.67 = (bf16[120,768]{1,0:T(8,128)(2,1)S(1)}, bf16[120,768]{1,0:T(8,128)(2,1)S(1)}, u32[]{:S(2)}, u32[]{:S(2)}) collective-permute-start(bf16[120,768]{1,0:T(8,128)(2,1)S(1)} %get-tuple-element.380), channel_id=1, source_target_pairs={{0,24},{4,28},{8,16},{12,20},{16,8},{20,12},{24,0},{28,4},{1,25},{... | collective-permute-start | bytes 552968 | tf_op jit(solution)/shard_map/ppermute | solution.py:94
  442.8 14.0 %collective-permute-start.68 = (bf16[120,768]{1,0:T(8,128)(2,1)S(1)}, bf16[120,768]{1,0:T(8,128)(2,1)S(1)}, u32[]{:S(2)}, u32[]{:S(2)}) collective-permute-start(bf16[120,768]{1,0:T(8,128)(2,1)S(1)} %get-tuple-element.379), channel_id=1, source_target_pairs={{0,16},{4,20},{8,24},{12,28},{16,0},{20,4},{24,8},{28,12},{1,17},{... | collective-permute-start | bytes 552968 | tf_op jit(solution)/shard_map/ppermute | solution.py:94
  443.9 12.9 %collective-permute-start.69 = (bf16[120,768]{1,0:T(8,128)(2,1)S(1)}, bf16[120,768]{1,0:T(8,128)(2,1)S(1)}, u32[]{:S(2)}, u32[]{:S(2)}) collective-permute-start(bf16[120,768]{1,0:T(8,128)(2,1)S(1)} %get-tuple-element.378), channel_id=1, source_target_pairs={{0,8},{4,12},{8,0},{12,4},{16,24},{20,28},{24,16},{28,20},{1,9},{5... | collective-permute-start | bytes 552968 | tf_op jit(solution)/shard_map/ppermute | solution.py:94
  449.6 14.3 %collective-permute-start.62 = (f32[1920,128]{1,0:T(8,128)}, f32[1920,128]{1,0:T(8,128)S(1)}, u32[]{:S(2)}, u32[]{:S(2)}) collective-permute-start(f32[1920,128]{1,0:T(8,128)} %get-tuple-element.220), channel_id=1, source_target_pairs={{0,1},{1,0},{2,3},{3,2},{4,5},{5,4},{6,7},{7,6},{8,9},{9,8},{10,11... | collective-permute-start | bytes 2949128 | tf_op jit(solution)/shard_map/ppermute | solution.py:98
  459.9 22.2 %collective-permute-start.70 = (f32[60,768]{1,0:T(8,128)}, f32[60,768]{1,0:T(8,128)}, u32[]{:S(2)}, u32[]{:S(2)}) collective-permute-start(f32[60,768]{1,0:T(8,128)} %slice_bitcast_fusion.14), channel_id=1, source_target_pairs={{0,2},{1,3},{2,0},{3,1},{4,6},{5,7},{6,4},{7,5},{8,10},{9,11},{10,... | collective-permute-start | bytes 552968 | tf_op jit(solution)/shard_map/ppermute | solution.py:98
  465.1 12.3 %collective-permute-start.63 = (f32[960,128]{1,0:T(8,128)}, f32[960,128]{1,0:T(8,128)S(1)}, u32[]{:S(2)}, u32[]{:S(2)}) collective-permute-start(f32[960,128]{1,0:T(8,128)} %get-tuple-element.355), channel_id=1, source_target_pairs={{0,4},{4,0},{8,12},{12,8},{16,20},{20,16},{24,28},{28,24},{1,5},{5... | collective-permute-start | bytes 1474568 | tf_op jit(solution)/shard_map/ppermute | solution.py:94
  466.4 12.1 %collective-permute-start.65 = (f32[960,128]{1,0:T(8,128)}, f32[960,128]{1,0:T(8,128)}, u32[]{:S(2)}, u32[]{:S(2)}) collective-permute-start(f32[960,128]{1,0:T(8,128)} %get-tuple-element.356), channel_id=1, source_target_pairs={{0,2},{1,3},{2,0},{3,1},{4,6},{5,7},{6,4},{7,5},{8,10},{9,11},{10,... | collective-permute-start | bytes 1474568 | tf_op jit(solution)/shard_map/ppermute | solution.py:98
  479.6 10.9 %collective-permute-start.64 = (f32[960,128]{1,0:T(8,128)S(1)}, f32[960,128]{1,0:T(8,128)S(1)}, u32[]{:S(2)}, u32[]{:S(2)}) collective-permute-start(f32[960,128]{1,0:T(8,128)S(1)} %get-tuple-element.353), channel_id=1, source_target_pairs={{0,2},{1,3},{2,0},{3,1},{4,6},{5,7},{6,4},{7,5},{8,10},{9,11},{10,... | collective-permute-start | bytes 1474568 | tf_op jit(solution)/shard_map/ppermute | solution.py:98
  480.6 10.6 %collective-permute-start.66 = (f32[960,128]{1,0:T(8,128)S(1)}, f32[960,128]{1,0:T(8,128)S(1)}, u32[]{:S(2)}, u32[]{:S(2)}) collective-permute-start(f32[960,128]{1,0:T(8,128)S(1)} %get-tuple-element.354), channel_id=1, source_target_pairs={{0,4},{4,0},{8,12},{12,8},{16,20},{20,16},{24,28},{28,24},{1,5},{5... | collective-permute-start | bytes 1474568 | tf_op jit(solution)/shard_map/ppermute | solution.py:94
  483.1 9.2 %collective-permute-start.71 = (f32[2,60,768]{2,1,0:T(8,128)S(1)}, f32[2,60,768]{2,1,0:T(8,128)S(1)}, u32[]{:S(2)}, u32[]{:S(2)}) collective-permute-start(f32[2,60,768]{2,1,0:T(8,128)S(1)} %pad_maximum_fusion.38), channel_id=1, source_target_pairs={{0,1},{1,0},{2,3},{3,2},{4,5},{5,4},{6,7},{7,6},{8,9},{9,8},{10,11... | collective-permute-start | bytes 1105928 | tf_op jit(solution)/shard_map/ppermute | solution.py:98
  549.6 9.5 %collective-permute-start.73 = (bf16[120,768]{1,0:T(8,128)(2,1)S(1)}, bf16[120,768]{1,0:T(8,128)(2,1)S(1)}, u32[]{:S(2)}, u32[]{:S(2)}) collective-permute-start(bf16[120,768]{1,0:T(8,128)(2,1)S(1)} %get-tuple-element.377), channel_id=1, source_target_pairs={{0,24},{4,28},{8,16},{12,20},{16,8},{20,12},{24,0},{28,4},{1,25},{... | collective-permute-start | bytes 552968 | tf_op jit(solution)/shard_map/ppermute | solution.py:94
  550.4 15.8 %collective-permute-start.74 = (bf16[120,768]{1,0:T(8,128)(2,1)S(1)}, bf16[120,768]{1,0:T(8,128)(2,1)S(1)}, u32[]{:S(2)}, u32[]{:S(2)}) collective-permute-start(bf16[120,768]{1,0:T(8,128)(2,1)S(1)} %get-tuple-element.376), channel_id=1, source_target_pairs={{0,16},{4,20},{8,24},{12,28},{16,0},{20,4},{24,8},{28,12},{1,17},{... | collective-permute-start | bytes 552968 | tf_op jit(solution)/shard_map/ppermute | solution.py:94
  550.4 15.8 %collective-permute-start.75 = (bf16[120,768]{1,0:T(8,128)(2,1)S(1)}, bf16[120,768]{1,0:T(8,128)(2,1)S(1)}, u32[]{:S(2)}, u32[]{:S(2)}) collective-permute-start(bf16[120,768]{1,0:T(8,128)(2,1)S(1)} %get-tuple-element.375), channel_id=1, source_target_pairs={{0,8},{4,12},{8,0},{12,4},{16,24},{20,28},{24,16},{28,20},{1,9},{5... | collective-permute-start | bytes 552968 | tf_op jit(solution)/shard_map/ppermute | solution.py:94
  (105 other events, 524.8 us)
